TPU v7x, 32 devices: a whole 2x2x4 slice. The times are simulated.
32 devices in a mesh: group: 4 (over y, x), dp: 8 (over z, core).
Axes of the slice: x: 2, y: 2, z: 4, core: 2. Of those that a mesh axis runs over, the one named last changes fastest.
Arguments:
- hidden: bfloat16 [8192, 2048], P(('group', 'dp')), may hold values from 0 to 40, as said below
- weight: bfloat16 [2048, 1024], replicated, may hold values from -0.125 to 0.125
- partners: int32 [32, 256], P(('group', 'dp')), may hold values from 0 to 255, each once within a row
Outputs:
- whitened: bfloat16 [8192, 1024], P(('group', 'dp'))
- grad_weight: float32 [2048, 1024], P(('group', 'dp'))
- grad_hidden: bfloat16 [8192, 2048], P(('group', 'dp'))
Inputs may be any that keep to these rules, and one draw needn't show every extreme that they name: `hidden`: nonnegative activations. `partners`: each row is a permutation of 0 to 255.
All inputs are finite; a program needn't handle non-finite values.
Results may differ from a plain program's by a relative error of at most 0.0089.
Values sent between devices are 32-bit elements; how exact they have to be, the bound alone decides.
No kernel may reach another device: no remote copies, remote signals or barrier semaphores. Data moves between devices by JAX's collectives and lax.ppermute only.
A program may use at most 128 MiB of HBM per device.

v0:
```python
import functools

import jax
import jax.numpy as jnp
from jax import lax
from jax.experimental import pallas as pl
from jax.experimental.pallas import tpu as pltpu
from jax.sharding import PartitionSpec as P

AXES = ("group", "dp")
epsilon = 1e-06
f32 = jnp.float32
bf16 = jnp.bfloat16
NN = (((1,), (0,)), ((), ()))
NT = (((1,), (1,)), ((), ()))
TN = (((0,), (0,)), ((), ()))
BLK = 128
PAIR = 256
PANEL = 32
AHEAD = 16
VMEM = pl.BlockSpec(memory_space=pltpu.VMEM)
SMEM = pl.BlockSpec(memory_space=pltpu.SMEM)
HBM = pl.BlockSpec(memory_space=pltpu.HBM)


def split2(x):
    high = x.astype(bf16)
    return high, (x - high.astype(f32)).astype(bf16)


def split3(x):
    high = x.astype(bf16)
    rest = x - high.astype(f32)
    mid = rest.astype(bf16)
    return high, mid, (rest - mid.astype(f32)).astype(bf16)


def left6(parts, axis):
    high, mid, low = parts
    return jnp.concatenate([high, high, mid, high, low, mid], axis=axis)


def right6(parts, axis):
    high, mid, low = parts
    return jnp.concatenate([high, mid, high, low, high, mid], axis=axis)


def left3(parts, axis):
    return jnp.concatenate([parts[0], parts[0], parts[1]], axis=axis)


def right3(parts, axis):
    return jnp.concatenate([parts[0], parts[1], parts[0]], axis=axis)


def mm(a, b, dims):
    return lax.dot_general(a, b, dims, preferred_element_type=f32)


def dot6(a, b, dims):
    (ca,), (cb,) = dims[0]
    return mm(left6(split3(a), ca), right6(split3(b), cb), dims)


def dot3(a, b, dims):
    (ca,), (cb,) = dims[0]
    return mm(left3(split2(a), ca), right3(split2(b), cb), dims)


def starts(blocks):
    out, at = [], 0
    for j in range(blocks):
        out.append(at)
        at += (blocks - j - j % 2) * BLK
    return out, at


def radices(count):
    out = []
    while count > 1:
        out.append(4 if count % 4 == 0 else 2)
        count //= out[-1]
    return out


def rounds():
    groups, per = lax.axis_size("group"), lax.axis_size("dp")
    out, at = [(1, 2)], per
    for radix in radices(groups):
        out.append((at, radix))
        at *= radix
    at = 2
    for radix in radices(per // 2):
        out.append((at, radix))
        at *= radix
    return out


def place():
    index = lax.axis_index("group") * lax.axis_size("dp") + lax.axis_index("dp")
    out = 0
    for stride, radix in rounds():
        out = out * radix + (index // stride) % radix
    return out.astype(jnp.int32).reshape(1, 1)


def swap(x, stride, by):
    count = lax.axis_size("group") * lax.axis_size("dp")
    return lax.ppermute(x, AXES, [(i, i ^ (by * stride)) for i in range(count)])


def combine_kernel(size, listed, parts, radix, *refs):
    ins, outs = refs[:parts], refs[parts:]
    total, more = ins[0][0:size, :], ins[0][size + listed :, :]
    for r in ins[1:]:
        total = total + r[0:size, :]
        more = more + r[size + listed :, :]
    if listed:
        more = jnp.concatenate([r[size : size + listed, :] for r in ins] + [more], 0)
    if radix == 1:
        outs[0][...] = total
        outs[1][...] = more
        return
    cut = size // radix
    for i, out in enumerate(outs):
        out[0:cut, :] = total[i * cut : (i + 1) * cut, :]
        out[cut:, :] = more


def reduce_scatter(keep, send, size, listed):
    steps = rounds()
    summed = keep.shape[0] - size - listed
    pieces = [keep, send]
    for at, (stride, radix) in enumerate(steps):
        ins = [pieces[0]] + [swap(p, stride, by) for by, p in enumerate(pieces) if by]
        after = steps[at + 1][1] if at + 1 < len(steps) else 1
        more = listed * radix + summed
        shapes = [(size // after + more, BLK)] * after if after > 1 else [(size, BLK), (more, BLK)]
        pieces = call(
            functools.partial(combine_kernel, size, listed, len(ins), after),
            [(s, f32) for s in shapes],
            *ins,
        )
        listed, size = listed * radix, size // after
    return pieces


def all_gather(x):
    steps = rounds()
    parts = [x]
    for at in range(len(steps) - 1, 0, -1):
        stride, radix = steps[at]
        whole = parts[0] if len(parts) == 1 else jnp.concatenate(parts, 0)
        parts = [whole] + [swap(whole, stride, by) for by in range(1, radix)]
    return parts + [swap(p, 1, 1) for p in parts]


def padded(rows):
    unit = 8 * lax.axis_size("group") * lax.axis_size("dp")
    return -(-rows // unit) * unit


def gather_into(pos, parts, out_ref, devices):
    chunk = out_ref.shape[0] // devices
    each = devices // len(parts)
    for i, part in enumerate(parts):
        for j in range(each):
            to = pl.multiple_of(((i * each + j) ^ pos) * chunk, 8)
            out_ref[pl.ds(to, chunk), :] = part[j * chunk : (j + 1) * chunk, :]


def scatter_from(pos, src_ref, keep_ref, send_ref, devices):
    chunk = src_ref.shape[0] // devices
    half = devices // 2
    for i in range(devices):
        at = pl.multiple_of((i ^ pos) * chunk, 8)
        out = keep_ref if i < half else send_ref
        out[(i % half) * chunk : (i % half + 1) * chunk, :] = src_ref[pl.ds(at, chunk), :]


def put_row(out_ref, at, row):
    for i in range(row.shape[1] // BLK):
        out_ref[at + i : at + i + 1, :] = row[:, i * BLK : (i + 1) * BLK]


def put_extra(refs, at, rows):
    count = sum(row.shape[1] // BLK for row in rows)
    for ref in refs:
        end = at
        for row in rows:
            put_row(ref, end, row)
            end += row.shape[1] // BLK
        if count % 8:
            ref[end : at + count + 8 - count % 8, :] = jnp.zeros((8 - count % 8, BLK), f32)


def get_row(ref, at, blocks):
    return jnp.concatenate([ref[at + i : at + i + 1, :] for i in range(blocks)], 1)


def triangle():
    shape = (BLK, BLK)
    rows, cols = lax.broadcasted_iota(jnp.int32, shape, 0), lax.broadcasted_iota(jnp.int32, shape, 1)
    return rows > cols, rows == cols


def lower_products(left, right, out_ref, blocks):
    at, total = starts(blocks)
    n = blocks * BLK
    below, middle = triangle()
    diagonals = []
    for j in range(0, blocks, 2):
        lo = j * BLK
        part = mm(left[:, lo:], right[:, lo : lo + PAIR], TN)
        other = part[BLK:PAIR, BLK:]
        diagonals.append(jnp.sum(jnp.where(middle, other, 0.0), axis=0, keepdims=True))
        out_ref[at[j] : at[j] + BLK, :] = jnp.where(below, part[:BLK, :BLK], jnp.where(middle, part[:BLK, :BLK], other.T))
        out_ref[at[j] + BLK : at[j] + n - lo, :] = part[BLK:, :BLK]
        if lo + PAIR < n:
            out_ref[at[j + 1] : at[j + 1] + n - lo - PAIR, :] = part[PAIR:, BLK:]
    if out_ref.shape[0] > total:
        out_ref[total:, :] = jnp.zeros((out_ref.shape[0] - total, BLK), f32)
    return diagonals


def unpack(pay_ref, at, diagonal):
    below, middle = triangle()
    packed = pay_ref[at : at + BLK, :]
    one = jnp.where(below, packed, 0.0)
    one = jnp.where(middle, packed, one + one.T)
    two = jnp.where(below | middle, 0.0, packed)
    two = jnp.where(middle, diagonal, two + two.T)
    return one, two


def front_kernel(blocks, devices, pos_ref, hid_hbm, w_hbm, emb_hbm, keep_ref, send_ref, pay_ref, hid_ref, w_ref, emb_ref, sems):
    slabs = sems.shape[0] - 2
    deep = w_hbm.shape[0] // slabs
    copies = [pltpu.make_async_copy(hid_hbm, hid_ref, sems.at[slabs])]
    for i in range(slabs):
        rows = pl.ds(i * deep, deep)
        copies.append(pltpu.make_async_copy(w_hbm.at[rows, :], w_ref.at[rows, :], sems.at[i]))
    for copy in copies:
        copy.start()
    copies[0].wait()
    emb = 0.0
    for i in range(slabs):
        copies[1 + i].wait()
        emb = emb + mm(hid_ref[:, i * deep : (i + 1) * deep], w_ref[i * deep : (i + 1) * deep, :], NN)
    emb_ref[...] = emb
    out = pltpu.make_async_copy(emb_ref, emb_hbm, sems.at[slabs + 1])
    out.start()
    total = jnp.sum(emb, axis=0, keepdims=True)
    parts = split3(emb - total / emb.shape[0])
    diagonals = lower_products(left6(parts, 0), right6(parts, 0), pay_ref, blocks)
    scatter_from(pos_ref[0, 0], pay_ref, keep_ref, send_ref, devices)
    put_extra((keep_ref, send_ref), pay_ref.shape[0] // 2, [total] + diagonals)
    out.wait()


def turn_kernel(me_ref, hid_ref, keep_ref, send_ref, turned_ref):
    turned_ref[...] = hid_ref[...].astype(f32).T
    count = lax.axis_size("group") * lax.axis_size("dp")
    own = turned_ref.shape[0] // count
    core = me_ref[0, 0] % 2
    for out, c in ((keep_ref, core), (send_ref, 1 - core)):
        for i in range(count // 2):
            rows = turned_ref[pl.ds(pl.multiple_of((2 * i + c) * own, 8), own), :]
            out[i * own : (i + 1) * own, :] = rows


def order_kernel(orders, me_ref, keep_ref, got_ref, *refs):
    outs, part_ref = refs[:-1], refs[-1]
    chip = me_ref[0, 0] // 2
    own = part_ref.shape[0] >> len(orders[0])
    local = keep_ref.shape[1]
    for bits, out in zip(orders, outs):
        for i in range(1 << len(bits)):
            far = 0
            for t, bit in enumerate(reversed(bits)):
                far |= bit * ((i >> t) & 1)
            rows = pl.ds(pl.multiple_of((chip ^ (far // 2)) * own, 8), own)
            part_ref[i * own : (i + 1) * own, :local] = keep_ref[rows, :]
            part_ref[i * own : (i + 1) * own, local:] = got_ref[rows, :]
        out[...] = part_ref[...].astype(bf16)


def part_kernel(at, width, turned_ref, mine_ref, other_ref, keep_ref, send_ref):
    cols = slice(at, at + width)
    rows = jnp.concatenate([mine_ref[:, cols], other_ref[:, cols]], 0).astype(bf16)
    part = mm(turned_ref[...], rows, NN)
    half = keep_ref.shape[0]
    keep_ref[...] = part[:half]
    send_ref[...] = part[half:]


def lane(x, c):
    return jnp.broadcast_to(x[:, c : c + 1], (x.shape[0], BLK))


def sub(x, i):
    return jnp.broadcast_to(x[i : i + 1, :], (8, x.shape[1]))


def eye():
    shape = (BLK, BLK)
    return (lax.broadcasted_iota(jnp.int32, shape, 0) == lax.broadcasted_iota(jnp.int32, shape, 1)).astype(f32)


def inverse_factor(s, out):
    row = lax.broadcasted_iota(jnp.int32, (8, BLK), 0)
    t = eye()
    count = PANEL // 8
    outs = []
    for at in range(0, BLK, PANEL):
        r = [s[8 * q : 8 * q + 8] for q in range(count)]
        v = [t[8 * q : 8 * q + 8] for q in range(count)]
        pivots = [jnp.ones((8, BLK), f32)] * count
        for first in range(0, PANEL, AHEAD):
            last = first + AHEAD
            a = {(l, q): lane(r[q], at + l) for l in range(first, last) for q in range(l // 8, count)}
            for c in range(first, last):
                p, i = c // 8, c % 8
                piv = {l: sub(a[c, l // 8], l % 8) for l in range(c, last)}
                inv = 1.0 / piv[c]
                pivots[p] = jnp.where(row == i, piv[c], pivots[p])
                rs, vs = sub(r[p], i), sub(v[p], i)
                for q in range(p, count):
                    if q == p and i == 7:
                        continue
                    m = a[c, q] * inv
                    if q == p:
                        m = jnp.where(row > i, m, 0.0)
                    for l in range(c + 1, last):
                        if q >= l // 8:
                            a[l, q] = a[l, q] - m * piv[l]
                    r[q] = r[q] - m * rs
                    v[q] = v[q] - m * vs
            yield
        scale = [lax.rsqrt(p) for p in pivots]
        u = jnp.concatenate([x * g for x, g in zip(r, scale)], 0)
        w = jnp.concatenate([x * g for x, g in zip(v, scale)], 0)
        outs.append(w)
        if at + PANEL < BLK:
            us, ws = split3(u), split3(w)
            right = jnp.concatenate([right6(us, 0), right6(ws, 0)], axis=1)
            update = mm(left6(us, 0), right, TN)
            s = s[PANEL:] - update[at + PANEL :, :BLK]
            t = t[PANEL:] - update[at + PANEL :, BLK:]
    out.append(jnp.concatenate(outs, 0))


def inverse_pair(s11, s21, s22, out):
    got = []
    yield from inverse_factor(s11, got)
    l21 = dot6(s21, got[0], NT)
    rest = s22 - dot6(l21, l21, NT)
    yield
    yield from inverse_factor(rest, got)
    x21 = -dot6(got[1], dot6(l21, got[0], NN), NN)
    top = jnp.concatenate([got[0], jnp.zeros((BLK, BLK), f32)], 1)
    out.append(jnp.concatenate([top, jnp.concatenate([x21, got[1]], 1)], 0))


def factor_kernel(blocks, total_rows, devices, parts, *refs):
    pos_ref, sums_ref, emb_ref, partner_ref = refs[:4]
    part_refs = refs[4 : 4 + parts]
    xt_refs, white_refs = refs[4 + parts : 6 + parts], refs[6 + parts : 8 + parts]
    grad_ref, keep_ref, send_ref, a_ref, pay_ref, high_ref, mid_ref, low_ref = refs[8 + parts : 16 + parts]
    x_refs = refs[16 + parts :]
    pos = pos_ref[0, 0]
    gather_into(pos, part_refs, pay_ref, devices)
    n = blocks * BLK
    local = emb_ref.shape[0]
    at, _ = starts(blocks)
    sums = jnp.concatenate([sums_ref[pl.ds(j, devices, blocks), :] for j in range(blocks)], 1)
    mean = jnp.sum(sums, axis=0, keepdims=True) / total_rows
    apart = sums / local - mean
    left, right = left6(split3(apart), 0), right6(split3(apart), 0)
    pairs = blocks // 2
    for p in range(pairs):
        lo, hi = p * PAIR, (p + 1) * PAIR
        between = local * mm(left[:, lo:], right[:, lo:hi], TN)
        begin, after = at[2 * p], at[2 * p + 1]
        d = devices * blocks + p
        one, two = unpack(pay_ref, begin, sums_ref[d : d + 1, :])
        scale = 1.0 / (total_rows - 1)
        a_ref[p, lo : lo + BLK, :BLK] = (one + between[:BLK, :BLK]) * scale
        a_ref[p, lo + BLK : n, :BLK] = (pay_ref[begin + BLK : begin + n - lo, :] + between[BLK:, :BLK]) * scale
        a_ref[p, lo + BLK : hi, BLK:] = (two + between[BLK:PAIR, BLK:]) * scale
        if hi < n:
            a_ref[p, hi:n, BLK:] = (pay_ref[after : after + n - hi, :] + between[PAIR:, BLK:]) * scale
        a_ref[p, n:, :] = emb_ref[:, lo:hi] - mean[:, lo:hi]
    last = pairs * PAIR

    def rows_of(tile):
        return pl.ds(pl.multiple_of(tile * PAIR, PAIR), PAIR) if tile is not None else slice(last, last + local)

    def keep_parts(tile, x):
        for ref, part in zip((high_ref, mid_ref, low_ref), split3(x)):
            ref[rows_of(tile), :] = part

    def parts_at(tile):
        return [ref[rows_of(tile), :] for ref in (high_ref, mid_ref, low_ref)]

    def solve(q, tile, x):
        if tile is None:
            part = mm(left3(split2(a_ref[q, rows_of(tile), :]), 1), right3(x, 1), NT)
        else:
            part = mm(left6(split3(a_ref[q, rows_of(tile), :]), 1), right6(x, 1), NT)
        a_ref[q, rows_of(tile), :] = part
        keep_parts(tile, part)

    def update(j, tile, right, valid, fresh=False):
        if tile is None:
            part = mm(left3(parts_at(tile), 1), right3(parts_at(right), 1), NT)
        else:
            part = mm(left6(parts_at(tile), 1), right6(parts_at(right), 1), NT)
        have = a_ref[j, rows_of(tile), :]
        if fresh:
            have = have * (1.0 - valid)
        a_ref[j, rows_of(tile), :] = have - part * valid

    def chain(p):
        lo = pl.multiple_of(p * PAIR, PAIR)
        top, low = pl.ds(lo, BLK), pl.ds(pl.multiple_of(lo + BLK, BLK), BLK)
        got = []
        return got, inverse_pair(a_ref[p, top, :BLK], a_ref[p, low, :BLK], a_ref[p, low, BLK:], got)

    def settle(p, x):
        a_ref[p, rows_of(p), :] = x.T
        for ref, part in zip(x_refs, split3(x)):
            ref[...] = part
        solve(p, p + 1, [ref[...] for ref in x_refs])
        next_parts = parts_at(p + 1)
        a_ref[p + 1, rows_of(p + 1), :] -= mm(left6(next_parts, 1), right6(next_parts, 1), NT)

    got, steps = chain(0)
    for _ in steps:
        pass
    settle(0, got[0])

    def step(p, _):
        q = p - 1
        x = [ref[...] for ref in x_refs]
        tasks = [lambda: keep_parts(q, a_ref[q, rows_of(q), :])]
        others = [(q + r) % pairs for r in range(2, pairs)]
        tasks += [functools.partial(solve, q, tile, x) for tile in others + [None]]
        for u in range(pairs - 1):
            j = q + 1 + u
            valid = jnp.where(j < pairs, 1.0, 0.0).astype(f32)
            j = j % pairs
            tasks.append(functools.partial(update, j, q, j, valid, True))
            tasks += [functools.partial(update, j, t, j, valid) for t in others[max(u - 1, 0) :] + [None]]
        got, steps = chain(p)
        count = 2 * BLK // AHEAD + 1
        for i, _ in enumerate(steps):
            for _ in range(-(-len(tasks) // max(count - i, 1))):
                tasks.pop(0)()
        for task in tasks:
            task()

        @pl.when(p + 1 < pairs)
        def _():
            settle(p, got[0])

        @pl.when(p + 1 == pairs)
        def _():
            a_ref[p, rows_of(p), :] = got[0].T
            for ref, part in zip(x_refs, split3(got[0])):
                ref[...] = part

        return 0

    lax.fori_loop(1, pairs, step, 0)
    x = [ref[...] for ref in x_refs]
    for tile in list(range(pairs - 1)) + [None]:
        solve(pairs - 1, tile, x)
    for p in range(pairs):
        lo, hi = p * PAIR, (p + 1) * PAIR
        for ref, part in zip(xt_refs, split2(a_ref[p, 0:hi, :])):
            ref[0:hi, lo:hi] = part
    white = jnp.concatenate([a_ref[p, n:, :] for p in range(pairs)], 1)
    white_parts = split2(white)
    for ref, part in zip(white_refs, white_parts):
        ref[...] = part
    rows = white.shape[0]
    norm = jnp.sqrt(jnp.sum(white * white, axis=1, keepdims=True) + epsilon)
    unit = white / norm
    hit = (lax.broadcasted_iota(jnp.int32, (rows, rows), 0) == partner_ref[...]).astype(f32)
    both = (hit + hit.T).astype(bf16)
    parts = split3(unit)
    near = mm(jnp.concatenate([both] * 3, 1), jnp.concatenate(parts, 0), NN)
    grad_unit = 2.0 * (2.0 * unit - near)
    inner = jnp.sum(white * grad_unit, axis=1, keepdims=True)
    grad = grad_unit / norm - white * (inner / (norm * norm * norm))
    grad_ref[...] = grad
    diagonals = lower_products(left3(split2(grad), 0), right3(white_parts, 0), pay_ref, blocks)
    scatter_from(pos, pay_ref, keep_ref, send_ref, devices)
    totals = [jnp.sum(rows, axis=0, keepdims=True) for rows in (grad, white)]
    put_extra((keep_ref, send_ref), pay_ref.shape[0] // 2, totals + diagonals)


def moment_product(parts, pay_ref, diagonals, blocks):
    n = blocks * BLK
    at, _ = starts(blocks)
    outs = [0.0] * (blocks // 2)
    for j in range(0, blocks, 2):
        lo, hi = j * BLK, (j + 2) * BLK
        cross = pay_ref[at[j] + BLK : at[j] + PAIR, :]
        one, two = unpack(pay_ref, at[j], diagonals[j // 2])
        column = jnp.concatenate([jnp.concatenate([one, cross], 0), jnp.concatenate([cross.T, two], 0)], 1)
        outs[j // 2] += mm(left3([p[:, lo:hi] for p in parts], 1), right3(split2(column), 0), NN)
        if hi < n:
            rest = [pay_ref[at[j] + PAIR : at[j] + n - lo, :], pay_ref[at[j + 1] : at[j + 1] + n - hi, :]]
            rest = split2(jnp.concatenate(rest, 1))
            outs[j // 2] += mm(left3([p[:, hi:] for p in parts], 1), right3(rest, 0), NN)
            turned = mm(left3([p[:, lo:hi] for p in parts], 1), right3(rest, 1), NT)
            for i in range(hi, n, PAIR):
                outs[i // PAIR] += turned[:, i - hi : i - hi + PAIR]
    return jnp.concatenate(outs, 1)


def back_kernel(blocks, total_rows, devices, parts, *refs):
    pos_ref, sums_ref, grad_ref = refs[:3]
    xt_refs, white_refs = refs[3:5], refs[5:7]
    part_refs = refs[7 : 7 + parts]
    out_ref, wide_ref, pay_ref = refs[7 + parts :]
    gather_into(pos_ref[0, 0], part_refs, pay_ref, devices)
    n = blocks * BLK
    sums = split2(jnp.broadcast_to(get_row(sums_ref, blocks, blocks), (16, n)))
    rows = [jnp.concatenate([w[...], s], 0) for w, s in zip(white_refs, sums)]
    firsts = jnp.concatenate([grad_ref[...], jnp.broadcast_to(get_row(sums_ref, 0, blocks), (16, n))], 0)
    diagonals = [sums_ref[2 * blocks + p : 2 * blocks + p + 1, :] for p in range(blocks // 2)]
    left = split2(firsts - moment_product(rows, pay_ref, diagonals, blocks) / (total_rows - 1))
    local = grad_ref.shape[0]
    for lo in range(0, n, PAIR):
        here = slice(lo, lo + PAIR)
        cent = mm(left3([p[:, lo:] for p in left], 1), right3([x[here, lo:] for x in xt_refs], 1), NT)
        grad_z = (cent[:local] - cent[local : local + 1, :] / total_rows).astype(bf16)
        out_ref[:, here] = grad_z
        wide_ref[:, here] = grad_z.astype(f32)


def call(kernel, outs, *args, scratch=(), limit=24, places=None):
    return pl.pallas_call(
        kernel,
        out_shape=tuple(jax.ShapeDtypeStruct(s, t) for s, t in outs),
        in_specs=[SMEM if a.dtype == jnp.int32 and a.size == 1 else (VMEM if places is None else HBM) for a in args],
        out_specs=(VMEM,) * len(outs) if places is None else places,
        scratch_shapes=list(scratch),
        compiler_params=pltpu.CompilerParams(vmem_limit_bytes=limit * 2**20),
    )(*args)


def halving():
    per, groups = lax.axis_size("dp"), lax.axis_size("group")
    group = [per << i for i in range(groups.bit_length() - 1)]
    rest = [2 << i for i in range(per.bit_length() - 2)]
    return (group + rest, group[::-1] + rest, rest + group), (3, 3, 2)


def weight_sums(turned, mine, wide, weight):
    orders, shares = halving()
    unit = wide.shape[1] // sum(shares)
    other = swap(wide, 1, 1)
    kept, first, at = [], [], 0
    for share, h in zip(shares, turned):
        shape = ((h.shape[0] // 2, share * unit), f32)
        k, s = call(functools.partial(part_kernel, at * unit, share * unit), [shape, shape], h, mine, other)
        kept.append(k)
        first.append(s)
        at += share
    first[-1], mine = lax.optimization_barrier((first[-1], mine))
    sent = [swap(s, order[0], 1) for s, order in zip(first, orders)]
    product = mm(mine, weight, NT).astype(bf16)
    kept, product = lax.optimization_barrier((kept, product))
    orders = list(orders)
    last = kept[-1]
    for step in range(1, len(orders[0])):
        if len(orders) == 3 and orders[0][step:] == orders[1][step:]:
            both = lax.optimization_barrier((kept[0], sent[0], kept[1], sent[1], last))
            last = both[4]
            kept = [jnp.concatenate([both[0], both[2]], 1), kept[2]]
            sent = [jnp.concatenate([both[1], both[3]], 1), sent[2]]
            orders = orders[1:]
        for p, order in enumerate(orders):
            k, r, last = lax.optimization_barrier((kept[p], sent[p], last))
            size = k.shape[0] // 2
            last = k[size:] + r[size:]
            kept[p] = k[:size] + r[:size]
            sent[p] = swap(last, order[step], 1)
    return jnp.concatenate([k + r for k, r in zip(kept, sent)], 1), product


def body(hidden, weight, partners):
    local, hid = hidden.shape
    emb = weight.shape[1]
    blocks = emb // BLK
    devices = lax.axis_size("group") * lax.axis_size("dp")
    total_rows = local * devices
    _, packed = starts(blocks)
    rows = padded(packed)
    half = rows // 2
    extra = -(-(blocks // 2) // 8) * 8
    pos = place()
    pay_scratch = pltpu.VMEM((rows, BLK), f32)

    slabs = 4
    embedded, keep, send = call(
        functools.partial(front_kernel, blocks, devices),
        [((local, emb), f32)] + [((half + blocks + extra, BLK), f32)] * 2,
        pos,
        hidden,
        weight,
        scratch=[
            pay_scratch,
            pltpu.VMEM((local, hid), bf16),
            pltpu.VMEM((hid, emb), bf16),
            pltpu.VMEM((local, emb), f32),
            pltpu.SemaphoreType.DMA((slabs + 2,)),
        ],
        limit=58,
        places=(HBM, VMEM, VMEM),
    )
    keep, send, early = lax.optimization_barrier((keep, send, hidden))
    me = (lax.axis_index("group") * lax.axis_size("dp") + lax.axis_index("dp")).astype(jnp.int32).reshape(1, 1)
    turned_keep, turned_send = call(
        turn_kernel,
        [((hid // 2, local), f32)] * 2,
        me,
        early,
        scratch=[pltpu.VMEM((hid, local), f32)],
        limit=58,
    )
    orders, _ = halving()
    turned = call(
        functools.partial(order_kernel, orders),
        [((hid // 2, 2 * local), bf16)] * len(orders),
        me,
        turned_keep,
        swap(turned_send, 1, 1),
        scratch=[pltpu.VMEM((hid // 2, 2 * local), f32)],
    )
    part, sums = reduce_scatter(keep, send, half, blocks)
    parts = all_gather(part)
    parts[-1], turned = lax.optimization_barrier((parts[-1], turned))
    xh, xl, wh, wl, grad, keep, send = call(
        functools.partial(factor_kernel, blocks, total_rows, devices, len(parts)),
        [((emb, emb), bf16)] * 2
        + [((local, emb), bf16)] * 2
        + [((local, emb), f32)]
        + [((half + 2 * blocks + extra, BLK), f32)] * 2,
        pos,
        sums,
        embedded,
        partners,
        *parts,
        scratch=[pltpu.VMEM((emb // PAIR, emb + local, PAIR), f32), pay_scratch]
        + [pltpu.VMEM((emb + local, PAIR), bf16)] * 3
        + [pltpu.VMEM((PAIR, PAIR), bf16)] * 3,
        limit=32,
    )
    part, sums = reduce_scatter(keep, send, half, 0)
    parts = all_gather(part)
    grad_z, wide = call(
        functools.partial(back_kernel, blocks, total_rows, devices, len(parts)),
        [((local, emb), bf16), ((local, emb), f32)],
        pos,
        sums,
        grad,
        xh,
        xl,
        wh,
        wl,
        *parts,
        scratch=[pay_scratch],
        limit=32,
    )
    grad_weight, grad_hidden = weight_sums(turned, grad_z, wide, weight)
    return (wh, grad_weight, grad_hidden)


def solution(mesh):
    return jax.shard_map(
        body,
        mesh=mesh,
        in_specs=(P(AXES, None), P(), P(AXES, None)),
        out_specs=(P(AXES, None), P(AXES, None), P(AXES, None)),
        check_vma=False,
    )
```

profile of v0, /device:TPU:0, one launch (start us, length us, event | category | flops | bytes accessed | tf_op | source)
XLA Modules:
  0.0 214.0 jit_solution(9319693026828435049)
XLA Ops:
  0.7 7.0 %shard_map.58 = (f32[256,1024]{1,0:T(8,128)}, f32[2064,128]{1,0:T(8,128)}, f32[2064,128]{1,0:T(8,128)}) custom-call(s32[1,1]{1,0:T(1,128)} %bitcast.pos_ref.refs_0_, bf16[256,2048]{1,0:T(8,128)(2,1)} %hid_ref, bf16[2048,1024]{1,0:T(8,128)(2,1)} %w_hbm.1), custom_call_target="tpu_custom_call" | custom-call | tf_op jit(solution)/shard_map/pallas_call | solution.py:546
  8.2 2.5 %collective-permute-done.refs_1_ = f32[2064,128]{1,0:T(8,128)S(1)} collective-permute-done((f32[2064,128]{1,0:T(8,128)}, f32[2064,128]{1,0:T(8,128)S(1)}, u32[]{:S(2)}, u32[]{:S(2)}) %collective-permute-start) | collective-permute-done | bytes 1056800 | tf_op jit(solution)/shard_map/ppermute | solution.py:109
  12.0 2.9 %collective-permute-start.1 = (f32[536,128]{1,0:T(8,128)S(1)}, f32[536,128]{1,0:T(8,128)S(1)}, u32[]{:S(2)}, u32[]{:S(2)}) collective-permute-start(f32[536,128]{1,0:T(8,128)S(1)} %get-tuple-element.82), channel_id=1, source_target_pairs={{0,8},{1,9},{2,10},{3,11},{4,12},{5,13},{6,14},{7,15},{8,0},{9,1},... | collective-permute-start | bytes 823304 | tf_op jit(solution)/shard_map/ppermute | solution.py:109
  16.5 5.8 %collective-permute-done.1.refs_1_ = f32[536,128]{1,0:T(8,128)S(1)} collective-permute-done((f32[536,128]{1,0:T(8,128)S(1)}, f32[536,128]{1,0:T(8,128)S(1)}, u32[]{:S(2)}, u32[]{:S(2)}) %collective-permute-start.1) | collective-permute-done | bytes 274464 | tf_op jit(solution)/shard_map/ppermute | solution.py:109
  22.3 6.9 %collective-permute-done.2.refs_2_ = f32[536,128]{1,0:T(8,128)S(1)} collective-permute-done((f32[536,128]{1,0:T(8,128)S(1)}, f32[536,128]{1,0:T(8,128)S(1)}, u32[]{:S(2)}, u32[]{:S(2)}) %collective-permute-start.2) | collective-permute-done | bytes 274464 | tf_op jit(solution)/shard_map/ppermute | solution.py:109
  30.9 2.6 %collective-permute-start.5 = (f32[200,128]{1,0:T(8,128)S(1)}, f32[200,128]{1,0:T(8,128)S(1)}, u32[]{:S(2)}, u32[]{:S(2)}) collective-permute-start(f32[200,128]{1,0:T(8,128)S(1)} %get-tuple-element.87), channel_id=1, source_target_pairs={{0,4},{1,5},{2,6},{3,7},{4,0},{5,1},{6,2},{7,3},{8,12},{9,13},{10,... | collective-permute-start | bytes 307208 | tf_op jit(solution)/shard_map/ppermute | solution.py:109
  33.7 3.4 %shard_map.62 = (f32[1024,256]{1,0:T(8,128)}, f32[1024,256]{1,0:T(8,128)}) custom-call(s32[1,1]{1,0:T(1,128)} %bitcast.1.me_ref, bf16[256,2048]{1,0:T(8,128)(2,1)} %hid_ref), custom_call_target="tpu_custom_call" | custom-call | tf_op jit(solution)/shard_map/pallas_call | solution.py:546
  37.1 3.8 %collective-permute-done.5.refs_2_ = f32[200,128]{1,0:T(8,128)S(1)} collective-permute-done((f32[200,128]{1,0:T(8,128)S(1)}, f32[200,128]{1,0:T(8,128)S(1)}, u32[]{:S(2)}, u32[]{:S(2)}) %collective-permute-start.5) | collective-permute-done | bytes 102432 | tf_op jit(solution)/shard_map/ppermute | solution.py:109
  40.9 2.5 %collective-permute-start.9 = (f32[128,128]{1,0:T(8,128)S(1)}, f32[128,128]{1,0:T(8,128)S(1)}, u32[]{:S(2)}, u32[]{:S(2)}) collective-permute-start(f32[128,128]{1,0:T(8,128)S(1)} %get-tuple-element.91), channel_id=1, source_target_pairs={{0,6},{1,7},{2,4},{3,5},{4,2},{5,3},{6,0},{7,1},{8,14},{9,15},{10,... | collective-permute-start | bytes 196616 | tf_op jit(solution)/shard_map/ppermute | solution.py:109
  45.4 3.3 %collective-permute-done.7 = f32[128,128]{1,0:T(8,128)S(1)} collective-permute-done((f32[128,128]{1,0:T(8,128)S(1)}, f32[128,128]{1,0:T(8,128)S(1)}, u32[]{:S(2)}, u32[]{:S(2)}) %collective-permute-start.7) | collective-permute-done | bytes 65568 | tf_op jit(solution)/shard_map/ppermute | solution.py:109
  52.9 5.0 %collective-permute-done.12.refs_7_ = f32[512,128]{1,0:T(8,128)S(1)} collective-permute-done((f32[512,128]{1,0:T(8,128)S(1)}, f32[512,128]{1,0:T(8,128)S(1)}, u32[]{:S(2)}, u32[]{:S(2)}) %collective-permute-start.12) | collective-permute-done | bytes 262176 | tf_op jit(solution)/shard_map/ppermute | solution.py:109
  58.5 2.1 %collective-permute-done.11.refs_6_ = f32[512,128]{1,0:T(8,128)S(1)} collective-permute-done((f32[512,128]{1,0:T(8,128)S(1)}, f32[512,128]{1,0:T(8,128)S(1)}, u32[]{:S(2)}, u32[]{:S(2)}) %collective-permute-start.11) | collective-permute-done | bytes 262176 | tf_op jit(solution)/shard_map/ppermute | solution.py:109
  62.7 35.8 %shard_map.64 = (bf16[1024,1024]{1,0:T(8,128)(2,1)S(1)}, bf16[1024,1024]{1,0:T(8,128)(2,1)S(1)}, bf16[256,1024]{1,0:T(8,128)(2,1)}, bf16[256,1024]{1,0:T(8,128)(...) custom-call(s32[1,1]{1,0:T(1,128)} %bitcast.pos_ref.refs_0_, ...), custom_call_target="tpu_custom_call" | custom-call | tf_op jit(solution)/shard_map/pallas_call | solution.py:546
  98.9 2.3 %collective-permute-done.18.refs_1_ = f32[2072,128]{1,0:T(8,128)S(1)} collective-permute-done((f32[2072,128]{1,0:T(8,128)S(1)}, f32[2072,128]{1,0:T(8,128)S(1)}, u32[]{:S(2)}, u32[]{:S(2)}) %collective-permute-start.18) | collective-permute-done | bytes 1060896 | tf_op jit(solution)/shard_map/ppermute | solution.py:109
  105.0 5.9 %collective-permute-done.19.refs_1_ = f32[536,128]{1,0:T(8,128)S(1)} collective-permute-done((f32[536,128]{1,0:T(8,128)S(1)}, f32[536,128]{1,0:T(8,128)S(1)}, u32[]{:S(2)}, u32[]{:S(2)}) %collective-permute-start.19) | collective-permute-done | bytes 274464 | tf_op jit(solution)/shard_map/ppermute | solution.py:109
  111.8 5.1 %collective-permute-done.21.refs_3_ = f32[536,128]{1,0:T(8,128)S(1)} collective-permute-done((f32[536,128]{1,0:T(8,128)S(1)}, f32[536,128]{1,0:T(8,128)S(1)}, u32[]{:S(2)}, u32[]{:S(2)}) %collective-permute-start.21) | collective-permute-done | bytes 274464 | tf_op jit(solution)/shard_map/ppermute | solution.py:109
  118.1 2.1 collective-permute-start.23
  121.9 3.3 %collective-permute-done.23.refs_2_ = f32[152,128]{1,0:T(8,128)S(1)} collective-permute-done((f32[152,128]{1,0:T(8,128)S(1)}, f32[152,128]{1,0:T(8,128)S(1)}, u32[]{:S(2)}, u32[]{:S(2)}) %collective-permute-start.23) | collective-permute-done | bytes 77856 | tf_op jit(solution)/shard_map/ppermute | solution.py:109
  126.5 2.1 collective-permute-start.27
  129.1 1.9 collective-permute-start.25
  131.0 2.4 %collective-permute-done.25 = f32[128,128]{1,0:T(8,128)S(1)} collective-permute-done((f32[128,128]{1,0:T(8,128)S(1)}, f32[128,128]{1,0:T(8,128)S(1)}, u32[]{:S(2)}, u32[]{:S(2)}) %collective-permute-start.25) | collective-permute-done | bytes 65568 | tf_op jit(solution)/shard_map/ppermute | solution.py:109
  137.9 4.8 %collective-permute-done.30.refs_10_ = f32[512,128]{1,0:T(8,128)S(1)} collective-permute-done((f32[512,128]{1,0:T(8,128)S(1)}, f32[512,128]{1,0:T(8,128)S(1)}, u32[]{:S(2)}, u32[]{:S(2)}) %collective-permute-start.30) | collective-permute-done | bytes 262176 | tf_op jit(solution)/shard_map/ppermute | solution.py:109
  142.8 2.7 %collective-permute-done.29.refs_9_ = f32[512,128]{1,0:T(8,128)S(1)} collective-permute-done((f32[512,128]{1,0:T(8,128)S(1)}, f32[512,128]{1,0:T(8,128)S(1)}, u32[]{:S(2)}, u32[]{:S(2)}) %collective-permute-start.29) | collective-permute-done | bytes 262176 | tf_op jit(solution)/shard_map/ppermute | solution.py:109
  147.4 4.9 %shard_map.68 = (bf16[256,1024]{1,0:T(8,128)(2,1)S(1)}, f32[256,1024]{1,0:T(8,128)S(1)}) custom-call(s32[1,1]{1,0:T(1,128)} %bitcast.pos_ref.refs_0_, f32[24,128]{1,0:T(8,128)S(1)} %get-tuple-element.111.refs_1_, f32[256,1024]{1,0:T(8,128)S(1)} %get-tuple-element.112.refs_2_, bf16[1024,1024]{1,0:T(8,128)(2,1)S(1)} %get-tuple-element.113.refs_3_, ...), custom_call_target="tpu_custom_call" | custom-call | tf_op jit(solution)/shard_map/pallas_call | solution.py:546
  152.5 2.5 %collective-permute-done.35.other_ref = f32[256,1024]{1,0:T(8,128)S(1)} collective-permute-done((f32[256,1024]{1,0:T(8,128)S(1)}, f32[256,1024]{1,0:T(8,128)S(1)}, u32[]{:S(2)}, u32[]{:S(2)}) %collective-permute-start.35) | collective-permute-done | bytes 1048608 | tf_op jit(solution)/shard_map/ppermute | solution.py:109
  160.2 2.3 %convolution_convert_fusion = bf16[256,2048]{1,0:T(8,128)(2,1)} fusion(bf16[256,1024]{1,0:T(8,128)(2,1)S(1)} %get-tuple-element.125.mine_ref, bf16[2048,1024]{1,0:T(8,128)(2,1)S(1)} %copy-done.5), kind=kOutput, calls=%fused_computation | convolution fusion | flops 1074266112 | bytes 5767168 | tf_op jit(solution)/shard_map/dot_general | solution.py:57
  162.5 12.9 %collective-permute-done.36 = f32[512,384]{1,0:T(8,128)S(1)} collective-permute-done((f32[512,384]{1,0:T(8,128)S(1)}, f32[512,384]{1,0:T(8,128)S(1)}, u32[]{:S(2)}, u32[]{:S(2)}) %collective-permute-start.36) | collective-permute-done | bytes 786464 | tf_op jit(solution)/shard_map/ppermute | solution.py:109
  180.7 6.3 %collective-permute-done.39 = f32[256,384]{1,0:T(8,128)S(1)} collective-permute-done((f32[256,384]{1,0:T(8,128)S(1)}, f32[256,384]{1,0:T(8,128)S(1)}, u32[]{:S(2)}, u32[]{:S(2)}) %collective-permute-start.39) | collective-permute-done | bytes 393248 | tf_op jit(solution)/shard_map/ppermute | solution.py:109
  189.0 3.2 %collective-permute-done.42 = f32[256,256]{1,0:T(8,128)S(1)} collective-permute-done((f32[256,256]{1,0:T(8,128)S(1)}, f32[256,256]{1,0:T(8,128)S(1)}, u32[]{:S(2)}, u32[]{:S(2)}) %collective-permute-start.42) | collective-permute-done | bytes 262176 | tf_op jit(solution)/shard_map/ppermute | solution.py:109
  193.7 6.8 %collective-permute-done.41 = f32[128,768]{1,0:T(8,128)S(1)} collective-permute-done((f32[128,768]{1,0:T(8,128)S(1)}, f32[128,768]{1,0:T(8,128)S(1)}, u32[]{:S(2)}, u32[]{:S(2)}) %collective-permute-start.41) | collective-permute-done | bytes 393248 | tf_op jit(solution)/shard_map/ppermute | solution.py:109
  202.3 2.6 %collective-permute-done.45 = f32[64,256]{1,0:T(8,128)S(1)} collective-permute-done((f32[64,256]{1,0:T(8,128)S(1)}, f32[64,256]{1,0:T(8,128)S(1)}, u32[]{:S(2)}, u32[]{:S(2)}) %collective-permute-start.45) | collective-permute-done | bytes 65568 | tf_op jit(solution)/shard_map/ppermute | solution.py:109
  205.0 8.3 %collective-permute-done.43 = f32[64,768]{1,0:T(8,128)S(1)} collective-permute-done((f32[64,768]{1,0:T(8,128)S(1)}, f32[64,768]{1,0:T(8,128)S(1)}, u32[]{:S(2)}, u32[]{:S(2)}) %collective-permute-start.43) | collective-permute-done | bytes 196640 | tf_op jit(solution)/shard_map/ppermute | solution.py:109
  (106 shorter events, 47.1 us)
Async XLA Ops:
  12.0 10.3 %collective-permute-start.1 = (f32[536,128]{1,0:T(8,128)S(1)}, f32[536,128]{1,0:T(8,128)S(1)}, u32[]{:S(2)}, u32[]{:S(2)}) collective-permute-start(f32[536,128]{1,0:T(8,128)S(1)} %get-tuple-element.82), channel_id=1, source_target_pairs={{0,8},{1,9},{2,10},{3,11},{4,12},{5,13},{6,14},{7,15},{8,0},{9,1},... | collective-permute-start | bytes 823304 | tf_op jit(solution)/shard_map/ppermute | solution.py:109
  14.9 14.2 %collective-permute-start.2 = (f32[536,128]{1,0:T(8,128)S(1)}, f32[536,128]{1,0:T(8,128)S(1)}, u32[]{:S(2)}, u32[]{:S(2)}) collective-permute-start(f32[536,128]{1,0:T(8,128)S(1)} %get-tuple-element.83), channel_id=1, source_target_pairs={{0,16},{1,17},{2,18},{3,19},{4,20},{5,21},{6,22},{7,23},{8,24},{9,... | collective-permute-start | bytes 823304 | tf_op jit(solution)/shard_map/ppermute | solution.py:109
  16.5 12.7 %collective-permute-start.3 = (f32[536,128]{1,0:T(8,128)S(1)}, f32[536,128]{1,0:T(8,128)S(1)}, u32[]{:S(2)}, u32[]{:S(2)}) collective-permute-start(f32[536,128]{1,0:T(8,128)S(1)} %get-tuple-element.84), channel_id=1, source_target_pairs={{0,24},{1,25},{2,26},{3,27},{4,28},{5,29},{6,30},{7,31},{8,16},{9,... | collective-permute-start | bytes 823304 | tf_op jit(solution)/shard_map/ppermute | solution.py:109
  29.3 7.8 %collective-permute-start.4 = (f32[200,128]{1,0:T(8,128)S(1)}, f32[200,128]{1,0:T(8,128)S(1)}, u32[]{:S(2)}, u32[]{:S(2)}) collective-permute-start(f32[200,128]{1,0:T(8,128)S(1)} %get-tuple-element.86), channel_id=1, source_target_pairs={{0,2},{1,3},{2,0},{3,1},{4,6},{5,7},{6,4},{7,5},{8,10},{9,11},{10,... | collective-permute-start | bytes 307208 | tf_op jit(solution)/shard_map/ppermute | solution.py:109
  30.9 10.0 %collective-permute-start.5 = (f32[200,128]{1,0:T(8,128)S(1)}, f32[200,128]{1,0:T(8,128)S(1)}, u32[]{:S(2)}, u32[]{:S(2)}) collective-permute-start(f32[200,128]{1,0:T(8,128)S(1)} %get-tuple-element.87), channel_id=1, source_target_pairs={{0,4},{1,5},{2,6},{3,7},{4,0},{5,1},{6,2},{7,3},{8,12},{9,13},{10,... | collective-permute-start | bytes 307208 | tf_op jit(solution)/shard_map/ppermute | solution.py:109
  33.5 7.4 %collective-permute-start.6 = (f32[200,128]{1,0:T(8,128)S(1)}, f32[200,128]{1,0:T(8,128)S(1)}, u32[]{:S(2)}, u32[]{:S(2)}) collective-permute-start(f32[200,128]{1,0:T(8,128)S(1)} %get-tuple-element.88), channel_id=1, source_target_pairs={{0,6},{1,7},{2,4},{3,5},{4,2},{5,3},{6,0},{7,1},{8,14},{9,15},{10,... | collective-permute-start | bytes 307208 | tf_op jit(solution)/shard_map/ppermute | solution.py:109
  37.1 24.0 %collective-permute-start.17 = (f32[1024,256]{1,0:T(8,128)}, f32[1024,256]{1,0:T(8,128)S(1)}, u32[]{:S(2)}, u32[]{:S(2)}) collective-permute-start(f32[1024,256]{1,0:T(8,128)} %get-tuple-element.94), channel_id=1, source_target_pairs={{0,1},{1,0},{2,3},{3,2},{4,5},{5,4},{6,7},{7,6},{8,9},{9,8},{10,11... | collective-permute-start | bytes 3145736 | tf_op jit(solution)/shard_map/ppermute | solution.py:109
  40.9 8.4 %collective-permute-start.9 = (f32[128,128]{1,0:T(8,128)S(1)}, f32[128,128]{1,0:T(8,128)S(1)}, u32[]{:S(2)}, u32[]{:S(2)}) collective-permute-start(f32[128,128]{1,0:T(8,128)S(1)} %get-tuple-element.91), channel_id=1, source_target_pairs={{0,6},{1,7},{2,4},{3,5},{4,2},{5,3},{6,0},{7,1},{8,14},{9,15},{10,... | collective-permute-start | bytes 196616 | tf_op jit(solution)/shard_map/ppermute | solution.py:109
  43.5 5.9 %collective-permute-start.8 = (f32[128,128]{1,0:T(8,128)S(1)}, f32[128,128]{1,0:T(8,128)S(1)}, u32[]{:S(2)}, u32[]{:S(2)}) collective-permute-start(f32[128,128]{1,0:T(8,128)S(1)} %get-tuple-element.91), channel_id=1, source_target_pairs={{0,4},{1,5},{2,6},{3,7},{4,0},{5,1},{6,2},{7,3},{8,12},{9,13},{10,... | collective-permute-start | bytes 196616 | tf_op jit(solution)/shard_map/ppermute | solution.py:109
  49.4 8.6 %collective-permute-start.12 = (f32[512,128]{1,0:T(8,128)S(1)}, f32[512,128]{1,0:T(8,128)S(1)}, u32[]{:S(2)}, u32[]{:S(2)}) collective-permute-start(f32[512,128]{1,0:T(8,128)S(1)} %constant_dynamic-update-slice_fusion.refs_4_), channel_id=1, source_target_pairs={{0,24},{1,25},{2,26},{3,27},{4,28},{5,29},{6,30},{7,31},{8,16},{9,... | collective-permute-start | bytes 786440 | tf_op jit(solution)/shard_map/ppermute | solution.py:109
  50.9 9.8 %collective-permute-start.11 = (f32[512,128]{1,0:T(8,128)S(1)}, f32[512,128]{1,0:T(8,128)S(1)}, u32[]{:S(2)}, u32[]{:S(2)}) collective-permute-start(f32[512,128]{1,0:T(8,128)S(1)} %constant_dynamic-update-slice_fusion.refs_4_), channel_id=1, source_target_pairs={{0,16},{1,17},{2,18},{3,19},{4,20},{5,21},{6,22},{7,23},{8,24},{9,... | collective-permute-start | bytes 786440 | tf_op jit(solution)/shard_map/ppermute | solution.py:109
  52.3 8.6 %collective-permute-start.10 = (f32[512,128]{1,0:T(8,128)S(1)}, f32[512,128]{1,0:T(8,128)S(1)}, u32[]{:S(2)}, u32[]{:S(2)}) collective-permute-start(f32[512,128]{1,0:T(8,128)S(1)} %constant_dynamic-update-slice_fusion.refs_4_), channel_id=1, source_target_pairs={{0,8},{1,9},{2,10},{3,11},{4,12},{5,13},{6,14},{7,15},{8,0},{9,1},... | collective-permute-start | bytes 786440 | tf_op jit(solution)/shard_map/ppermute | solution.py:109
  101.4 9.5 %collective-permute-start.19 = (f32[536,128]{1,0:T(8,128)S(1)}, f32[536,128]{1,0:T(8,128)S(1)}, u32[]{:S(2)}, u32[]{:S(2)}) collective-permute-start(f32[536,128]{1,0:T(8,128)S(1)} %get-tuple-element.104), channel_id=1, source_target_pairs={{0,8},{1,9},{2,10},{3,11},{4,12},{5,13},{6,14},{7,15},{8,0},{9,1},... | collective-permute-start | bytes 823304 | tf_op jit(solution)/shard_map/ppermute | solution.py:109
  102.7 9.1 %collective-permute-start.20 = (f32[536,128]{1,0:T(8,128)S(1)}, f32[536,128]{1,0:T(8,128)S(1)}, u32[]{:S(2)}, u32[]{:S(2)}) collective-permute-start(f32[536,128]{1,0:T(8,128)S(1)} %get-tuple-element.105), channel_id=1, source_target_pairs={{0,16},{1,17},{2,18},{3,19},{4,20},{5,21},{6,22},{7,23},{8,24},{9,... | collective-permute-start | bytes 823304 | tf_op jit(solution)/shard_map/ppermute | solution.py:109
  103.6 13.3 %collective-permute-start.21 = (f32[536,128]{1,0:T(8,128)S(1)}, f32[536,128]{1,0:T(8,128)S(1)}, u32[]{:S(2)}, u32[]{:S(2)}) collective-permute-start(f32[536,128]{1,0:T(8,128)S(1)} %get-tuple-element.106), channel_id=1, source_target_pairs={{0,24},{1,25},{2,26},{3,27},{4,28},{5,29},{6,30},{7,31},{8,16},{9,... | collective-permute-start | bytes 823304 | tf_op jit(solution)/shard_map/ppermute | solution.py:109
  118.1 7.2 %collective-permute-start.23 = (f32[152,128]{1,0:T(8,128)S(1)}, f32[152,128]{1,0:T(8,128)S(1)}, u32[]{:S(2)}, u32[]{:S(2)}) collective-permute-start(f32[152,128]{1,0:T(8,128)S(1)} %get-tuple-element.109), channel_id=1, source_target_pairs={{0,4},{1,5},{2,6},{3,7},{4,0},{5,1},{6,2},{7,3},{8,12},{9,13},{10,... | collective-permute-start | bytes 233480 | tf_op jit(solution)/shard_map/ppermute | solution.py:109
  120.2 6.3 %collective-permute-start.24 = (f32[152,128]{1,0:T(8,128)S(1)}, f32[152,128]{1,0:T(8,128)S(1)}, u32[]{:S(2)}, u32[]{:S(2)}) collective-permute-start(f32[152,128]{1,0:T(8,128)S(1)} %get-tuple-element.110), channel_id=1, source_target_pairs={{0,6},{1,7},{2,4},{3,5},{4,2},{5,3},{6,0},{7,1},{8,14},{9,15},{10,... | collective-permute-start | bytes 233480 | tf_op jit(solution)/shard_map/ppermute | solution.py:109
  126.5 7.9 %collective-permute-start.27 = (f32[128,128]{1,0:T(8,128)S(1)}, f32[128,128]{1,0:T(8,128)S(1)}, u32[]{:S(2)}, u32[]{:S(2)}) collective-permute-start(f32[128,128]{1,0:T(8,128)S(1)} %get-tuple-element.116), channel_id=1, source_target_pairs={{0,6},{1,7},{2,4},{3,5},{4,2},{5,3},{6,0},{7,1},{8,14},{9,15},{10,... | collective-permute-start | bytes 196616 | tf_op jit(solution)/shard_map/ppermute | solution.py:109
  128.6 5.8 %collective-permute-start.26 = (f32[128,128]{1,0:T(8,128)S(1)}, f32[128,128]{1,0:T(8,128)S(1)}, u32[]{:S(2)}, u32[]{:S(2)}) collective-permute-start(f32[128,128]{1,0:T(8,128)S(1)} %get-tuple-element.116), channel_id=1, source_target_pairs={{0,4},{1,5},{2,6},{3,7},{4,0},{5,1},{6,2},{7,3},{8,12},{9,13},{10,... | collective-permute-start | bytes 196616 | tf_op jit(solution)/shard_map/ppermute | solution.py:109
  134.4 8.4 %collective-permute-start.30 = (f32[512,128]{1,0:T(8,128)S(1)}, f32[512,128]{1,0:T(8,128)S(1)}, u32[]{:S(2)}, u32[]{:S(2)}) collective-permute-start(f32[512,128]{1,0:T(8,128)S(1)} %constant_dynamic-update-slice_fusion.4.refs_7_), channel_id=1, source_target_pairs={{0,24},{1,25},{2,26},{3,27},{4,28},{5,29},{6,30},{7,31},{8,16},{9,... | collective-permute-start | bytes 786440 | tf_op jit(solution)/shard_map/ppermute | solution.py:109
  136.0 9.5 %collective-permute-start.29 = (f32[512,128]{1,0:T(8,128)S(1)}, f32[512,128]{1,0:T(8,128)S(1)}, u32[]{:S(2)}, u32[]{:S(2)}) collective-permute-start(f32[512,128]{1,0:T(8,128)S(1)} %constant_dynamic-update-slice_fusion.4.refs_7_), channel_id=1, source_target_pairs={{0,16},{1,17},{2,18},{3,19},{4,20},{5,21},{6,22},{7,23},{8,24},{9,... | collective-permute-start | bytes 786440 | tf_op jit(solution)/shard_map/ppermute | solution.py:109
  136.7 8.7 %collective-permute-start.28 = (f32[512,128]{1,0:T(8,128)S(1)}, f32[512,128]{1,0:T(8,128)S(1)}, u32[]{:S(2)}, u32[]{:S(2)}) collective-permute-start(f32[512,128]{1,0:T(8,128)S(1)} %constant_dynamic-update-slice_fusion.4.refs_7_), channel_id=1, source_target_pairs={{0,8},{1,9},{2,10},{3,11},{4,12},{5,13},{6,14},{7,15},{8,0},{9,1},... | collective-permute-start | bytes 786440 | tf_op jit(solution)/shard_map/ppermute | solution.py:109
  137.9 8.0 %collective-permute-start.31 = (f32[512,128]{1,0:T(8,128)S(1)}, f32[512,128]{1,0:T(8,128)S(1)}, u32[]{:S(2)}, u32[]{:S(2)}) collective-permute-start(f32[512,128]{1,0:T(8,128)S(1)} %constant_dynamic-update-slice_fusion.4.refs_7_), channel_id=1, source_target_pairs={{0,1},{1,0},{2,3},{3,2},{4,5},{5,4},{6,7},{7,6},{8,9},{9,8},{10,11... | collective-permute-start | bytes 786440 | tf_op jit(solution)/shard_map/ppermute | solution.py:109
  155.7 19.7 %collective-permute-start.36 = (f32[512,384]{1,0:T(8,128)S(1)}, f32[512,384]{1,0:T(8,128)S(1)}, u32[]{:S(2)}, u32[]{:S(2)}) collective-permute-start(f32[512,384]{1,0:T(8,128)S(1)} %get-tuple-element.127), channel_id=1, source_target_pairs={{0,8},{1,9},{2,10},{3,11},{4,12},{5,13},{6,14},{7,15},{8,0},{9,1},... | collective-permute-start | bytes 2359304 | tf_op jit(solution)/shard_map/ppermute | solution.py:109
  157.4 19.4 %collective-permute-start.38 = (f32[512,384]{1,0:T(8,128)S(1)}, f32[512,384]{1,0:T(8,128)S(1)}, u32[]{:S(2)}, u32[]{:S(2)}) collective-permute-start(f32[512,384]{1,0:T(8,128)S(1)} %get-tuple-element.132), channel_id=1, source_target_pairs={{0,16},{1,17},{2,18},{3,19},{4,20},{5,21},{6,22},{7,23},{8,24},{9,... | collective-permute-start | bytes 2359304 | tf_op jit(solution)/shard_map/ppermute | solution.py:109
  159.2 19.6 %collective-permute-start.40 = (f32[512,256]{1,0:T(8,128)S(1)}, f32[512,256]{1,0:T(8,128)S(1)}, u32[]{:S(2)}, u32[]{:S(2)}) collective-permute-start(f32[512,256]{1,0:T(8,128)S(1)} %get-tuple-element.135), channel_id=1, source_target_pairs={{0,2},{1,3},{2,0},{3,1},{4,6},{5,7},{6,4},{7,5},{8,10},{9,11},{10,... | collective-permute-start | bytes 1572872 | tf_op jit(solution)/shard_map/ppermute | solution.py:109
  176.9 10.1 %collective-permute-start.39 = (f32[256,384]{1,0:T(8,128)S(1)}, f32[256,384]{1,0:T(8,128)S(1)}, u32[]{:S(2)}, u32[]{:S(2)}) collective-permute-start(f32[256,384]{1,0:T(8,128)S(1)} %get-tuple-element.154), channel_id=1, source_target_pairs={{0,8},{1,9},{2,10},{3,11},{4,12},{5,13},{6,14},{7,15},{8,0},{9,1},... | collective-permute-start | bytes 1179656 | tf_op jit(solution)/shard_map/ppermute | solution.py:109
  178.0 9.7 %collective-permute-start.37 = (f32[256,384]{1,0:T(8,128)S(1)}, f32[256,384]{1,0:T(8,128)S(1)}, u32[]{:S(2)}, u32[]{:S(2)}) collective-permute-start(f32[256,384]{1,0:T(8,128)S(1)} %get-tuple-element.156), channel_id=1, source_target_pairs={{0,16},{1,17},{2,18},{3,19},{4,20},{5,21},{6,22},{7,23},{8,24},{9,... | collective-permute-start | bytes 1179656 | tf_op jit(solution)/shard_map/ppermute | solution.py:109
  178.9 13.3 %collective-permute-start.42 = (f32[256,256]{1,0:T(8,128)S(1)}, f32[256,256]{1,0:T(8,128)S(1)}, u32[]{:S(2)}, u32[]{:S(2)}) collective-permute-start(f32[256,256]{1,0:T(8,128)S(1)} %get-tuple-element.157), channel_id=1, source_target_pairs={{0,4},{1,5},{2,6},{3,7},{4,0},{5,1},{6,2},{7,3},{8,12},{9,13},{10,... | collective-permute-start | bytes 786440 | tf_op jit(solution)/shard_map/ppermute | solution.py:109
  188.0 12.5 %collective-permute-start.41 = (f32[128,768]{1,0:T(8,128)S(1)}, f32[128,768]{1,0:T(8,128)S(1)}, u32[]{:S(2)}, u32[]{:S(2)}) collective-permute-start(f32[128,768]{1,0:T(8,128)S(1)} %get-tuple-element.152), channel_id=1, source_target_pairs={{0,2},{1,3},{2,0},{3,1},{4,6},{5,7},{6,4},{7,5},{8,10},{9,11},{10,... | collective-permute-start | bytes 1179656 | tf_op jit(solution)/shard_map/ppermute | solution.py:109
  192.3 8.3 %collective-permute-start.44 = (f32[128,256]{1,0:T(8,128)S(1)}, f32[128,256]{1,0:T(8,128)S(1)}, u32[]{:S(2)}, u32[]{:S(2)}) collective-permute-start(f32[128,256]{1,0:T(8,128)S(1)} %get-tuple-element.159), channel_id=1, source_target_pairs={{0,8},{1,9},{2,10},{3,11},{4,12},{5,13},{6,14},{7,15},{8,0},{9,1},... | collective-permute-start | bytes 393224 | tf_op jit(solution)/shard_map/ppermute | solution.py:109
  201.9 11.3 %collective-permute-start.43 = (f32[64,768]{1,0:T(8,128)S(1)}, f32[64,768]{1,0:T(8,128)S(1)}, u32[]{:S(2)}, u32[]{:S(2)}) collective-permute-start(f32[64,768]{1,0:T(8,128)S(1)} %slice_add_fusion.8), channel_id=1, source_target_pairs={{0,4},{1,5},{2,6},{3,7},{4,0},{5,1},{6,2},{7,3},{8,12},{9,13},{10,... | collective-permute-start | bytes 589832 | tf_op jit(solution)/shard_map/ppermute | solution.py:109
  (20 other events, 169.2 us)
where the time goes:
time: 214 us
  waiting for transfers between devices  107 us (50%)
  Pallas kernels  53.7 us (25%)
  starting transfers between devices  46.5 us (22%)
  local copies, waits for them, and re-layouts  2.52 us (1%)
  matrix products  2.26 us (1%)
    ppermute x46, waiting for transfers between devices, swap(): return lax.ppermute(x, AXES, [(i, i ^ by * stride) for i in range(count)])  107 us
    pallas_call x14, Pallas kernels, call(): pl.pallas_call(kernel, out_shape=tuple((jax.ShapeDtypeStruct(s, t) for s,...  53.7 us
    ppermute x46, starting transfers between devices, swap(): return lax.ppermute(x, AXES, [(i, i ^ by * stride) for i in range(count)])  46.5 us
  transfers between devices with their start and end apart: 46, of which 31 were waited for; matrix products, arithmetic and copies ran while one was open for 1% of the time, Pallas kernels for 2%

commit v1 on v0

--- a/solution.py
+++ b/solution.py
@@ -145,14 +145,16 @@
     return pieces
 
 
-def all_gather(x):
+def all_gather(x, beside=()):
     steps = rounds()
     parts = [x]
     for at in range(len(steps) - 1, 0, -1):
         stride, radix = steps[at]
         whole = parts[0] if len(parts) == 1 else jnp.concatenate(parts, 0)
         parts = [whole] + [swap(whole, stride, by) for by in range(1, radix)]
-    return parts + [swap(p, 1, 1) for p in parts]
+        if at == len(steps) - 1:
+            parts, beside = lax.optimization_barrier((parts, beside))
+    return parts + [swap(p, 1, 1) for p in parts], beside
 
 
 def padded(rows):
@@ -233,7 +235,7 @@
     return one, two
 
 
-def front_kernel(blocks, devices, pos_ref, hid_hbm, w_hbm, emb_hbm, keep_ref, send_ref, pay_ref, hid_ref, w_ref, emb_ref, sems):
+def front_kernel(blocks, devices, pos_ref, hid_hbm, w_hbm, emb_hbm, keep_ref, send_ref, hid_ref, pay_ref, w_ref, emb_ref, sems):
     slabs = sems.shape[0] - 2
     deep = w_hbm.shape[0] // slabs
     copies = [pltpu.make_async_copy(hid_hbm, hid_ref, sems.at[slabs])]
@@ -270,25 +272,27 @@
 
 
 def order_kernel(orders, me_ref, keep_ref, got_ref, *refs):
-    outs, part_ref = refs[:-1], refs[-1]
+    near_refs, far_refs, part_ref = refs[: len(orders)], refs[len(orders) : -1], refs[-1]
     chip = me_ref[0, 0] // 2
-    own = part_ref.shape[0] >> len(orders[0])
+    half = part_ref.shape[0]
+    own = half * 2 >> len(orders[0])
     local = keep_ref.shape[1]
-    for bits, out in zip(orders, outs):
-        for i in range(1 << len(bits)):
-            far = 0
-            for t, bit in enumerate(reversed(bits)):
-                far |= bit * ((i >> t) & 1)
-            rows = pl.ds(pl.multiple_of((chip ^ (far // 2)) * own, 8), own)
-            part_ref[i * own : (i + 1) * own, :local] = keep_ref[rows, :]
-            part_ref[i * own : (i + 1) * own, local:] = got_ref[rows, :]
-        out[...] = part_ref[...].astype(bf16)
-
-
-def part_kernel(at, width, turned_ref, mine_ref, other_ref, keep_ref, send_ref):
-    cols = slice(at, at + width)
-    rows = jnp.concatenate([mine_ref[:, cols], other_ref[:, cols]], 0).astype(bf16)
-    part = mm(turned_ref[...], rows, NN)
+    for bits, near_ref, far_ref in zip(orders, near_refs, far_refs):
+        for side, out in ((0, part_ref), (1, far_ref)):
+            for i in range(half // own):
+                far = bits[0] * side
+                for t, bit in enumerate(reversed(bits[1:])):
+                    far |= bit * ((i >> t) & 1)
+                rows = pl.ds(pl.multiple_of((chip ^ (far // 2)) * own, 8), own)
+                out[i * own : (i + 1) * own, :local] = keep_ref[rows, :]
+                out[i * own : (i + 1) * own, local:] = got_ref[rows, :]
+        near_ref[...] = part_ref[...].astype(bf16)
+
+
+def part_kernel(near_ref, far_ref, *refs):
+    rows, (keep_ref, send_ref) = refs[:4], refs[4:]
+    left = jnp.concatenate([near_ref[...], far_ref[...].astype(bf16)], 1)
+    part = mm(left, jnp.concatenate([r[...].astype(bf16) for r in rows], 0), NN)
     half = keep_ref.shape[0]
     keep_ref[...] = part[:half]
     send_ref[...] = part[half:]
@@ -365,9 +369,8 @@
 def factor_kernel(blocks, total_rows, devices, parts, *refs):
     pos_ref, sums_ref, emb_ref, partner_ref = refs[:4]
     part_refs = refs[4 : 4 + parts]
-    xt_refs, white_refs = refs[4 + parts : 6 + parts], refs[6 + parts : 8 + parts]
-    grad_ref, keep_ref, send_ref, a_ref, pay_ref, high_ref, mid_ref, low_ref = refs[8 + parts : 16 + parts]
-    x_refs = refs[16 + parts :]
+    white_refs, x_refs = refs[4 + parts : 6 + parts], refs[6 + parts : 9 + parts]
+    a_ref, grad_ref, keep_ref, send_ref, pay_ref, high_ref, mid_ref, low_ref = refs[9 + parts :]
     pos = pos_ref[0, 0]
     gather_into(pos, part_refs, pay_ref, devices)
     n = blocks * BLK
@@ -473,13 +476,7 @@
         return 0
 
     lax.fori_loop(1, pairs, step, 0)
-    x = [ref[...] for ref in x_refs]
-    for tile in list(range(pairs - 1)) + [None]:
-        solve(pairs - 1, tile, x)
-    for p in range(pairs):
-        lo, hi = p * PAIR, (p + 1) * PAIR
-        for ref, part in zip(xt_refs, split2(a_ref[p, 0:hi, :])):
-            ref[0:hi, lo:hi] = part
+    solve(pairs - 1, None, [ref[...] for ref in x_refs])
     white = jnp.concatenate([a_ref[p, n:, :] for p in range(pairs)], 1)
     white_parts = split2(white)
     for ref, part in zip(white_refs, white_parts):
@@ -501,6 +498,19 @@
     put_extra((keep_ref, send_ref), pay_ref.shape[0] // 2, totals + diagonals)
 
 
+def inverse_kernel(a_ref, *refs):
+    x, outs = [ref[...] for ref in refs[:3]], refs[3:]
+    pairs = a_ref.shape[0]
+    for p in range(pairs):
+        lo, hi = p * PAIR, (p + 1) * PAIR
+        for i in range(0, hi, PAIR):
+            have = a_ref[p, i : i + PAIR, :]
+            if p == pairs - 1 and i < lo:
+                have = mm(left6(split3(have), 1), right6(x, 1), NT)
+            for out, part in zip(outs, split2(have)):
+                out[i : i + PAIR, lo:hi] = part
+
+
 def moment_product(parts, pay_ref, diagonals, blocks):
     n = blocks * BLK
     at, _ = starts(blocks)
@@ -521,11 +531,11 @@
     return jnp.concatenate(outs, 1)
 
 
-def back_kernel(blocks, total_rows, devices, parts, *refs):
+def back_kernel(blocks, total_rows, devices, parts, shares, *refs):
     pos_ref, sums_ref, grad_ref = refs[:3]
     xt_refs, white_refs = refs[3:5], refs[5:7]
     part_refs = refs[7 : 7 + parts]
-    out_ref, wide_ref, pay_ref = refs[7 + parts :]
+    out_ref, wide_refs, pay_ref = refs[7 + parts], refs[8 + parts : -1], refs[-1]
     gather_into(pos_ref[0, 0], part_refs, pay_ref, devices)
     n = blocks * BLK
     sums = split2(jnp.broadcast_to(get_row(sums_ref, blocks, blocks), (16, n)))
@@ -539,10 +549,16 @@
         cent = mm(left3([p[:, lo:] for p in left], 1), right3([x[here, lo:] for x in xt_refs], 1), NT)
         grad_z = (cent[:local] - cent[local : local + 1, :] / total_rows).astype(bf16)
         out_ref[:, here] = grad_z
-        wide_ref[:, here] = grad_z.astype(f32)
-
-
-def call(kernel, outs, *args, scratch=(), limit=24, places=None):
+        wide = grad_z.astype(f32)
+        at = 0
+        for ref, share in zip(wide_refs, shares):
+            first, last = max(at, lo), min(at + share, lo + PAIR)
+            if first < last:
+                ref[:, first - at : last - at] = wide[:, first - lo : last - lo]
+            at += share
+
+
+def call(kernel, outs, *args, scratch=(), limit=24, places=None, flops=10**6):
     return pl.pallas_call(
         kernel,
         out_shape=tuple(jax.ShapeDtypeStruct(s, t) for s, t in outs),
@@ -550,34 +566,36 @@
         out_specs=(VMEM,) * len(outs) if places is None else places,
         scratch_shapes=list(scratch),
         compiler_params=pltpu.CompilerParams(vmem_limit_bytes=limit * 2**20),
+        cost_estimate=pl.CostEstimate(flops=flops, bytes_accessed=10**6, transcendentals=0),
     )(*args)
 
 
-def halving():
+def halving(emb):
     per, groups = lax.axis_size("dp"), lax.axis_size("group")
     group = [per << i for i in range(groups.bit_length() - 1)]
     rest = [2 << i for i in range(per.bit_length() - 2)]
-    return (group + rest, group[::-1] + rest, rest + group), (3, 3, 2)
-
-
-def weight_sums(turned, mine, wide, weight):
-    orders, shares = halving()
-    unit = wide.shape[1] // sum(shares)
-    other = swap(wide, 1, 1)
-    kept, first, at = [], [], 0
-    for share, h in zip(shares, turned):
-        shape = ((h.shape[0] // 2, share * unit), f32)
-        k, s = call(functools.partial(part_kernel, at * unit, share * unit), [shape, shape], h, mine, other)
-        kept.append(k)
-        first.append(s)
-        at += share
-    first[-1], mine = lax.optimization_barrier((first[-1], mine))
-    sent = [swap(s, order[0], 1) for s, order in zip(first, orders)]
+    return (group + rest, group[::-1] + rest, rest + group), (3 * emb // 8, 3 * emb // 8, emb // 4)
+
+
+def weight_sums(near, far, wide, mine, weight):
+    orders, shares = halving(weight.shape[1])
+    there = [swap(w, order[0], 1) for w, order in zip(wide, orders)]
+    beside = [swap(w, 1, 1) for w in wide]
     product = mm(mine, weight, NT).astype(bf16)
-    kept, product = lax.optimization_barrier((kept, product))
+    beside, product = lax.optimization_barrier((beside, product))
+    kept, sent, last = [None] * len(orders), [None] * len(orders), product
+    for group in ((2,), (0, 1)):
+        ins = [there[p] for p in group], [beside[p] for p in group], last
+        ins, others, last = lax.optimization_barrier(ins)
+        if group == (2,):
+            product = last
+        across = [swap(t, 1, 1) for t in ins]
+        for p, t, o, c in zip(group, ins, others, across):
+            shape = ((near[p].shape[0] // 2, shares[p]), f32)
+            kept[p], last = call(part_kernel, [shape, shape], near[p], far[p], wide[p], o, t, c)
+            sent[p] = swap(last, orders[p][1], 1)
     orders = list(orders)
-    last = kept[-1]
-    for step in range(1, len(orders[0])):
+    for step in range(2, len(orders[0])):
         if len(orders) == 3 and orders[0][step:] == orders[1][step:]:
             both = lax.optimization_barrier((kept[0], sent[0], kept[1], sent[1], last))
             last = both[4]
@@ -607,23 +625,19 @@
     pay_scratch = pltpu.VMEM((rows, BLK), f32)
 
     slabs = 4
-    embedded, keep, send = call(
+    embedded, keep, send, early = call(
         functools.partial(front_kernel, blocks, devices),
-        [((local, emb), f32)] + [((half + blocks + extra, BLK), f32)] * 2,
+        [((local, emb), f32)] + [((half + blocks + extra, BLK), f32)] * 2 + [((local, hid), bf16)],
         pos,
-        hidden,
-        weight,
+        *(pltpu.with_memory_space_constraint(a, pltpu.HBM) for a in (hidden, weight)),
         scratch=[
             pay_scratch,
-            pltpu.VMEM((local, hid), bf16),
             pltpu.VMEM((hid, emb), bf16),
             pltpu.VMEM((local, emb), f32),
             pltpu.SemaphoreType.DMA((slabs + 2,)),
         ],
-        limit=58,
-        places=(HBM, VMEM, VMEM),
+        places=(HBM, VMEM, VMEM, VMEM),
     )
-    keep, send, early = lax.optimization_barrier((keep, send, hidden))
     me = (lax.axis_index("group") * lax.axis_size("dp") + lax.axis_index("dp")).astype(jnp.int32).reshape(1, 1)
     turned_keep, turned_send = call(
         turn_kernel,
@@ -631,41 +645,44 @@
         me,
         early,
         scratch=[pltpu.VMEM((hid, local), f32)],
-        limit=58,
+        flops=10**9,
     )
-    orders, _ = halving()
+    orders, shares = halving(emb)
     turned = call(
         functools.partial(order_kernel, orders),
-        [((hid // 2, 2 * local), bf16)] * len(orders),
+        [((hid // 4, 2 * local), bf16)] * len(orders) + [((hid // 4, 2 * local), f32)] * len(orders),
         me,
         turned_keep,
         swap(turned_send, 1, 1),
-        scratch=[pltpu.VMEM((hid // 2, 2 * local), f32)],
+        scratch=[pltpu.VMEM((hid // 4, 2 * local), f32)],
+        flops=10**9,
     )
     part, sums = reduce_scatter(keep, send, half, blocks)
-    parts = all_gather(part)
-    parts[-1], turned = lax.optimization_barrier((parts[-1], turned))
-    xh, xl, wh, wl, grad, keep, send = call(
+    parts, turned = all_gather(part, turned)
+    near = turned[: len(orders)]
+    far = [swap(t, order[0], 1) for t, order in zip(turned[len(orders) :], orders)]
+    wh, wl, x1, x2, x3, eliminated, grad, keep, send = call(
         functools.partial(factor_kernel, blocks, total_rows, devices, len(parts)),
-        [((emb, emb), bf16)] * 2
-        + [((local, emb), bf16)] * 2
-        + [((local, emb), f32)]
+        [((local, emb), bf16)] * 2
+        + [((PAIR, PAIR), bf16)] * 3
+        + [((emb // PAIR, emb + local, PAIR), f32), ((local, emb), f32)]
         + [((half + 2 * blocks + extra, BLK), f32)] * 2,
         pos,
         sums,
         embedded,
         partners,
         *parts,
-        scratch=[pltpu.VMEM((emb // PAIR, emb + local, PAIR), f32), pay_scratch]
-        + [pltpu.VMEM((emb + local, PAIR), bf16)] * 3
-        + [pltpu.VMEM((PAIR, PAIR), bf16)] * 3,
+        scratch=[pay_scratch] + [pltpu.VMEM((emb + local, PAIR), bf16)] * 3,
         limit=32,
+        flops=3 * 10**10,
     )
+    keep, send, far = lax.optimization_barrier((keep, send, far))
     part, sums = reduce_scatter(keep, send, half, 0)
-    parts = all_gather(part)
-    grad_z, wide = call(
-        functools.partial(back_kernel, blocks, total_rows, devices, len(parts)),
-        [((local, emb), bf16), ((local, emb), f32)],
+    inverse = call(inverse_kernel, [((emb, emb), bf16)] * 2, eliminated, x1, x2, x3, flops=3 * 10**9)
+    parts, (xh, xl) = all_gather(part, inverse)
+    grad_z, *wide = call(
+        functools.partial(back_kernel, blocks, total_rows, devices, len(parts), shares),
+        [((local, emb), bf16)] + [((local, share), f32) for share in shares],
         pos,
         sums,
         grad,
@@ -677,7 +694,7 @@
         scratch=[pay_scratch],
         limit=32,
     )
-    grad_weight, grad_hidden = weight_sums(turned, grad_z, wide, weight)
+    grad_weight, grad_hidden = weight_sums(near, far, wide, grad_z, weight)
     return (wh, grad_weight, grad_hidden)
 
 

time: 214 us -> 205 us (0.958)
  waiting for transfers between devices: 107 us -> 100 us
  Pallas kernels: 53.7 us -> 50.7 us
  starting transfers between devices: 46.5 us -> 49.2 us
  local copies, waits for them, and re-layouts: 2.52 us -> 0.06 us
    ppermute x46 -> x54, waiting for transfers between devices: 107 us -> 100 us  [swap(): return lax.ppermute(x, AXES, [(i, i ^ by * stride) for i in range(count)])]
    pallas_call x14 -> x15, Pallas kernels: 53.7 us -> 50.7 us  [call(): pl.pallas_call(kernel, out_shape=tuple((jax.ShapeDtypeStruct(s, t) for s,...]
    ppermute x46 -> x54, starting transfers between devices: 46.5 us -> 49.2 us  [swap(): return lax.ppermute(x, AXES, [(i, i ^ by * stride) for i in range(count)])]
    unnamed x18 -> x12, local copies, waits for them, and re-layouts: 2.51 us -> 0.05 us
  transfers between devices with their start and end apart: 46 -> 54, of which waited for: 31 -> 31; matrix products, arithmetic and copies ran while one was open for 1% -> 1% of each run, Pallas kernels for 2% -> 19%
where the time goes in v1:
time: 205 us; the launch traced here: 204 us
  waiting for transfers between devices  100 us (49%)
  Pallas kernels  50.7 us (25%)
  starting transfers between devices  49.2 us (24%)
  matrix products  2.26 us (1%)
    ppermute x54, waiting for transfers between devices, swap(): return lax.ppermute(x, AXES, [(i, i ^ by * stride) for i in range(count)])  100 us
    pallas_call x15, Pallas kernels, call(): pl.pallas_call(kernel, out_shape=tuple((jax.ShapeDtypeStruct(s, t) for s,...  50.7 us
    ppermute x54, starting transfers between devices, swap(): return lax.ppermute(x, AXES, [(i, i ^ by * stride) for i in range(count)])  49.2 us
  transfers between devices with their start and end apart: 54, of which 31 were waited for; matrix products, arithmetic and copies ran while one was open for 1% of the time, Pallas kernels for 19%

profile of v1, /device:TPU:0, one launch (start us, length us, event | category | flops | bytes accessed | tf_op | source)
XLA Modules:
  0.0 204.4 jit_solution(15954442943047830401)
XLA Ops:
  0.7 5.8 %shard_map.58 = (f32[256,1024]{1,0:T(8,128)S(1)}, f32[2064,128]{1,0:T(8,128)S(1)}, f32[2064,128]{1,0:T(8,128)S(1)}, bf16[256,2048]{1,0:T(8,128)(2,1)S(1)}) custom-call(s32[1,1]{1,0:T(1,128)} %bitcast.pos_ref.refs_0_, bf16[256,2048]{1,0:T(8,128)(2,1)} %hid_hbm.1, bf16[2048,1024]{1,0:T(8,128)(2,1)} %w_hbm.1), custom_call_target="tpu_custom_call" | custom-call | flops 1000000 | bytes 1000000 | tf_op jit(solution)/shard_map/pallas_call | solution.py:562
  9.5 2.9 %collective-permute-start.1 = (f32[536,128]{1,0:T(8,128)S(1)}, f32[536,128]{1,0:T(8,128)S(1)}, u32[]{:S(2)}, u32[]{:S(2)}) collective-permute-start(f32[536,128]{1,0:T(8,128)S(1)} %get-tuple-element.103), channel_id=1, source_target_pairs={{0,8},{1,9},{2,10},{3,11},{4,12},{5,13},{6,14},{7,15},{8,0},{9,1},... | collective-permute-start | bytes 823304 | tf_op jit(solution)/shard_map/ppermute | solution.py:109
  13.9 5.8 %collective-permute-done.1.refs_1_ = f32[536,128]{1,0:T(8,128)S(1)} collective-permute-done((f32[536,128]{1,0:T(8,128)S(1)}, f32[536,128]{1,0:T(8,128)S(1)}, u32[]{:S(2)}, u32[]{:S(2)}) %collective-permute-start.1) | collective-permute-done | bytes 274464 | tf_op jit(solution)/shard_map/ppermute | solution.py:109
  19.8 6.9 %collective-permute-done.2.refs_2_ = f32[536,128]{1,0:T(8,128)S(1)} collective-permute-done((f32[536,128]{1,0:T(8,128)S(1)}, f32[536,128]{1,0:T(8,128)S(1)}, u32[]{:S(2)}, u32[]{:S(2)}) %collective-permute-start.2) | collective-permute-done | bytes 274464 | tf_op jit(solution)/shard_map/ppermute | solution.py:109
  26.7 1.6 collective-permute-start.4
  28.3 2.6 %collective-permute-start.5 = (f32[200,128]{1,0:T(8,128)S(1)}, f32[200,128]{1,0:T(8,128)S(1)}, u32[]{:S(2)}, u32[]{:S(2)}) collective-permute-start(f32[200,128]{1,0:T(8,128)S(1)} %get-tuple-element.108), channel_id=1, source_target_pairs={{0,4},{1,5},{2,6},{3,7},{4,0},{5,1},{6,2},{7,3},{8,12},{9,13},{10,... | collective-permute-start | bytes 307208 | tf_op jit(solution)/shard_map/ppermute | solution.py:109
  32.4 5.9 %collective-permute-done.5.refs_2_ = f32[200,128]{1,0:T(8,128)S(1)} collective-permute-done((f32[200,128]{1,0:T(8,128)S(1)}, f32[200,128]{1,0:T(8,128)S(1)}, u32[]{:S(2)}, u32[]{:S(2)}) %collective-permute-start.5) | collective-permute-done | bytes 102432 | tf_op jit(solution)/shard_map/ppermute | solution.py:109
  38.4 2.5 %collective-permute-start.9 = (f32[128,128]{1,0:T(8,128)S(1)}, f32[128,128]{1,0:T(8,128)S(1)}, u32[]{:S(2)}, u32[]{:S(2)}) collective-permute-start(f32[128,128]{1,0:T(8,128)S(1)} %get-tuple-element.122), channel_id=1, source_target_pairs={{0,6},{1,7},{2,4},{3,5},{4,2},{5,3},{6,0},{7,1},{8,14},{9,15},{10,... | collective-permute-start | bytes 196616 | tf_op jit(solution)/shard_map/ppermute | solution.py:109
  44.6 2.1 %collective-permute-done.8 = f32[128,128]{1,0:T(8,128)S(1)} collective-permute-done((f32[128,128]{1,0:T(8,128)S(1)}, f32[128,128]{1,0:T(8,128)S(1)}, u32[]{:S(2)}, u32[]{:S(2)}) %collective-permute-start.8) | collective-permute-done | bytes 65568 | tf_op jit(solution)/shard_map/ppermute | solution.py:109
  50.4 4.8 %collective-permute-done.13.refs_7_ = f32[512,128]{1,0:T(8,128)S(1)} collective-permute-done((f32[512,128]{1,0:T(8,128)S(1)}, f32[512,128]{1,0:T(8,128)S(1)}, u32[]{:S(2)}, u32[]{:S(2)}) %collective-permute-start.13) | collective-permute-done | bytes 262176 | tf_op jit(solution)/shard_map/ppermute | solution.py:109
  55.2 2.7 %collective-permute-done.12.refs_6_ = f32[512,128]{1,0:T(8,128)S(1)} collective-permute-done((f32[512,128]{1,0:T(8,128)S(1)}, f32[512,128]{1,0:T(8,128)S(1)}, u32[]{:S(2)}, u32[]{:S(2)}) %collective-permute-start.12) | collective-permute-done | bytes 262176 | tf_op jit(solution)/shard_map/ppermute | solution.py:109
  61.4 35.2 %shard_map.64 = (bf16[256,1024]{1,0:T(8,128)(2,1)}, bf16[256,1024]{1,0:T(8,128)(2,1)S(1)}, bf16[256,256]{1,0:T(8,128)(2,1)S(1)}, bf16[256,256]{1,0:T(8,128)(2,1)...) custom-call(s32[1,1]{1,0:T(1,128)} %bitcast.pos_ref.refs_0_, ...), custom_call_target="tpu_custom_call" | custom-call | flops 30000001024 | bytes 1000000 | tf_op jit(solution)/shard_map/pallas_call | solution.py:562
  96.7 2.7 %collective-permute-done.21.refs_1_ = f32[2072,128]{1,0:T(8,128)S(1)} collective-permute-done((f32[2072,128]{1,0:T(8,128)S(1)}, f32[2072,128]{1,0:T(8,128)S(1)}, u32[]{:S(2)}, u32[]{:S(2)}) %collective-permute-start.21) | collective-permute-done | bytes 1060896 | tf_op jit(solution)/shard_map/ppermute | solution.py:109
  103.1 5.9 %collective-permute-done.22.refs_1_ = f32[536,128]{1,0:T(8,128)S(1)} collective-permute-done((f32[536,128]{1,0:T(8,128)S(1)}, f32[536,128]{1,0:T(8,128)S(1)}, u32[]{:S(2)}, u32[]{:S(2)}) %collective-permute-start.22) | collective-permute-done | bytes 274464 | tf_op jit(solution)/shard_map/ppermute | solution.py:109
  109.0 6.2 %collective-permute-done.23.refs_2_ = f32[536,128]{1,0:T(8,128)S(1)} collective-permute-done((f32[536,128]{1,0:T(8,128)S(1)}, f32[536,128]{1,0:T(8,128)S(1)}, u32[]{:S(2)}, u32[]{:S(2)}) %collective-permute-start.23) | collective-permute-done | bytes 274464 | tf_op jit(solution)/shard_map/ppermute | solution.py:109
  117.6 2.1 %collective-permute-start.27 = (f32[152,128]{1,0:T(8,128)S(1)}, f32[152,128]{1,0:T(8,128)S(1)}, u32[]{:S(2)}, u32[]{:S(2)}) collective-permute-start(f32[152,128]{1,0:T(8,128)S(1)} %get-tuple-element.143), channel_id=1, source_target_pairs={{0,6},{1,7},{2,4},{3,5},{4,2},{5,3},{6,0},{7,1},{8,14},{9,15},{10,... | collective-permute-start | bytes 233480 | tf_op jit(solution)/shard_map/ppermute | solution.py:109
  119.8 4.7 %collective-permute-done.26.refs_2_ = f32[152,128]{1,0:T(8,128)S(1)} collective-permute-done((f32[152,128]{1,0:T(8,128)S(1)}, f32[152,128]{1,0:T(8,128)S(1)}, u32[]{:S(2)}, u32[]{:S(2)}) %collective-permute-start.26) | collective-permute-done | bytes 77856 | tf_op jit(solution)/shard_map/ppermute | solution.py:109
  124.6 1.9 collective-permute-start.30
  130.7 1.7 collective-permute-done.29
  136.1 5.1 %collective-permute-done.33.refs_10_ = f32[512,128]{1,0:T(8,128)S(1)} collective-permute-done((f32[512,128]{1,0:T(8,128)S(1)}, f32[512,128]{1,0:T(8,128)S(1)}, u32[]{:S(2)}, u32[]{:S(2)}) %collective-permute-start.33) | collective-permute-done | bytes 262176 | tf_op jit(solution)/shard_map/ppermute | solution.py:109
  141.2 2.4 %collective-permute-done.32.refs_9_ = f32[512,128]{1,0:T(8,128)S(1)} collective-permute-done((f32[512,128]{1,0:T(8,128)S(1)}, f32[512,128]{1,0:T(8,128)S(1)}, u32[]{:S(2)}, u32[]{:S(2)}) %collective-permute-start.32) | collective-permute-done | bytes 262176 | tf_op jit(solution)/shard_map/ppermute | solution.py:109
  145.5 4.9 %shard_map.69 = (bf16[256,1024]{1,0:T(8,128)(2,1)S(1)}, f32[256,384]{1,0:T(8,128)S(1)}, f32[256,384]{1,0:T(8,128)S(1)}, f32[256,256]{1,0:T(8,128)S(1)}) custom-call(s32[1,1]{1,0:T(1,128)} %bitcast.pos_ref.refs_0_, f32[24,128]{1,0:T(8,128)S(1)} %get-tuple-element.144.refs_1_, f32[256,1024]{1,0:T(8,128)S(1)} %get-tuple-element.145.refs_2_, ...), custom_call_target="tpu_custom_call" | custom-call | flops 1000000 | bytes 1000000 | tf_op jit(solution)/shard_map/pallas_call | solution.py:562
  153.0 2.3 %convolution_convert_fusion = bf16[256,2048]{1,0:T(8,128)(2,1)} fusion(bf16[256,1024]{1,0:T(8,128)(2,1)S(1)} %get-tuple-element.163, bf16[2048,1024]{1,0:T(8,128)(2,1)S(1)} %copy-done.2), kind=kOutput, calls=%fused_computation | convolution fusion | flops 1074266112 | bytes 5767168 | tf_op jit(solution)/shard_map/dot_general | solution.py:57
  155.3 3.9 %collective-permute-done.43.refs_2_ = f32[256,256]{1,0:T(8,128)S(1)} collective-permute-done((f32[256,256]{1,0:T(8,128)S(1)}, f32[256,256]{1,0:T(8,128)S(1)}, u32[]{:S(2)}, u32[]{:S(2)}) %collective-permute-start.43) | collective-permute-done | bytes 262176 | tf_op jit(solution)/shard_map/ppermute | solution.py:109
  159.2 1.5 collective-permute-done.44.refs_3_
  168.5 2.2 %collective-permute-start.50 = (f32[256,256]{1,0:T(8,128)S(1)}, f32[256,256]{1,0:T(8,128)S(1)}, u32[]{:S(2)}, u32[]{:S(2)}) collective-permute-start(f32[256,256]{1,0:T(8,128)S(1)} %get-tuple-element.172), channel_id=1, source_target_pairs={{0,4},{1,5},{2,6},{3,7},{4,0},{5,1},{6,2},{7,3},{8,12},{9,13},{10,... | collective-permute-start | bytes 786440 | tf_op jit(solution)/shard_map/ppermute | solution.py:109
  170.7 6.5 %collective-permute-done.46 = f32[256,384]{1,0:T(8,128)S(1)} collective-permute-done((f32[256,384]{1,0:T(8,128)S(1)}, f32[256,384]{1,0:T(8,128)S(1)}, u32[]{:S(2)}, u32[]{:S(2)}) %collective-permute-start.46) | collective-permute-done | bytes 393248 | tf_op jit(solution)/shard_map/ppermute | solution.py:109
  178.8 1.6 collective-permute-start.49
  180.4 2.5 %collective-permute-done.50 = f32[256,256]{1,0:T(8,128)S(1)} collective-permute-done((f32[256,256]{1,0:T(8,128)S(1)}, f32[256,256]{1,0:T(8,128)S(1)}, u32[]{:S(2)}, u32[]{:S(2)}) %collective-permute-start.50) | collective-permute-done | bytes 262176 | tf_op jit(solution)/shard_map/ppermute | solution.py:109
  184.2 7.1 %collective-permute-done.49 = f32[128,768]{1,0:T(8,128)S(1)} collective-permute-done((f32[128,768]{1,0:T(8,128)S(1)}, f32[128,768]{1,0:T(8,128)S(1)}, u32[]{:S(2)}, u32[]{:S(2)}) %collective-permute-start.49) | collective-permute-done | bytes 393248 | tf_op jit(solution)/shard_map/ppermute | solution.py:109
  192.8 2.8 %collective-permute-done.53 = f32[64,256]{1,0:T(8,128)S(1)} collective-permute-done((f32[64,256]{1,0:T(8,128)S(1)}, f32[64,256]{1,0:T(8,128)S(1)}, u32[]{:S(2)}, u32[]{:S(2)}) %collective-permute-start.53) | collective-permute-done | bytes 65568 | tf_op jit(solution)/shard_map/ppermute | solution.py:109
  195.7 8.0 %collective-permute-done.51 = f32[64,768]{1,0:T(8,128)S(1)} collective-permute-done((f32[64,768]{1,0:T(8,128)S(1)}, f32[64,768]{1,0:T(8,128)S(1)}, u32[]{:S(2)}, u32[]{:S(2)}) %collective-permute-start.51) | collective-permute-done | bytes 196640 | tf_op jit(solution)/shard_map/ppermute | solution.py:109
  (114 shorter events, 48.6 us)
Async XLA Ops:
  7.8 35.0 %collective-permute-start.10 = (f32[1024,256]{1,0:T(8,128)S(1)}, f32[1024,256]{1,0:T(8,128)S(1)}, u32[]{:S(2)}, u32[]{:S(2)}) collective-permute-start(f32[1024,256]{1,0:T(8,128)S(1)} %get-tuple-element.115), channel_id=1, source_target_pairs={{0,1},{1,0},{2,3},{3,2},{4,5},{5,4},{6,7},{7,6},{8,9},{9,8},{10,11... | collective-permute-start | bytes 3145736 | tf_op jit(solution)/shard_map/ppermute | solution.py:109
  9.5 10.3 %collective-permute-start.1 = (f32[536,128]{1,0:T(8,128)S(1)}, f32[536,128]{1,0:T(8,128)S(1)}, u32[]{:S(2)}, u32[]{:S(2)}) collective-permute-start(f32[536,128]{1,0:T(8,128)S(1)} %get-tuple-element.103), channel_id=1, source_target_pairs={{0,8},{1,9},{2,10},{3,11},{4,12},{5,13},{6,14},{7,15},{8,0},{9,1},... | collective-permute-start | bytes 823304 | tf_op jit(solution)/shard_map/ppermute | solution.py:109
  12.4 14.2 %collective-permute-start.2 = (f32[536,128]{1,0:T(8,128)S(1)}, f32[536,128]{1,0:T(8,128)S(1)}, u32[]{:S(2)}, u32[]{:S(2)}) collective-permute-start(f32[536,128]{1,0:T(8,128)S(1)} %get-tuple-element.104), channel_id=1, source_target_pairs={{0,16},{1,17},{2,18},{3,19},{4,20},{5,21},{6,22},{7,23},{8,24},{9,... | collective-permute-start | bytes 823304 | tf_op jit(solution)/shard_map/ppermute | solution.py:109
  13.9 12.7 %collective-permute-start.3 = (f32[536,128]{1,0:T(8,128)S(1)}, f32[536,128]{1,0:T(8,128)S(1)}, u32[]{:S(2)}, u32[]{:S(2)}) collective-permute-start(f32[536,128]{1,0:T(8,128)S(1)} %get-tuple-element.105), channel_id=1, source_target_pairs={{0,24},{1,25},{2,26},{3,27},{4,28},{5,29},{6,30},{7,31},{8,16},{9,... | collective-permute-start | bytes 823304 | tf_op jit(solution)/shard_map/ppermute | solution.py:109
  28.3 10.0 %collective-permute-start.5 = (f32[200,128]{1,0:T(8,128)S(1)}, f32[200,128]{1,0:T(8,128)S(1)}, u32[]{:S(2)}, u32[]{:S(2)}) collective-permute-start(f32[200,128]{1,0:T(8,128)S(1)} %get-tuple-element.108), channel_id=1, source_target_pairs={{0,4},{1,5},{2,6},{3,7},{4,0},{5,1},{6,2},{7,3},{8,12},{9,13},{10,... | collective-permute-start | bytes 307208 | tf_op jit(solution)/shard_map/ppermute | solution.py:109
  30.9 7.4 %collective-permute-start.6 = (f32[200,128]{1,0:T(8,128)S(1)}, f32[200,128]{1,0:T(8,128)S(1)}, u32[]{:S(2)}, u32[]{:S(2)}) collective-permute-start(f32[200,128]{1,0:T(8,128)S(1)} %get-tuple-element.109), channel_id=1, source_target_pairs={{0,6},{1,7},{2,4},{3,5},{4,2},{5,3},{6,0},{7,1},{8,14},{9,15},{10,... | collective-permute-start | bytes 307208 | tf_op jit(solution)/shard_map/ppermute | solution.py:109
  38.4 6.3 %collective-permute-start.9 = (f32[128,128]{1,0:T(8,128)S(1)}, f32[128,128]{1,0:T(8,128)S(1)}, u32[]{:S(2)}, u32[]{:S(2)}) collective-permute-start(f32[128,128]{1,0:T(8,128)S(1)} %get-tuple-element.122), channel_id=1, source_target_pairs={{0,6},{1,7},{2,4},{3,5},{4,2},{5,3},{6,0},{7,1},{8,14},{9,15},{10,... | collective-permute-start | bytes 196616 | tf_op jit(solution)/shard_map/ppermute | solution.py:109
  46.8 8.3 %collective-permute-start.13 = (f32[512,128]{1,0:T(8,128)S(1)}, f32[512,128]{1,0:T(8,128)S(1)}, u32[]{:S(2)}, u32[]{:S(2)}) collective-permute-start(f32[512,128]{1,0:T(8,128)S(1)} %constant_dynamic-update-slice_fusion.refs_4_), channel_id=1, source_target_pairs={{0,24},{1,25},{2,26},{3,27},{4,28},{5,29},{6,30},{7,31},{8,16},{9,... | collective-permute-start | bytes 786440 | tf_op jit(solution)/shard_map/ppermute | solution.py:109
  48.3 9.5 %collective-permute-start.12 = (f32[512,128]{1,0:T(8,128)S(1)}, f32[512,128]{1,0:T(8,128)S(1)}, u32[]{:S(2)}, u32[]{:S(2)}) collective-permute-start(f32[512,128]{1,0:T(8,128)S(1)} %constant_dynamic-update-slice_fusion.refs_4_), channel_id=1, source_target_pairs={{0,16},{1,17},{2,18},{3,19},{4,20},{5,21},{6,22},{7,23},{8,24},{9,... | collective-permute-start | bytes 786440 | tf_op jit(solution)/shard_map/ppermute | solution.py:109
  49.8 8.1 %collective-permute-start.11 = (f32[512,128]{1,0:T(8,128)S(1)}, f32[512,128]{1,0:T(8,128)S(1)}, u32[]{:S(2)}, u32[]{:S(2)}) collective-permute-start(f32[512,128]{1,0:T(8,128)S(1)} %constant_dynamic-update-slice_fusion.refs_4_), channel_id=1, source_target_pairs={{0,8},{1,9},{2,10},{3,11},{4,12},{5,13},{6,14},{7,15},{8,0},{9,1},... | collective-permute-start | bytes 786440 | tf_op jit(solution)/shard_map/ppermute | solution.py:109
  50.4 9.4 %collective-permute-start.14 = (f32[512,128]{1,0:T(8,128)S(1)}, f32[512,128]{1,0:T(8,128)S(1)}, u32[]{:S(2)}, u32[]{:S(2)}) collective-permute-start(f32[512,128]{1,0:T(8,128)S(1)} %constant_dynamic-update-slice_fusion.refs_4_), channel_id=1, source_target_pairs={{0,1},{1,0},{2,3},{3,2},{4,5},{5,4},{6,7},{7,6},{8,9},{9,8},{10,11... | collective-permute-start | bytes 786440 | tf_op jit(solution)/shard_map/ppermute | solution.py:109
  58.4 38.3 %collective-permute-start.18 = (f32[512,512]{1,0:T(8,128)S(1)}, f32[512,512]{1,0:T(8,128)S(1)}, u32[]{:S(2)}, u32[]{:S(2)}) collective-permute-start(f32[512,512]{1,0:T(8,128)S(1)} %get-tuple-element.130), channel_id=1, source_target_pairs={{0,8},{1,9},{2,10},{3,11},{4,12},{5,13},{6,14},{7,15},{8,0},{9,1},... | collective-permute-start | bytes 3145736 | tf_op jit(solution)/shard_map/ppermute | solution.py:109
  59.8 36.8 %collective-permute-start.19 = (f32[512,512]{1,0:T(8,128)S(1)}, f32[512,512]{1,0:T(8,128)S(1)}, u32[]{:S(2)}, u32[]{:S(2)}) collective-permute-start(f32[512,512]{1,0:T(8,128)S(1)} %get-tuple-element.131), channel_id=1, source_target_pairs={{0,16},{1,17},{2,18},{3,19},{4,20},{5,21},{6,22},{7,23},{8,24},{9,... | collective-permute-start | bytes 3145736 | tf_op jit(solution)/shard_map/ppermute | solution.py:109
  60.4 36.2 %collective-permute-start.20 = (f32[512,512]{1,0:T(8,128)S(1)}, f32[512,512]{1,0:T(8,128)S(1)}, u32[]{:S(2)}, u32[]{:S(2)}) collective-permute-start(f32[512,512]{1,0:T(8,128)S(1)} %get-tuple-element.132), channel_id=1, source_target_pairs={{0,2},{1,3},{2,0},{3,1},{4,6},{5,7},{6,4},{7,5},{8,10},{9,11},{10,... | collective-permute-start | bytes 3145736 | tf_op jit(solution)/shard_map/ppermute | solution.py:109
  99.5 9.5 %collective-permute-start.22 = (f32[536,128]{1,0:T(8,128)S(1)}, f32[536,128]{1,0:T(8,128)S(1)}, u32[]{:S(2)}, u32[]{:S(2)}) collective-permute-start(f32[536,128]{1,0:T(8,128)S(1)} %get-tuple-element.137), channel_id=1, source_target_pairs={{0,8},{1,9},{2,10},{3,11},{4,12},{5,13},{6,14},{7,15},{8,0},{9,1},... | collective-permute-start | bytes 823304 | tf_op jit(solution)/shard_map/ppermute | solution.py:109
  101.0 14.2 %collective-permute-start.23 = (f32[536,128]{1,0:T(8,128)S(1)}, f32[536,128]{1,0:T(8,128)S(1)}, u32[]{:S(2)}, u32[]{:S(2)}) collective-permute-start(f32[536,128]{1,0:T(8,128)S(1)} %get-tuple-element.138), channel_id=1, source_target_pairs={{0,16},{1,17},{2,18},{3,19},{4,20},{5,21},{6,22},{7,23},{8,24},{9,... | collective-permute-start | bytes 823304 | tf_op jit(solution)/shard_map/ppermute | solution.py:109
  101.6 13.5 %collective-permute-start.24 = (f32[536,128]{1,0:T(8,128)S(1)}, f32[536,128]{1,0:T(8,128)S(1)}, u32[]{:S(2)}, u32[]{:S(2)}) collective-permute-start(f32[536,128]{1,0:T(8,128)S(1)} %get-tuple-element.139), channel_id=1, source_target_pairs={{0,24},{1,25},{2,26},{3,27},{4,28},{5,29},{6,30},{7,31},{8,16},{9,... | collective-permute-start | bytes 823304 | tf_op jit(solution)/shard_map/ppermute | solution.py:109
  116.4 8.2 %collective-permute-start.26 = (f32[152,128]{1,0:T(8,128)S(1)}, f32[152,128]{1,0:T(8,128)S(1)}, u32[]{:S(2)}, u32[]{:S(2)}) collective-permute-start(f32[152,128]{1,0:T(8,128)S(1)} %get-tuple-element.142), channel_id=1, source_target_pairs={{0,4},{1,5},{2,6},{3,7},{4,0},{5,1},{6,2},{7,3},{8,12},{9,13},{10,... | collective-permute-start | bytes 233480 | tf_op jit(solution)/shard_map/ppermute | solution.py:109
  117.6 6.9 %collective-permute-start.27 = (f32[152,128]{1,0:T(8,128)S(1)}, f32[152,128]{1,0:T(8,128)S(1)}, u32[]{:S(2)}, u32[]{:S(2)}) collective-permute-start(f32[152,128]{1,0:T(8,128)S(1)} %get-tuple-element.143), channel_id=1, source_target_pairs={{0,6},{1,7},{2,4},{3,5},{4,2},{5,3},{6,0},{7,1},{8,14},{9,15},{10,... | collective-permute-start | bytes 233480 | tf_op jit(solution)/shard_map/ppermute | solution.py:109
  132.5 8.7 %collective-permute-start.33 = (f32[512,128]{1,0:T(8,128)S(1)}, f32[512,128]{1,0:T(8,128)S(1)}, u32[]{:S(2)}, u32[]{:S(2)}) collective-permute-start(f32[512,128]{1,0:T(8,128)S(1)} %constant_dynamic-update-slice_fusion.4.refs_7_), channel_id=1, source_target_pairs={{0,24},{1,25},{2,26},{3,27},{4,28},{5,29},{6,30},{7,31},{8,16},{9,... | collective-permute-start | bytes 786440 | tf_op jit(solution)/shard_map/ppermute | solution.py:109
  134.0 9.6 %collective-permute-start.32 = (f32[512,128]{1,0:T(8,128)S(1)}, f32[512,128]{1,0:T(8,128)S(1)}, u32[]{:S(2)}, u32[]{:S(2)}) collective-permute-start(f32[512,128]{1,0:T(8,128)S(1)} %constant_dynamic-update-slice_fusion.4.refs_7_), channel_id=1, source_target_pairs={{0,16},{1,17},{2,18},{3,19},{4,20},{5,21},{6,22},{7,23},{8,24},{9,... | collective-permute-start | bytes 786440 | tf_op jit(solution)/shard_map/ppermute | solution.py:109
  134.6 9.0 %collective-permute-start.31 = (f32[512,128]{1,0:T(8,128)S(1)}, f32[512,128]{1,0:T(8,128)S(1)}, u32[]{:S(2)}, u32[]{:S(2)}) collective-permute-start(f32[512,128]{1,0:T(8,128)S(1)} %constant_dynamic-update-slice_fusion.4.refs_7_), channel_id=1, source_target_pairs={{0,8},{1,9},{2,10},{3,11},{4,12},{5,13},{6,14},{7,15},{8,0},{9,1},... | collective-permute-start | bytes 786440 | tf_op jit(solution)/shard_map/ppermute | solution.py:109
  136.1 8.1 %collective-permute-start.34 = (f32[512,128]{1,0:T(8,128)S(1)}, f32[512,128]{1,0:T(8,128)S(1)}, u32[]{:S(2)}, u32[]{:S(2)}) collective-permute-start(f32[512,128]{1,0:T(8,128)S(1)} %constant_dynamic-update-slice_fusion.4.refs_7_), channel_id=1, source_target_pairs={{0,1},{1,0},{2,3},{3,2},{4,5},{5,4},{6,7},{7,6},{8,9},{9,8},{10,11... | collective-permute-start | bytes 786440 | tf_op jit(solution)/shard_map/ppermute | solution.py:109
  150.6 8.6 %collective-permute-start.43 = (f32[256,256]{1,0:T(8,128)S(1)}, f32[256,256]{1,0:T(8,128)S(1)}, u32[]{:S(2)}, u32[]{:S(2)}) collective-permute-start(f32[256,256]{1,0:T(8,128)S(1)} %get-tuple-element.162.refs_0_), channel_id=1, source_target_pairs={{0,2},{1,3},{2,0},{3,1},{4,6},{5,7},{6,4},{7,5},{8,10},{9,11},{10,... | collective-permute-start | bytes 786440 | tf_op jit(solution)/shard_map/ppermute | solution.py:109
  151.1 11.5 %collective-permute-start.38 = (f32[256,384]{1,0:T(8,128)S(1)}, f32[256,384]{1,0:T(8,128)S(1)}, u32[]{:S(2)}, u32[]{:S(2)}) collective-permute-start(f32[256,384]{1,0:T(8,128)S(1)} %get-tuple-element.160.refs_0_), channel_id=1, source_target_pairs={{0,8},{1,9},{2,10},{3,11},{4,12},{5,13},{6,14},{7,15},{8,0},{9,1},... | collective-permute-start | bytes 1179656 | tf_op jit(solution)/shard_map/ppermute | solution.py:109
  152.2 11.4 %collective-permute-start.39 = (f32[256,384]{1,0:T(8,128)S(1)}, f32[256,384]{1,0:T(8,128)S(1)}, u32[]{:S(2)}, u32[]{:S(2)}) collective-permute-start(f32[256,384]{1,0:T(8,128)S(1)} %get-tuple-element.161.refs_0_), channel_id=1, source_target_pairs={{0,16},{1,17},{2,18},{3,19},{4,20},{5,21},{6,22},{7,23},{8,24},{9,... | collective-permute-start | bytes 1179656 | tf_op jit(solution)/shard_map/ppermute | solution.py:109
  166.0 11.2 %collective-permute-start.46 = (f32[256,384]{1,0:T(8,128)S(1)}, f32[256,384]{1,0:T(8,128)S(1)}, u32[]{:S(2)}, u32[]{:S(2)}) collective-permute-start(f32[256,384]{1,0:T(8,128)S(1)} %get-tuple-element.176), channel_id=1, source_target_pairs={{0,16},{1,17},{2,18},{3,19},{4,20},{5,21},{6,22},{7,23},{8,24},{9,... | collective-permute-start | bytes 1179656 | tf_op jit(solution)/shard_map/ppermute | solution.py:109
  167.6 10.9 %collective-permute-start.48 = (f32[256,384]{1,0:T(8,128)S(1)}, f32[256,384]{1,0:T(8,128)S(1)}, u32[]{:S(2)}, u32[]{:S(2)}) collective-permute-start(f32[256,384]{1,0:T(8,128)S(1)} %get-tuple-element.182), channel_id=1, source_target_pairs={{0,8},{1,9},{2,10},{3,11},{4,12},{5,13},{6,14},{7,15},{8,0},{9,1},... | collective-permute-start | bytes 1179656 | tf_op jit(solution)/shard_map/ppermute | solution.py:109
  168.5 14.4 %collective-permute-start.50 = (f32[256,256]{1,0:T(8,128)S(1)}, f32[256,256]{1,0:T(8,128)S(1)}, u32[]{:S(2)}, u32[]{:S(2)}) collective-permute-start(f32[256,256]{1,0:T(8,128)S(1)} %get-tuple-element.172), channel_id=1, source_target_pairs={{0,4},{1,5},{2,6},{3,7},{4,0},{5,1},{6,2},{7,3},{8,12},{9,13},{10,... | collective-permute-start | bytes 786440 | tf_op jit(solution)/shard_map/ppermute | solution.py:109
  178.8 12.5 %collective-permute-start.49 = (f32[128,768]{1,0:T(8,128)S(1)}, f32[128,768]{1,0:T(8,128)S(1)}, u32[]{:S(2)}, u32[]{:S(2)}) collective-permute-start(f32[128,768]{1,0:T(8,128)S(1)} %get-tuple-element.198), channel_id=1, source_target_pairs={{0,2},{1,3},{2,0},{3,1},{4,6},{5,7},{6,4},{7,5},{8,10},{9,11},{10,... | collective-permute-start | bytes 1179656 | tf_op jit(solution)/shard_map/ppermute | solution.py:109
  183.0 8.3 %collective-permute-start.52 = (f32[128,256]{1,0:T(8,128)S(1)}, f32[128,256]{1,0:T(8,128)S(1)}, u32[]{:S(2)}, u32[]{:S(2)}) collective-permute-start(f32[128,256]{1,0:T(8,128)S(1)} %get-tuple-element.199), channel_id=1, source_target_pairs={{0,8},{1,9},{2,10},{3,11},{4,12},{5,13},{6,14},{7,15},{8,0},{9,1},... | collective-permute-start | bytes 393224 | tf_op jit(solution)/shard_map/ppermute | solution.py:109
  192.8 10.9 %collective-permute-start.51 = (f32[64,768]{1,0:T(8,128)S(1)}, f32[64,768]{1,0:T(8,128)S(1)}, u32[]{:S(2)}, u32[]{:S(2)}) collective-permute-start(f32[64,768]{1,0:T(8,128)S(1)} %slice_add_fusion.2), channel_id=1, source_target_pairs={{0,4},{1,5},{2,6},{3,7},{4,0},{5,1},{6,2},{7,3},{8,12},{9,13},{10,... | collective-permute-start | bytes 589832 | tf_op jit(solution)/shard_map/ppermute | solution.py:109
  (25 other events, 125.5 us)

commit v2 on v1

--- a/solution.py
+++ b/solution.py
@@ -105,8 +105,12 @@
 
 
 def swap(x, stride, by):
+    return exchange(x, (by * stride, by * stride))
+
+
+def exchange(x, bits):
     count = lax.axis_size("group") * lax.axis_size("dp")
-    return lax.ppermute(x, AXES, [(i, i ^ (by * stride)) for i in range(count)])
+    return lax.ppermute(x, AXES, [(i, i ^ bits[i % 2]) for i in range(count)])
 
 
 def combine_kernel(size, listed, parts, radix, *refs):
@@ -273,17 +277,18 @@
 
 def order_kernel(orders, me_ref, keep_ref, got_ref, *refs):
     near_refs, far_refs, part_ref = refs[: len(orders)], refs[len(orders) : -1], refs[-1]
-    chip = me_ref[0, 0] // 2
+    chip, core = me_ref[0, 0] // 2, me_ref[0, 0] % 2
     half = part_ref.shape[0]
     own = half * 2 >> len(orders[0])
     local = keep_ref.shape[1]
     for bits, near_ref, far_ref in zip(orders, near_refs, far_refs):
         for side, out in ((0, part_ref), (1, far_ref)):
             for i in range(half // own):
-                far = bits[0] * side
+                far = [bits[0][0] * side] * 2
                 for t, bit in enumerate(reversed(bits[1:])):
-                    far |= bit * ((i >> t) & 1)
-                rows = pl.ds(pl.multiple_of((chip ^ (far // 2)) * own, 8), own)
+                    far = [f | b * ((i >> t) & 1) for f, b in zip(far, bit)]
+                differ = far[0] // 2 if far[0] == far[1] else jnp.where(core == 0, far[0] // 2, far[1] // 2)
+                rows = pl.ds(pl.multiple_of((chip ^ differ) * own, 8), own)
                 out[i * own : (i + 1) * own, :local] = keep_ref[rows, :]
                 out[i * own : (i + 1) * own, local:] = got_ref[rows, :]
         near_ref[...] = part_ref[...].astype(bf16)
@@ -572,14 +577,16 @@
 
 def halving(emb):
     per, groups = lax.axis_size("dp"), lax.axis_size("group")
-    group = [per << i for i in range(groups.bit_length() - 1)]
+    group = [(per << i,) * 2 for i in range(groups.bit_length() - 1)]
     rest = [2 << i for i in range(per.bit_length() - 2)]
-    return (group + rest, group[::-1] + rest, rest + group), (3 * emb // 8, 3 * emb // 8, emb // 4)
+    crossed = list(zip(rest, rest[1::-1] + rest[2:]))
+    rest = [(bit, bit) for bit in rest]
+    return (group + crossed, group[::-1] + crossed, rest + group), (3 * emb // 8, 3 * emb // 8, emb // 4)
 
 
 def weight_sums(near, far, wide, mine, weight):
     orders, shares = halving(weight.shape[1])
-    there = [swap(w, order[0], 1) for w, order in zip(wide, orders)]
+    there = [exchange(w, order[0]) for w, order in zip(wide, orders)]
     beside = [swap(w, 1, 1) for w in wide]
     product = mm(mine, weight, NT).astype(bf16)
     beside, product = lax.optimization_barrier((beside, product))
@@ -593,21 +600,24 @@
         for p, t, o, c in zip(group, ins, others, across):
             shape = ((near[p].shape[0] // 2, shares[p]), f32)
             kept[p], last = call(part_kernel, [shape, shape], near[p], far[p], wide[p], o, t, c)
-            sent[p] = swap(last, orders[p][1], 1)
+            sent[p] = exchange(last, orders[p][1])
     orders = list(orders)
     for step in range(2, len(orders[0])):
-        if len(orders) == 3 and orders[0][step:] == orders[1][step:]:
-            both = lax.optimization_barrier((kept[0], sent[0], kept[1], sent[1], last))
-            last = both[4]
-            kept = [jnp.concatenate([both[0], both[2]], 1), kept[2]]
-            sent = [jnp.concatenate([both[1], both[3]], 1), sent[2]]
-            orders = orders[1:]
-        for p, order in enumerate(orders):
+        for p in reversed(range(len(orders))):
+            if p == 1 and len(orders) == 3 and orders[0][step:] == orders[1][step:]:
+                both = lax.optimization_barrier((kept[0], sent[0], kept[1], sent[1], last))
+                last = both[4]
+                kept = [jnp.concatenate([both[0], both[2]], 1), kept[2]]
+                sent = [jnp.concatenate([both[1], both[3]], 1), sent[2]]
+                orders = orders[1:]
+                p = 0
             k, r, last = lax.optimization_barrier((kept[p], sent[p], last))
             size = k.shape[0] // 2
             last = k[size:] + r[size:]
             kept[p] = k[:size] + r[:size]
-            sent[p] = swap(last, order[step], 1)
+            sent[p] = exchange(last, orders[p][step])
+            if p == 0:
+                break
     return jnp.concatenate([k + r for k, r in zip(kept, sent)], 1), product
 
 
@@ -660,7 +670,7 @@
     part, sums = reduce_scatter(keep, send, half, blocks)
     parts, turned = all_gather(part, turned)
     near = turned[: len(orders)]
-    far = [swap(t, order[0], 1) for t, order in zip(turned[len(orders) :], orders)]
+    far = [exchange(t, order[0]) for t, order in zip(turned[len(orders) :], orders)]
     wh, wl, x1, x2, x3, eliminated, grad, keep, send = call(
         functools.partial(factor_kernel, blocks, total_rows, devices, len(parts)),
         [((local, emb), bf16)] * 2

time: 205 us -> 200 us (0.976)
  waiting for transfers between devices: 100 us -> 95.7 us
    ppermute x54, waiting for transfers between devices: 100 us -> 95.7 us  [exchange(): return lax.ppermute(x, AXES, [(i, i ^ bits[i % 2]) for i in range(count)])]
  transfers between devices with their start and end apart: 54 -> 54, of which waited for: 31 -> 28; matrix products, arithmetic and copies ran while one was open for 1% -> 1% of each run, Pallas kernels for 19% -> 20%
where the time goes in v2:
time: 200 us
  waiting for transfers between devices  95.7 us (48%)
  Pallas kernels  50.7 us (25%)
  starting transfers between devices  49.2 us (25%)
  matrix products  2.26 us (1%)
    ppermute x54, waiting for transfers between devices, exchange(): return lax.ppermute(x, AXES, [(i, i ^ bits[i % 2]) for i in range(count)])  95.7 us
    pallas_call x15, Pallas kernels, call(): pl.pallas_call(kernel, out_shape=tuple((jax.ShapeDtypeStruct(s, t) for s,...  50.7 us
    ppermute x54, starting transfers between devices, exchange(): return lax.ppermute(x, AXES, [(i, i ^ bits[i % 2]) for i in range(count)])  49.2 us
  transfers between devices with their start and end apart: 54, of which 28 were waited for; matrix products, arithmetic and copies ran while one was open for 1% of the time, Pallas kernels for 20%

profile of v2, /device:TPU:0, one launch (start us, length us, event | category | flops | bytes accessed | tf_op | source)
XLA Modules:
  0.0 199.9 jit_solution(4483059028506354679)
XLA Ops:
  0.7 5.8 %shard_map.58 = (f32[256,1024]{1,0:T(8,128)S(1)}, f32[2064,128]{1,0:T(8,128)S(1)}, f32[2064,128]{1,0:T(8,128)S(1)}, bf16[256,2048]{1,0:T(8,128)(2,1)S(1)}) custom-call(s32[1,1]{1,0:T(1,128)} %bitcast.pos_ref.refs_0_, bf16[256,2048]{1,0:T(8,128)(2,1)} %hid_hbm.1, bf16[2048,1024]{1,0:T(8,128)(2,1)} %w_hbm.1), custom_call_target="tpu_custom_call" | custom-call | flops 1000000 | bytes 1000000 | tf_op jit(solution)/shard_map/pallas_call | solution.py:567
  9.5 2.9 %collective-permute-start.1 = (f32[536,128]{1,0:T(8,128)S(1)}, f32[536,128]{1,0:T(8,128)S(1)}, u32[]{:S(2)}, u32[]{:S(2)}) collective-permute-start(f32[536,128]{1,0:T(8,128)S(1)} %get-tuple-element.103), channel_id=1, source_target_pairs={{0,8},{1,9},{2,10},{3,11},{4,12},{5,13},{6,14},{7,15},{8,0},{9,1},... | collective-permute-start | bytes 823304 | tf_op jit(solution)/shard_map/ppermute | solution.py:113
  12.4 1.5 collective-permute-start.2
  13.9 5.8 %collective-permute-done.1.refs_1_ = f32[536,128]{1,0:T(8,128)S(1)} collective-permute-done((f32[536,128]{1,0:T(8,128)S(1)}, f32[536,128]{1,0:T(8,128)S(1)}, u32[]{:S(2)}, u32[]{:S(2)}) %collective-permute-start.1) | collective-permute-done | bytes 274464 | tf_op jit(solution)/shard_map/ppermute | solution.py:113
  19.8 6.9 %collective-permute-done.2.refs_2_ = f32[536,128]{1,0:T(8,128)S(1)} collective-permute-done((f32[536,128]{1,0:T(8,128)S(1)}, f32[536,128]{1,0:T(8,128)S(1)}, u32[]{:S(2)}, u32[]{:S(2)}) %collective-permute-start.2) | collective-permute-done | bytes 274464 | tf_op jit(solution)/shard_map/ppermute | solution.py:113
  26.7 1.6 collective-permute-start.4
  28.3 2.6 %collective-permute-start.5 = (f32[200,128]{1,0:T(8,128)S(1)}, f32[200,128]{1,0:T(8,128)S(1)}, u32[]{:S(2)}, u32[]{:S(2)}) collective-permute-start(f32[200,128]{1,0:T(8,128)S(1)} %get-tuple-element.108), channel_id=1, source_target_pairs={{0,4},{1,5},{2,6},{3,7},{4,0},{5,1},{6,2},{7,3},{8,12},{9,13},{10,... | collective-permute-start | bytes 307208 | tf_op jit(solution)/shard_map/ppermute | solution.py:113
  32.4 5.9 %collective-permute-done.5.refs_2_ = f32[200,128]{1,0:T(8,128)S(1)} collective-permute-done((f32[200,128]{1,0:T(8,128)S(1)}, f32[200,128]{1,0:T(8,128)S(1)}, u32[]{:S(2)}, u32[]{:S(2)}) %collective-permute-start.5) | collective-permute-done | bytes 102432 | tf_op jit(solution)/shard_map/ppermute | solution.py:113
  38.4 2.5 %collective-permute-start.9 = (f32[128,128]{1,0:T(8,128)S(1)}, f32[128,128]{1,0:T(8,128)S(1)}, u32[]{:S(2)}, u32[]{:S(2)}) collective-permute-start(f32[128,128]{1,0:T(8,128)S(1)} %get-tuple-element.122), channel_id=1, source_target_pairs={{0,6},{1,7},{2,4},{3,5},{4,2},{5,3},{6,0},{7,1},{8,14},{9,15},{10,... | collective-permute-start | bytes 196616 | tf_op jit(solution)/shard_map/ppermute | solution.py:113
  44.6 2.1 %collective-permute-done.8 = f32[128,128]{1,0:T(8,128)S(1)} collective-permute-done((f32[128,128]{1,0:T(8,128)S(1)}, f32[128,128]{1,0:T(8,128)S(1)}, u32[]{:S(2)}, u32[]{:S(2)}) %collective-permute-start.8) | collective-permute-done | bytes 65568 | tf_op jit(solution)/shard_map/ppermute | solution.py:113
  46.8 1.5 collective-permute-start.13
  50.4 4.8 %collective-permute-done.13.refs_7_ = f32[512,128]{1,0:T(8,128)S(1)} collective-permute-done((f32[512,128]{1,0:T(8,128)S(1)}, f32[512,128]{1,0:T(8,128)S(1)}, u32[]{:S(2)}, u32[]{:S(2)}) %collective-permute-start.13) | collective-permute-done | bytes 262176 | tf_op jit(solution)/shard_map/ppermute | solution.py:113
  55.2 2.7 %collective-permute-done.12.refs_6_ = f32[512,128]{1,0:T(8,128)S(1)} collective-permute-done((f32[512,128]{1,0:T(8,128)S(1)}, f32[512,128]{1,0:T(8,128)S(1)}, u32[]{:S(2)}, u32[]{:S(2)}) %collective-permute-start.12) | collective-permute-done | bytes 262176 | tf_op jit(solution)/shard_map/ppermute | solution.py:113
  61.4 35.2 %shard_map.64 = (bf16[256,1024]{1,0:T(8,128)(2,1)}, bf16[256,1024]{1,0:T(8,128)(2,1)S(1)}, bf16[256,256]{1,0:T(8,128)(2,1)S(1)}, bf16[256,256]{1,0:T(8,128)(2,1)...) custom-call(s32[1,1]{1,0:T(1,128)} %bitcast.pos_ref.refs_0_, ...), custom_call_target="tpu_custom_call" | custom-call | flops 30000001024 | bytes 1000000 | tf_op jit(solution)/shard_map/pallas_call | solution.py:567
  96.7 2.7 %collective-permute-done.21.refs_1_ = f32[2072,128]{1,0:T(8,128)S(1)} collective-permute-done((f32[2072,128]{1,0:T(8,128)S(1)}, f32[2072,128]{1,0:T(8,128)S(1)}, u32[]{:S(2)}, u32[]{:S(2)}) %collective-permute-start.21) | collective-permute-done | bytes 1060896 | tf_op jit(solution)/shard_map/ppermute | solution.py:113
  103.1 5.9 %collective-permute-done.22.refs_1_ = f32[536,128]{1,0:T(8,128)S(1)} collective-permute-done((f32[536,128]{1,0:T(8,128)S(1)}, f32[536,128]{1,0:T(8,128)S(1)}, u32[]{:S(2)}, u32[]{:S(2)}) %collective-permute-start.22) | collective-permute-done | bytes 274464 | tf_op jit(solution)/shard_map/ppermute | solution.py:113
  109.0 6.2 %collective-permute-done.23.refs_2_ = f32[536,128]{1,0:T(8,128)S(1)} collective-permute-done((f32[536,128]{1,0:T(8,128)S(1)}, f32[536,128]{1,0:T(8,128)S(1)}, u32[]{:S(2)}, u32[]{:S(2)}) %collective-permute-start.23) | collective-permute-done | bytes 274464 | tf_op jit(solution)/shard_map/ppermute | solution.py:113
  117.6 2.1 %collective-permute-start.27 = (f32[152,128]{1,0:T(8,128)S(1)}, f32[152,128]{1,0:T(8,128)S(1)}, u32[]{:S(2)}, u32[]{:S(2)}) collective-permute-start(f32[152,128]{1,0:T(8,128)S(1)} %get-tuple-element.143), channel_id=1, source_target_pairs={{0,6},{1,7},{2,4},{3,5},{4,2},{5,3},{6,0},{7,1},{8,14},{9,15},{10,... | collective-permute-start | bytes 233480 | tf_op jit(solution)/shard_map/ppermute | solution.py:113
  119.8 4.7 %collective-permute-done.26.refs_2_ = f32[152,128]{1,0:T(8,128)S(1)} collective-permute-done((f32[152,128]{1,0:T(8,128)S(1)}, f32[152,128]{1,0:T(8,128)S(1)}, u32[]{:S(2)}, u32[]{:S(2)}) %collective-permute-start.26) | collective-permute-done | bytes 77856 | tf_op jit(solution)/shard_map/ppermute | solution.py:113
  124.6 1.9 collective-permute-start.30
  127.5 1.5 collective-permute-start.28
  130.7 1.7 collective-permute-done.29
  136.1 5.1 %collective-permute-done.33.refs_10_ = f32[512,128]{1,0:T(8,128)S(1)} collective-permute-done((f32[512,128]{1,0:T(8,128)S(1)}, f32[512,128]{1,0:T(8,128)S(1)}, u32[]{:S(2)}, u32[]{:S(2)}) %collective-permute-start.33) | collective-permute-done | bytes 262176 | tf_op jit(solution)/shard_map/ppermute | solution.py:113
  141.2 2.4 %collective-permute-done.32.refs_9_ = f32[512,128]{1,0:T(8,128)S(1)} collective-permute-done((f32[512,128]{1,0:T(8,128)S(1)}, f32[512,128]{1,0:T(8,128)S(1)}, u32[]{:S(2)}, u32[]{:S(2)}) %collective-permute-start.32) | collective-permute-done | bytes 262176 | tf_op jit(solution)/shard_map/ppermute | solution.py:113
  145.5 4.9 %shard_map.69 = (bf16[256,1024]{1,0:T(8,128)(2,1)S(1)}, f32[256,384]{1,0:T(8,128)S(1)}, f32[256,384]{1,0:T(8,128)S(1)}, f32[256,256]{1,0:T(8,128)S(1)}) custom-call(s32[1,1]{1,0:T(1,128)} %bitcast.pos_ref.refs_0_, f32[24,128]{1,0:T(8,128)S(1)} %get-tuple-element.144.refs_1_, f32[256,1024]{1,0:T(8,128)S(1)} %get-tuple-element.145.refs_2_, ...), custom_call_target="tpu_custom_call" | custom-call | flops 1000000 | bytes 1000000 | tf_op jit(solution)/shard_map/pallas_call | solution.py:567
  153.0 2.3 %convolution_convert_fusion = bf16[256,2048]{1,0:T(8,128)(2,1)} fusion(bf16[256,1024]{1,0:T(8,128)(2,1)S(1)} %get-tuple-element.163, bf16[2048,1024]{1,0:T(8,128)(2,1)S(1)} %copy-done.2), kind=kOutput, calls=%fused_computation | convolution fusion | flops 1074266112 | bytes 5767168 | tf_op jit(solution)/shard_map/dot_general | solution.py:57
  155.3 3.9 %collective-permute-done.43.refs_2_ = f32[256,256]{1,0:T(8,128)S(1)} collective-permute-done((f32[256,256]{1,0:T(8,128)S(1)}, f32[256,256]{1,0:T(8,128)S(1)}, u32[]{:S(2)}, u32[]{:S(2)}) %collective-permute-start.43) | collective-permute-done | bytes 262176 | tf_op jit(solution)/shard_map/ppermute | solution.py:113
  159.2 1.5 collective-permute-done.44.refs_3_
  169.5 9.3 %collective-permute-done.49 = f32[256,256]{1,0:T(8,128)S(1)} collective-permute-done((f32[256,256]{1,0:T(8,128)S(1)}, f32[256,256]{1,0:T(8,128)S(1)}, u32[]{:S(2)}, u32[]{:S(2)}) %collective-permute-start.49) | collective-permute-done | bytes 262176 | tf_op jit(solution)/shard_map/ppermute | solution.py:113
  181.2 4.2 %collective-permute-done.51 = f32[128,256]{1,0:T(8,128)S(1)} collective-permute-done((f32[128,256]{1,0:T(8,128)S(1)}, f32[128,256]{1,0:T(8,128)S(1)}, u32[]{:S(2)}, u32[]{:S(2)}) %collective-permute-start.51) | collective-permute-done | bytes 131104 | tf_op jit(solution)/shard_map/ppermute | solution.py:113
  186.5 3.9 %collective-permute-done.50 = f32[128,768]{1,0:T(8,128)S(1)} collective-permute-done((f32[128,768]{1,0:T(8,128)S(1)}, f32[128,768]{1,0:T(8,128)S(1)}, u32[]{:S(2)}, u32[]{:S(2)}) %collective-permute-start.50) | collective-permute-done | bytes 393248 | tf_op jit(solution)/shard_map/ppermute | solution.py:113
  191.5 7.6 %collective-permute-done.52 = f32[64,768]{1,0:T(8,128)S(1)} collective-permute-done((f32[64,768]{1,0:T(8,128)S(1)}, f32[64,768]{1,0:T(8,128)S(1)}, u32[]{:S(2)}, u32[]{:S(2)}) %collective-permute-start.52) | collective-permute-done | bytes 196640 | tf_op jit(solution)/shard_map/ppermute | solution.py:113
  (114 shorter events, 45.2 us)
Async XLA Ops:
  7.8 35.0 %collective-permute-start.10 = (f32[1024,256]{1,0:T(8,128)S(1)}, f32[1024,256]{1,0:T(8,128)S(1)}, u32[]{:S(2)}, u32[]{:S(2)}) collective-permute-start(f32[1024,256]{1,0:T(8,128)S(1)} %get-tuple-element.115), channel_id=1, source_target_pairs={{0,1},{1,0},{2,3},{3,2},{4,5},{5,4},{6,7},{7,6},{8,9},{9,8},{10,11... | collective-permute-start | bytes 3145736 | tf_op jit(solution)/shard_map/ppermute | solution.py:113
  9.5 10.3 %collective-permute-start.1 = (f32[536,128]{1,0:T(8,128)S(1)}, f32[536,128]{1,0:T(8,128)S(1)}, u32[]{:S(2)}, u32[]{:S(2)}) collective-permute-start(f32[536,128]{1,0:T(8,128)S(1)} %get-tuple-element.103), channel_id=1, source_target_pairs={{0,8},{1,9},{2,10},{3,11},{4,12},{5,13},{6,14},{7,15},{8,0},{9,1},... | collective-permute-start | bytes 823304 | tf_op jit(solution)/shard_map/ppermute | solution.py:113
  12.4 14.2 %collective-permute-start.2 = (f32[536,128]{1,0:T(8,128)S(1)}, f32[536,128]{1,0:T(8,128)S(1)}, u32[]{:S(2)}, u32[]{:S(2)}) collective-permute-start(f32[536,128]{1,0:T(8,128)S(1)} %get-tuple-element.104), channel_id=1, source_target_pairs={{0,16},{1,17},{2,18},{3,19},{4,20},{5,21},{6,22},{7,23},{8,24},{9,... | collective-permute-start | bytes 823304 | tf_op jit(solution)/shard_map/ppermute | solution.py:113
  13.9 12.7 %collective-permute-start.3 = (f32[536,128]{1,0:T(8,128)S(1)}, f32[536,128]{1,0:T(8,128)S(1)}, u32[]{:S(2)}, u32[]{:S(2)}) collective-permute-start(f32[536,128]{1,0:T(8,128)S(1)} %get-tuple-element.105), channel_id=1, source_target_pairs={{0,24},{1,25},{2,26},{3,27},{4,28},{5,29},{6,30},{7,31},{8,16},{9,... | collective-permute-start | bytes 823304 | tf_op jit(solution)/shard_map/ppermute | solution.py:113
  28.3 10.0 %collective-permute-start.5 = (f32[200,128]{1,0:T(8,128)S(1)}, f32[200,128]{1,0:T(8,128)S(1)}, u32[]{:S(2)}, u32[]{:S(2)}) collective-permute-start(f32[200,128]{1,0:T(8,128)S(1)} %get-tuple-element.108), channel_id=1, source_target_pairs={{0,4},{1,5},{2,6},{3,7},{4,0},{5,1},{6,2},{7,3},{8,12},{9,13},{10,... | collective-permute-start | bytes 307208 | tf_op jit(solution)/shard_map/ppermute | solution.py:113
  30.9 7.4 %collective-permute-start.6 = (f32[200,128]{1,0:T(8,128)S(1)}, f32[200,128]{1,0:T(8,128)S(1)}, u32[]{:S(2)}, u32[]{:S(2)}) collective-permute-start(f32[200,128]{1,0:T(8,128)S(1)} %get-tuple-element.109), channel_id=1, source_target_pairs={{0,6},{1,7},{2,4},{3,5},{4,2},{5,3},{6,0},{7,1},{8,14},{9,15},{10,... | collective-permute-start | bytes 307208 | tf_op jit(solution)/shard_map/ppermute | solution.py:113
  38.4 6.3 %collective-permute-start.9 = (f32[128,128]{1,0:T(8,128)S(1)}, f32[128,128]{1,0:T(8,128)S(1)}, u32[]{:S(2)}, u32[]{:S(2)}) collective-permute-start(f32[128,128]{1,0:T(8,128)S(1)} %get-tuple-element.122), channel_id=1, source_target_pairs={{0,6},{1,7},{2,4},{3,5},{4,2},{5,3},{6,0},{7,1},{8,14},{9,15},{10,... | collective-permute-start | bytes 196616 | tf_op jit(solution)/shard_map/ppermute | solution.py:113
  46.8 8.3 %collective-permute-start.13 = (f32[512,128]{1,0:T(8,128)S(1)}, f32[512,128]{1,0:T(8,128)S(1)}, u32[]{:S(2)}, u32[]{:S(2)}) collective-permute-start(f32[512,128]{1,0:T(8,128)S(1)} %constant_dynamic-update-slice_fusion.refs_4_), channel_id=1, source_target_pairs={{0,24},{1,25},{2,26},{3,27},{4,28},{5,29},{6,30},{7,31},{8,16},{9,... | collective-permute-start | bytes 786440 | tf_op jit(solution)/shard_map/ppermute | solution.py:113
  48.3 9.5 %collective-permute-start.12 = (f32[512,128]{1,0:T(8,128)S(1)}, f32[512,128]{1,0:T(8,128)S(1)}, u32[]{:S(2)}, u32[]{:S(2)}) collective-permute-start(f32[512,128]{1,0:T(8,128)S(1)} %constant_dynamic-update-slice_fusion.refs_4_), channel_id=1, source_target_pairs={{0,16},{1,17},{2,18},{3,19},{4,20},{5,21},{6,22},{7,23},{8,24},{9,... | collective-permute-start | bytes 786440 | tf_op jit(solution)/shard_map/ppermute | solution.py:113
  49.8 8.1 %collective-permute-start.11 = (f32[512,128]{1,0:T(8,128)S(1)}, f32[512,128]{1,0:T(8,128)S(1)}, u32[]{:S(2)}, u32[]{:S(2)}) collective-permute-start(f32[512,128]{1,0:T(8,128)S(1)} %constant_dynamic-update-slice_fusion.refs_4_), channel_id=1, source_target_pairs={{0,8},{1,9},{2,10},{3,11},{4,12},{5,13},{6,14},{7,15},{8,0},{9,1},... | collective-permute-start | bytes 786440 | tf_op jit(solution)/shard_map/ppermute | solution.py:113
  50.4 9.4 %collective-permute-start.14 = (f32[512,128]{1,0:T(8,128)S(1)}, f32[512,128]{1,0:T(8,128)S(1)}, u32[]{:S(2)}, u32[]{:S(2)}) collective-permute-start(f32[512,128]{1,0:T(8,128)S(1)} %constant_dynamic-update-slice_fusion.refs_4_), channel_id=1, source_target_pairs={{0,1},{1,0},{2,3},{3,2},{4,5},{5,4},{6,7},{7,6},{8,9},{9,8},{10,11... | collective-permute-start | bytes 786440 | tf_op jit(solution)/shard_map/ppermute | solution.py:113
  58.4 38.3 %collective-permute-start.18 = (f32[512,512]{1,0:T(8,128)S(1)}, f32[512,512]{1,0:T(8,128)S(1)}, u32[]{:S(2)}, u32[]{:S(2)}) collective-permute-start(f32[512,512]{1,0:T(8,128)S(1)} %get-tuple-element.130), channel_id=1, source_target_pairs={{0,8},{1,9},{2,10},{3,11},{4,12},{5,13},{6,14},{7,15},{8,0},{9,1},... | collective-permute-start | bytes 3145736 | tf_op jit(solution)/shard_map/ppermute | solution.py:113
  59.8 36.8 %collective-permute-start.19 = (f32[512,512]{1,0:T(8,128)S(1)}, f32[512,512]{1,0:T(8,128)S(1)}, u32[]{:S(2)}, u32[]{:S(2)}) collective-permute-start(f32[512,512]{1,0:T(8,128)S(1)} %get-tuple-element.131), channel_id=1, source_target_pairs={{0,16},{1,17},{2,18},{3,19},{4,20},{5,21},{6,22},{7,23},{8,24},{9,... | collective-permute-start | bytes 3145736 | tf_op jit(solution)/shard_map/ppermute | solution.py:113
  60.4 36.2 %collective-permute-start.20 = (f32[512,512]{1,0:T(8,128)S(1)}, f32[512,512]{1,0:T(8,128)S(1)}, u32[]{:S(2)}, u32[]{:S(2)}) collective-permute-start(f32[512,512]{1,0:T(8,128)S(1)} %get-tuple-element.132), channel_id=1, source_target_pairs={{0,2},{1,3},{2,0},{3,1},{4,6},{5,7},{6,4},{7,5},{8,10},{9,11},{10,... | collective-permute-start | bytes 3145736 | tf_op jit(solution)/shard_map/ppermute | solution.py:113
  99.5 9.5 %collective-permute-start.22 = (f32[536,128]{1,0:T(8,128)S(1)}, f32[536,128]{1,0:T(8,128)S(1)}, u32[]{:S(2)}, u32[]{:S(2)}) collective-permute-start(f32[536,128]{1,0:T(8,128)S(1)} %get-tuple-element.137), channel_id=1, source_target_pairs={{0,8},{1,9},{2,10},{3,11},{4,12},{5,13},{6,14},{7,15},{8,0},{9,1},... | collective-permute-start | bytes 823304 | tf_op jit(solution)/shard_map/ppermute | solution.py:113
  101.0 14.2 %collective-permute-start.23 = (f32[536,128]{1,0:T(8,128)S(1)}, f32[536,128]{1,0:T(8,128)S(1)}, u32[]{:S(2)}, u32[]{:S(2)}) collective-permute-start(f32[536,128]{1,0:T(8,128)S(1)} %get-tuple-element.138), channel_id=1, source_target_pairs={{0,16},{1,17},{2,18},{3,19},{4,20},{5,21},{6,22},{7,23},{8,24},{9,... | collective-permute-start | bytes 823304 | tf_op jit(solution)/shard_map/ppermute | solution.py:113
  101.6 13.5 %collective-permute-start.24 = (f32[536,128]{1,0:T(8,128)S(1)}, f32[536,128]{1,0:T(8,128)S(1)}, u32[]{:S(2)}, u32[]{:S(2)}) collective-permute-start(f32[536,128]{1,0:T(8,128)S(1)} %get-tuple-element.139), channel_id=1, source_target_pairs={{0,24},{1,25},{2,26},{3,27},{4,28},{5,29},{6,30},{7,31},{8,16},{9,... | collective-permute-start | bytes 823304 | tf_op jit(solution)/shard_map/ppermute | solution.py:113
  116.4 8.2 %collective-permute-start.26 = (f32[152,128]{1,0:T(8,128)S(1)}, f32[152,128]{1,0:T(8,128)S(1)}, u32[]{:S(2)}, u32[]{:S(2)}) collective-permute-start(f32[152,128]{1,0:T(8,128)S(1)} %get-tuple-element.142), channel_id=1, source_target_pairs={{0,4},{1,5},{2,6},{3,7},{4,0},{5,1},{6,2},{7,3},{8,12},{9,13},{10,... | collective-permute-start | bytes 233480 | tf_op jit(solution)/shard_map/ppermute | solution.py:113
  117.6 6.9 %collective-permute-start.27 = (f32[152,128]{1,0:T(8,128)S(1)}, f32[152,128]{1,0:T(8,128)S(1)}, u32[]{:S(2)}, u32[]{:S(2)}) collective-permute-start(f32[152,128]{1,0:T(8,128)S(1)} %get-tuple-element.143), channel_id=1, source_target_pairs={{0,6},{1,7},{2,4},{3,5},{4,2},{5,3},{6,0},{7,1},{8,14},{9,15},{10,... | collective-permute-start | bytes 233480 | tf_op jit(solution)/shard_map/ppermute | solution.py:113
  124.6 6.1 %collective-permute-start.30 = (f32[128,128]{1,0:T(8,128)S(1)}, f32[128,128]{1,0:T(8,128)S(1)}, u32[]{:S(2)}, u32[]{:S(2)}) collective-permute-start(f32[128,128]{1,0:T(8,128)S(1)} %get-tuple-element.156), channel_id=1, source_target_pairs={{0,6},{1,7},{2,4},{3,5},{4,2},{5,3},{6,0},{7,1},{8,14},{9,15},{10,... | collective-permute-start | bytes 196616 | tf_op jit(solution)/shard_map/ppermute | solution.py:113
  132.5 8.7 %collective-permute-start.33 = (f32[512,128]{1,0:T(8,128)S(1)}, f32[512,128]{1,0:T(8,128)S(1)}, u32[]{:S(2)}, u32[]{:S(2)}) collective-permute-start(f32[512,128]{1,0:T(8,128)S(1)} %constant_dynamic-update-slice_fusion.4.refs_7_), channel_id=1, source_target_pairs={{0,24},{1,25},{2,26},{3,27},{4,28},{5,29},{6,30},{7,31},{8,16},{9,... | collective-permute-start | bytes 786440 | tf_op jit(solution)/shard_map/ppermute | solution.py:113
  134.0 9.6 %collective-permute-start.32 = (f32[512,128]{1,0:T(8,128)S(1)}, f32[512,128]{1,0:T(8,128)S(1)}, u32[]{:S(2)}, u32[]{:S(2)}) collective-permute-start(f32[512,128]{1,0:T(8,128)S(1)} %constant_dynamic-update-slice_fusion.4.refs_7_), channel_id=1, source_target_pairs={{0,16},{1,17},{2,18},{3,19},{4,20},{5,21},{6,22},{7,23},{8,24},{9,... | collective-permute-start | bytes 786440 | tf_op jit(solution)/shard_map/ppermute | solution.py:113
  134.6 9.0 %collective-permute-start.31 = (f32[512,128]{1,0:T(8,128)S(1)}, f32[512,128]{1,0:T(8,128)S(1)}, u32[]{:S(2)}, u32[]{:S(2)}) collective-permute-start(f32[512,128]{1,0:T(8,128)S(1)} %constant_dynamic-update-slice_fusion.4.refs_7_), channel_id=1, source_target_pairs={{0,8},{1,9},{2,10},{3,11},{4,12},{5,13},{6,14},{7,15},{8,0},{9,1},... | collective-permute-start | bytes 786440 | tf_op jit(solution)/shard_map/ppermute | solution.py:113
  136.1 8.1 %collective-permute-start.34 = (f32[512,128]{1,0:T(8,128)S(1)}, f32[512,128]{1,0:T(8,128)S(1)}, u32[]{:S(2)}, u32[]{:S(2)}) collective-permute-start(f32[512,128]{1,0:T(8,128)S(1)} %constant_dynamic-update-slice_fusion.4.refs_7_), channel_id=1, source_target_pairs={{0,1},{1,0},{2,3},{3,2},{4,5},{5,4},{6,7},{7,6},{8,9},{9,8},{10,11... | collective-permute-start | bytes 786440 | tf_op jit(solution)/shard_map/ppermute | solution.py:113
  150.6 8.6 %collective-permute-start.43 = (f32[256,256]{1,0:T(8,128)S(1)}, f32[256,256]{1,0:T(8,128)S(1)}, u32[]{:S(2)}, u32[]{:S(2)}) collective-permute-start(f32[256,256]{1,0:T(8,128)S(1)} %get-tuple-element.162.refs_0_), channel_id=1, source_target_pairs={{0,2},{1,3},{2,0},{3,1},{4,6},{5,7},{6,4},{7,5},{8,10},{9,11},{10,... | collective-permute-start | bytes 786440 | tf_op jit(solution)/shard_map/ppermute | solution.py:113
  151.1 11.5 %collective-permute-start.38 = (f32[256,384]{1,0:T(8,128)S(1)}, f32[256,384]{1,0:T(8,128)S(1)}, u32[]{:S(2)}, u32[]{:S(2)}) collective-permute-start(f32[256,384]{1,0:T(8,128)S(1)} %get-tuple-element.160.refs_0_), channel_id=1, source_target_pairs={{0,8},{1,9},{2,10},{3,11},{4,12},{5,13},{6,14},{7,15},{8,0},{9,1},... | collective-permute-start | bytes 1179656 | tf_op jit(solution)/shard_map/ppermute | solution.py:113
  152.2 11.4 %collective-permute-start.39 = (f32[256,384]{1,0:T(8,128)S(1)}, f32[256,384]{1,0:T(8,128)S(1)}, u32[]{:S(2)}, u32[]{:S(2)}) collective-permute-start(f32[256,384]{1,0:T(8,128)S(1)} %get-tuple-element.161.refs_0_), channel_id=1, source_target_pairs={{0,16},{1,17},{2,18},{3,19},{4,20},{5,21},{6,22},{7,23},{8,24},{9,... | collective-permute-start | bytes 1179656 | tf_op jit(solution)/shard_map/ppermute | solution.py:113
  164.0 14.7 %collective-permute-start.49 = (f32[256,256]{1,0:T(8,128)S(1)}, f32[256,256]{1,0:T(8,128)S(1)}, u32[]{:S(2)}, u32[]{:S(2)}) collective-permute-start(f32[256,256]{1,0:T(8,128)S(1)} %get-tuple-element.172), channel_id=1, source_target_pairs={{0,4},{1,5},{2,6},{3,7},{4,0},{5,1},{6,2},{7,3},{8,12},{9,13},{10,... | collective-permute-start | bytes 786440 | tf_op jit(solution)/shard_map/ppermute | solution.py:113
  166.2 12.6 %collective-permute-start.46 = (f32[256,384]{1,0:T(8,128)S(1)}, f32[256,384]{1,0:T(8,128)S(1)}, u32[]{:S(2)}, u32[]{:S(2)}) collective-permute-start(f32[256,384]{1,0:T(8,128)S(1)} %get-tuple-element.176), channel_id=1, source_target_pairs={{0,16},{1,17},{2,18},{3,19},{4,20},{5,21},{6,22},{7,23},{8,24},{9,... | collective-permute-start | bytes 1179656 | tf_op jit(solution)/shard_map/ppermute | solution.py:113
  168.3 10.6 %collective-permute-start.48 = (f32[256,384]{1,0:T(8,128)S(1)}, f32[256,384]{1,0:T(8,128)S(1)}, u32[]{:S(2)}, u32[]{:S(2)}) collective-permute-start(f32[256,384]{1,0:T(8,128)S(1)} %get-tuple-element.182), channel_id=1, source_target_pairs={{0,8},{1,9},{2,10},{3,11},{4,12},{5,13},{6,14},{7,15},{8,0},{9,1},... | collective-permute-start | bytes 1179656 | tf_op jit(solution)/shard_map/ppermute | solution.py:113
  179.0 11.4 %collective-permute-start.50 = (f32[128,768]{1,0:T(8,128)S(1)}, f32[128,768]{1,0:T(8,128)S(1)}, u32[]{:S(2)}, u32[]{:S(2)}) collective-permute-start(f32[128,768]{1,0:T(8,128)S(1)} %get-tuple-element.198), channel_id=1, source_target_pairs={{0,2},{1,5},{2,0},{3,7},{4,6},{5,1},{6,4},{7,3},{8,10},{9,13},{10,... | collective-permute-start | bytes 1179656 | tf_op jit(solution)/shard_map/ppermute | solution.py:113
  190.5 8.7 %collective-permute-start.52 = (f32[64,768]{1,0:T(8,128)S(1)}, f32[64,768]{1,0:T(8,128)S(1)}, u32[]{:S(2)}, u32[]{:S(2)}) collective-permute-start(f32[64,768]{1,0:T(8,128)S(1)} %slice_add_fusion.2), channel_id=1, source_target_pairs={{0,4},{1,3},{2,6},{3,1},{4,0},{5,7},{6,2},{7,5},{8,12},{9,11},{10,... | collective-permute-start | bytes 589832 | tf_op jit(solution)/shard_map/ppermute | solution.py:113
  (25 other events, 127.0 us)

commit v3 on v2

--- a/solution.py
+++ b/solution.py
@@ -85,23 +85,46 @@
 
 def rounds():
     groups, per = lax.axis_size("group"), lax.axis_size("dp")
-    out, at = [(1, 2)], per
+    out, at = [((1, 1), 2)], per
     for radix in radices(groups):
-        out.append((at, radix))
+        out.append(((at, at), radix))
         at *= radix
     at = 2
     for radix in radices(per // 2):
-        out.append((at, radix))
+        out.append(((at, at), radix))
         at *= radix
+    if crossed():
+        (one, radix), (two, _) = out[1:3]
+        out[1:3] = [((one[0], two[0]), radix), ((two[0], one[0]), radix)]
     return out
+
+
+def crossed():
+    group, rest = radices(lax.axis_size("group")), radices(lax.axis_size("dp") // 2)
+    return len(group) == 1 and len(rest) > 0 and group[0] == rest[0]
 
 
 def place():
     index = lax.axis_index("group") * lax.axis_size("dp") + lax.axis_index("dp")
     out = 0
-    for stride, radix in rounds():
+    for (stride, _), radix in rounds():
         out = out * radix + (index // stride) % radix
     return out.astype(jnp.int32).reshape(1, 1)
+
+
+def other_order(i):
+    if not crossed():
+        return i
+    radix = lax.axis_size("group")
+    low = lax.axis_size("dp") // 2 // radix
+    core, first, second = i // (low * radix * radix), i // (low * radix) % radix, i // low % radix
+    return ((core * radix + second) * radix + first) * low + i % low
+
+
+def chunk_at(pos, devices, i, same):
+    mine = pos // (devices // 2) == (0 if same else 1)
+    far = other_order(i)
+    return pos ^ (i if far == i else jnp.where(mine, i, far))
 
 
 def swap(x, stride, by):
@@ -136,7 +159,7 @@
     summed = keep.shape[0] - size - listed
     pieces = [keep, send]
     for at, (stride, radix) in enumerate(steps):
-        ins = [pieces[0]] + [swap(p, stride, by) for by, p in enumerate(pieces) if by]
+        ins = [pieces[0]] + [exchange(p, (by * stride[0], by * stride[1])) for by, p in enumerate(pieces) if by]
         after = steps[at + 1][1] if at + 1 < len(steps) else 1
         more = listed * radix + summed
         shapes = [(size // after + more, BLK)] * after if after > 1 else [(size, BLK), (more, BLK)]
@@ -155,7 +178,7 @@
     for at in range(len(steps) - 1, 0, -1):
         stride, radix = steps[at]
         whole = parts[0] if len(parts) == 1 else jnp.concatenate(parts, 0)
-        parts = [whole] + [swap(whole, stride, by) for by in range(1, radix)]
+        parts = [whole] + [exchange(whole, (by * stride[0], by * stride[1])) for by in range(1, radix)]
         if at == len(steps) - 1:
             parts, beside = lax.optimization_barrier((parts, beside))
     return parts + [swap(p, 1, 1) for p in parts], beside
@@ -171,7 +194,7 @@
     each = devices // len(parts)
     for i, part in enumerate(parts):
         for j in range(each):
-            to = pl.multiple_of(((i * each + j) ^ pos) * chunk, 8)
+            to = pl.multiple_of(chunk_at(pos, devices, i * each + j, i < len(parts) // 2) * chunk, 8)
             out_ref[pl.ds(to, chunk), :] = part[j * chunk : (j + 1) * chunk, :]
 
 
@@ -179,7 +202,7 @@
     chunk = src_ref.shape[0] // devices
     half = devices // 2
     for i in range(devices):
-        at = pl.multiple_of((i ^ pos) * chunk, 8)
+        at = pl.multiple_of(chunk_at(pos, devices, i, i < half) * chunk, 8)
         out = keep_ref if i < half else send_ref
         out[(i % half) * chunk : (i % half + 1) * chunk, :] = src_ref[pl.ds(at, chunk), :]
 

time: 200 us -> 191 us (0.955)
  waiting for transfers between devices: 95.7 us -> 84.1 us
  starting transfers between devices: 49.2 us -> 51.5 us
    ppermute x54, waiting for transfers between devices: 95.7 us -> 84.1 us  [exchange(): return lax.ppermute(x, AXES, [(i, i ^ bits[i % 2]) for i in range(count)])]
    ppermute x54, starting transfers between devices: 49.2 us -> 51.5 us  [exchange(): return lax.ppermute(x, AXES, [(i, i ^ bits[i % 2]) for i in range(count)])]
  transfers between devices with their start and end apart: 54 -> 54, of which waited for: 28 -> 31; matrix products, arithmetic and copies ran while one was open for 1% -> 1% of each run, Pallas kernels for 20% -> 21%
where the time goes in v3:
time: 191 us
  waiting for transfers between devices  84.1 us (44%)
  starting transfers between devices  51.5 us (27%)
  Pallas kernels  50.7 us (27%)
  matrix products  2.26 us (1%)
    ppermute x54, waiting for transfers between devices, exchange(): return lax.ppermute(x, AXES, [(i, i ^ bits[i % 2]) for i in range(count)])  84.1 us
    ppermute x54, starting transfers between devices, exchange(): return lax.ppermute(x, AXES, [(i, i ^ bits[i % 2]) for i in range(count)])  51.5 us
    pallas_call x15, Pallas kernels, call(): pl.pallas_call(kernel, out_shape=tuple((jax.ShapeDtypeStruct(s, t) for s,...  50.7 us
  transfers between devices with their start and end apart: 54, of which 31 were waited for; matrix products, arithmetic and copies ran while one was open for 1% of the time, Pallas kernels for 21%

profile of v3, /device:TPU:0, one launch (start us, length us, event | category | flops | bytes accessed | tf_op | source)
XLA Modules:
  0.0 190.7 jit_solution(6357600303089022132)
XLA Ops:
  0.7 5.8 %shard_map.58 = (f32[256,1024]{1,0:T(8,128)S(1)}, f32[2064,128]{1,0:T(8,128)S(1)}, f32[2064,128]{1,0:T(8,128)S(1)}, bf16[256,2048]{1,0:T(8,128)(2,1)S(1)}) custom-call(s32[1,1]{1,0:T(1,128)} %bitcast.pos_ref.refs_0_, bf16[256,2048]{1,0:T(8,128)(2,1)} %hid_hbm.1, bf16[2048,1024]{1,0:T(8,128)(2,1)} %w_hbm.1), custom_call_target="tpu_custom_call" | custom-call | flops 1000000 | bytes 1000000 | tf_op jit(solution)/shard_map/pallas_call | solution.py:590
  9.5 2.9 %collective-permute-start.1 = (f32[536,128]{1,0:T(8,128)S(1)}, f32[536,128]{1,0:T(8,128)S(1)}, u32[]{:S(2)}, u32[]{:S(2)}) collective-permute-start(f32[536,128]{1,0:T(8,128)S(1)} %get-tuple-element.103), channel_id=1, source_target_pairs={{0,8},{1,3},{2,10},{3,1},{4,12},{5,7},{6,14},{7,5},{8,0},{9,11},{1... | collective-permute-start | bytes 823304 | tf_op jit(solution)/shard_map/ppermute | solution.py:136
  13.9 2.9 %collective-permute-done.1.refs_1_ = f32[536,128]{1,0:T(8,128)S(1)} collective-permute-done((f32[536,128]{1,0:T(8,128)S(1)}, f32[536,128]{1,0:T(8,128)S(1)}, u32[]{:S(2)}, u32[]{:S(2)}) %collective-permute-start.1) | collective-permute-done | bytes 274464 | tf_op jit(solution)/shard_map/ppermute | solution.py:136
  16.9 5.0 %collective-permute-done.2.refs_2_ = f32[536,128]{1,0:T(8,128)S(1)} collective-permute-done((f32[536,128]{1,0:T(8,128)S(1)}, f32[536,128]{1,0:T(8,128)S(1)}, u32[]{:S(2)}, u32[]{:S(2)}) %collective-permute-start.2) | collective-permute-done | bytes 274464 | tf_op jit(solution)/shard_map/ppermute | solution.py:136
  21.9 1.6 collective-permute-start.4
  23.6 2.6 %collective-permute-start.5 = (f32[200,128]{1,0:T(8,128)S(1)}, f32[200,128]{1,0:T(8,128)S(1)}, u32[]{:S(2)}, u32[]{:S(2)}) collective-permute-start(f32[200,128]{1,0:T(8,128)S(1)} %get-tuple-element.108), channel_id=1, source_target_pairs={{0,4},{1,17},{2,6},{3,19},{4,0},{5,21},{6,2},{7,23},{8,12},{9,25},... | collective-permute-start | bytes 307208 | tf_op jit(solution)/shard_map/ppermute | solution.py:136
  26.7 3.6 %collective-permute-done.5.refs_2_ = f32[200,128]{1,0:T(8,128)S(1)} collective-permute-done((f32[200,128]{1,0:T(8,128)S(1)}, f32[200,128]{1,0:T(8,128)S(1)}, u32[]{:S(2)}, u32[]{:S(2)}) %collective-permute-start.5) | collective-permute-done | bytes 102432 | tf_op jit(solution)/shard_map/ppermute | solution.py:136
  30.2 2.4 %collective-permute-done.6.refs_3_ = f32[200,128]{1,0:T(8,128)S(1)} collective-permute-done((f32[200,128]{1,0:T(8,128)S(1)}, f32[200,128]{1,0:T(8,128)S(1)}, u32[]{:S(2)}, u32[]{:S(2)}) %collective-permute-start.6) | collective-permute-done | bytes 102432 | tf_op jit(solution)/shard_map/ppermute | solution.py:136
  34.2 2.9 %collective-permute-start.7 = (f32[128,128]{1,0:T(8,128)S(1)}, f32[128,128]{1,0:T(8,128)S(1)}, u32[]{:S(2)}, u32[]{:S(2)}) collective-permute-start(f32[128,128]{1,0:T(8,128)S(1)} %get-tuple-element.122), channel_id=1, source_target_pairs={{0,2},{1,9},{2,0},{3,11},{4,6},{5,13},{6,4},{7,15},{8,10},{9,1},{1... | collective-permute-start | bytes 196616 | tf_op jit(solution)/shard_map/ppermute | solution.py:136
  40.2 1.7 collective-permute-start.13
  43.8 3.9 %collective-permute-done.13.refs_7_ = f32[512,128]{1,0:T(8,128)S(1)} collective-permute-done((f32[512,128]{1,0:T(8,128)S(1)}, f32[512,128]{1,0:T(8,128)S(1)}, u32[]{:S(2)}, u32[]{:S(2)}) %collective-permute-start.13) | collective-permute-done | bytes 262176 | tf_op jit(solution)/shard_map/ppermute | solution.py:136
  47.7 2.7 %collective-permute-done.12.refs_6_ = f32[512,128]{1,0:T(8,128)S(1)} collective-permute-done((f32[512,128]{1,0:T(8,128)S(1)}, f32[512,128]{1,0:T(8,128)S(1)}, u32[]{:S(2)}, u32[]{:S(2)}) %collective-permute-start.12) | collective-permute-done | bytes 262176 | tf_op jit(solution)/shard_map/ppermute | solution.py:136
  51.8 1.7 collective-permute-start.18
  54.3 35.2 %shard_map.64 = (bf16[256,1024]{1,0:T(8,128)(2,1)}, bf16[256,1024]{1,0:T(8,128)(2,1)S(1)}, bf16[256,256]{1,0:T(8,128)(2,1)S(1)}, bf16[256,256]{1,0:T(8,128)(2,1)...) custom-call(s32[1,1]{1,0:T(1,128)} %bitcast.pos_ref.refs_0_, ...), custom_call_target="tpu_custom_call" | custom-call | flops 30000001024 | bytes 1000000 | tf_op jit(solution)/shard_map/pallas_call | solution.py:590
  89.6 2.7 %collective-permute-done.21.refs_1_ = f32[2072,128]{1,0:T(8,128)S(1)} collective-permute-done((f32[2072,128]{1,0:T(8,128)S(1)}, f32[2072,128]{1,0:T(8,128)S(1)}, u32[]{:S(2)}, u32[]{:S(2)}) %collective-permute-start.21) | collective-permute-done | bytes 1060896 | tf_op jit(solution)/shard_map/ppermute | solution.py:136
  95.9 3.0 %collective-permute-done.22.refs_1_ = f32[536,128]{1,0:T(8,128)S(1)} collective-permute-done((f32[536,128]{1,0:T(8,128)S(1)}, f32[536,128]{1,0:T(8,128)S(1)}, u32[]{:S(2)}, u32[]{:S(2)}) %collective-permute-start.22) | collective-permute-done | bytes 274464 | tf_op jit(solution)/shard_map/ppermute | solution.py:136
  98.9 4.3 %collective-permute-done.23.refs_2_ = f32[536,128]{1,0:T(8,128)S(1)} collective-permute-done((f32[536,128]{1,0:T(8,128)S(1)}, f32[536,128]{1,0:T(8,128)S(1)}, u32[]{:S(2)}, u32[]{:S(2)}) %collective-permute-start.23) | collective-permute-done | bytes 274464 | tf_op jit(solution)/shard_map/ppermute | solution.py:136
  107.8 3.5 %collective-permute-done.26.refs_2_ = f32[152,128]{1,0:T(8,128)S(1)} collective-permute-done((f32[152,128]{1,0:T(8,128)S(1)}, f32[152,128]{1,0:T(8,128)S(1)}, u32[]{:S(2)}, u32[]{:S(2)}) %collective-permute-start.26) | collective-permute-done | bytes 77856 | tf_op jit(solution)/shard_map/ppermute | solution.py:136
  112.6 2.0 %collective-permute-start.30 = (f32[128,128]{1,0:T(8,128)S(1)}, f32[128,128]{1,0:T(8,128)S(1)}, u32[]{:S(2)}, u32[]{:S(2)}) collective-permute-start(f32[128,128]{1,0:T(8,128)S(1)} %get-tuple-element.156), channel_id=1, source_target_pairs={{0,6},{1,25},{2,4},{3,27},{4,2},{5,29},{6,0},{7,31},{8,14},{9,17},... | collective-permute-start | bytes 196616 | tf_op jit(solution)/shard_map/ppermute | solution.py:136
  115.1 1.9 %collective-permute-start.28 = (f32[128,128]{1,0:T(8,128)S(1)}, f32[128,128]{1,0:T(8,128)S(1)}, u32[]{:S(2)}, u32[]{:S(2)}) collective-permute-start(f32[128,128]{1,0:T(8,128)S(1)} %get-tuple-element.156), channel_id=1, source_target_pairs={{0,2},{1,9},{2,0},{3,11},{4,6},{5,13},{6,4},{7,15},{8,10},{9,1},{1... | collective-permute-start | bytes 196616 | tf_op jit(solution)/shard_map/ppermute | solution.py:136
  120.4 1.8 collective-permute-start.33
  124.6 3.2 %collective-permute-done.33.refs_10_ = f32[512,128]{1,0:T(8,128)S(1)} collective-permute-done((f32[512,128]{1,0:T(8,128)S(1)}, f32[512,128]{1,0:T(8,128)S(1)}, u32[]{:S(2)}, u32[]{:S(2)}) %collective-permute-start.33) | collective-permute-done | bytes 262176 | tf_op jit(solution)/shard_map/ppermute | solution.py:136
  127.8 2.7 %collective-permute-done.32.refs_9_ = f32[512,128]{1,0:T(8,128)S(1)} collective-permute-done((f32[512,128]{1,0:T(8,128)S(1)}, f32[512,128]{1,0:T(8,128)S(1)}, u32[]{:S(2)}, u32[]{:S(2)}) %collective-permute-start.32) | collective-permute-done | bytes 262176 | tf_op jit(solution)/shard_map/ppermute | solution.py:136
  130.5 3.2 %collective-permute-start.36 = (f32[512,128]{1,0:T(8,128)S(1)}, f32[512,128]{1,0:T(8,128)S(1)}, u32[]{:S(2)}, u32[]{:S(2)}) collective-permute-start(f32[512,128]{1,0:T(8,128)S(1)} %collective-permute-done.32.refs_9_), channel_id=1, source_target_pairs={{0,1},{1,0},{2,3},{3,2},{4,5},{5,4},{6,7},{7,6},{8,9},{9,8},{10,11... | collective-permute-start | bytes 786440 | tf_op jit(solution)/shard_map/ppermute | solution.py:136
  135.2 4.9 %shard_map.69 = (bf16[256,1024]{1,0:T(8,128)(2,1)S(1)}, f32[256,384]{1,0:T(8,128)S(1)}, f32[256,384]{1,0:T(8,128)S(1)}, f32[256,256]{1,0:T(8,128)S(1)}) custom-call(s32[1,1]{1,0:T(1,128)} %bitcast.pos_ref.refs_0_, f32[24,128]{1,0:T(8,128)S(1)} %get-tuple-element.144.refs_1_, f32[256,1024]{1,0:T(8,128)S(1)} %get-tuple-element.145.refs_2_, ...), custom_call_target="tpu_custom_call" | custom-call | flops 1000000 | bytes 1000000 | tf_op jit(solution)/shard_map/pallas_call | solution.py:590
  142.7 2.3 %convolution_convert_fusion = bf16[256,2048]{1,0:T(8,128)(2,1)} fusion(bf16[256,1024]{1,0:T(8,128)(2,1)S(1)} %get-tuple-element.163, bf16[2048,1024]{1,0:T(8,128)(2,1)S(1)} %copy-done.2), kind=kOutput, calls=%fused_computation | convolution fusion | flops 1074266112 | bytes 5767168 | tf_op jit(solution)/shard_map/dot_general | solution.py:57
  145.0 3.9 %collective-permute-done.43.refs_2_ = f32[256,256]{1,0:T(8,128)S(1)} collective-permute-done((f32[256,256]{1,0:T(8,128)S(1)}, f32[256,256]{1,0:T(8,128)S(1)}, u32[]{:S(2)}, u32[]{:S(2)}) %collective-permute-start.43) | collective-permute-done | bytes 262176 | tf_op jit(solution)/shard_map/ppermute | solution.py:136
  153.6 2.9 %collective-permute-start.49 = (f32[256,256]{1,0:T(8,128)S(1)}, f32[256,256]{1,0:T(8,128)S(1)}, u32[]{:S(2)}, u32[]{:S(2)}) collective-permute-start(f32[256,256]{1,0:T(8,128)S(1)} %get-tuple-element.172), channel_id=1, source_target_pairs={{0,4},{1,5},{2,6},{3,7},{4,0},{5,1},{6,2},{7,3},{8,12},{9,13},{10,... | collective-permute-start | bytes 786440 | tf_op jit(solution)/shard_map/ppermute | solution.py:136
  159.9 8.7 %collective-permute-done.49 = f32[256,256]{1,0:T(8,128)S(1)} collective-permute-done((f32[256,256]{1,0:T(8,128)S(1)}, f32[256,256]{1,0:T(8,128)S(1)}, u32[]{:S(2)}, u32[]{:S(2)}) %collective-permute-start.49) | collective-permute-done | bytes 262176 | tf_op jit(solution)/shard_map/ppermute | solution.py:136
  171.1 4.5 %collective-permute-done.51 = f32[128,256]{1,0:T(8,128)S(1)} collective-permute-done((f32[128,256]{1,0:T(8,128)S(1)}, f32[128,256]{1,0:T(8,128)S(1)}, u32[]{:S(2)}, u32[]{:S(2)}) %collective-permute-start.51) | collective-permute-done | bytes 131104 | tf_op jit(solution)/shard_map/ppermute | solution.py:136
  176.6 5.0 %collective-permute-done.50 = f32[128,768]{1,0:T(8,128)S(1)} collective-permute-done((f32[128,768]{1,0:T(8,128)S(1)}, f32[128,768]{1,0:T(8,128)S(1)}, u32[]{:S(2)}, u32[]{:S(2)}) %collective-permute-start.50) | collective-permute-done | bytes 393248 | tf_op jit(solution)/shard_map/ppermute | solution.py:136
  181.8 8.2 %collective-permute-done.52 = f32[64,768]{1,0:T(8,128)S(1)} collective-permute-done((f32[64,768]{1,0:T(8,128)S(1)}, f32[64,768]{1,0:T(8,128)S(1)}, u32[]{:S(2)}, u32[]{:S(2)}) %collective-permute-start.52) | collective-permute-done | bytes 196640 | tf_op jit(solution)/shard_map/ppermute | solution.py:136
  (114 shorter events, 46.1 us)
Async XLA Ops:
  7.8 29.3 %collective-permute-start.10 = (f32[1024,256]{1,0:T(8,128)S(1)}, f32[1024,256]{1,0:T(8,128)S(1)}, u32[]{:S(2)}, u32[]{:S(2)}) collective-permute-start(f32[1024,256]{1,0:T(8,128)S(1)} %get-tuple-element.115), channel_id=1, source_target_pairs={{0,1},{1,0},{2,3},{3,2},{4,5},{5,4},{6,7},{7,6},{8,9},{9,8},{10,11... | collective-permute-start | bytes 3145736 | tf_op jit(solution)/shard_map/ppermute | solution.py:136
  9.5 7.4 %collective-permute-start.1 = (f32[536,128]{1,0:T(8,128)S(1)}, f32[536,128]{1,0:T(8,128)S(1)}, u32[]{:S(2)}, u32[]{:S(2)}) collective-permute-start(f32[536,128]{1,0:T(8,128)S(1)} %get-tuple-element.103), channel_id=1, source_target_pairs={{0,8},{1,3},{2,10},{3,1},{4,12},{5,7},{6,14},{7,5},{8,0},{9,11},{1... | collective-permute-start | bytes 823304 | tf_op jit(solution)/shard_map/ppermute | solution.py:136
  12.4 9.4 %collective-permute-start.2 = (f32[536,128]{1,0:T(8,128)S(1)}, f32[536,128]{1,0:T(8,128)S(1)}, u32[]{:S(2)}, u32[]{:S(2)}) collective-permute-start(f32[536,128]{1,0:T(8,128)S(1)} %get-tuple-element.104), channel_id=1, source_target_pairs={{0,16},{1,5},{2,18},{3,7},{4,20},{5,1},{6,22},{7,3},{8,24},{9,13},... | collective-permute-start | bytes 823304 | tf_op jit(solution)/shard_map/ppermute | solution.py:136
  13.9 7.9 %collective-permute-start.3 = (f32[536,128]{1,0:T(8,128)S(1)}, f32[536,128]{1,0:T(8,128)S(1)}, u32[]{:S(2)}, u32[]{:S(2)}) collective-permute-start(f32[536,128]{1,0:T(8,128)S(1)} %get-tuple-element.105), channel_id=1, source_target_pairs={{0,24},{1,7},{2,26},{3,5},{4,28},{5,3},{6,30},{7,1},{8,16},{9,15},... | collective-permute-start | bytes 823304 | tf_op jit(solution)/shard_map/ppermute | solution.py:136
  23.6 6.7 %collective-permute-start.5 = (f32[200,128]{1,0:T(8,128)S(1)}, f32[200,128]{1,0:T(8,128)S(1)}, u32[]{:S(2)}, u32[]{:S(2)}) collective-permute-start(f32[200,128]{1,0:T(8,128)S(1)} %get-tuple-element.108), channel_id=1, source_target_pairs={{0,4},{1,17},{2,6},{3,19},{4,0},{5,21},{6,2},{7,23},{8,12},{9,25},... | collective-permute-start | bytes 307208 | tf_op jit(solution)/shard_map/ppermute | solution.py:136
  26.2 6.5 %collective-permute-start.6 = (f32[200,128]{1,0:T(8,128)S(1)}, f32[200,128]{1,0:T(8,128)S(1)}, u32[]{:S(2)}, u32[]{:S(2)}) collective-permute-start(f32[200,128]{1,0:T(8,128)S(1)} %get-tuple-element.109), channel_id=1, source_target_pairs={{0,6},{1,25},{2,4},{3,27},{4,2},{5,29},{6,0},{7,31},{8,14},{9,17},... | collective-permute-start | bytes 307208 | tf_op jit(solution)/shard_map/ppermute | solution.py:136
  33.9 6.3 %collective-permute-start.8 = (f32[128,128]{1,0:T(8,128)S(1)}, f32[128,128]{1,0:T(8,128)S(1)}, u32[]{:S(2)}, u32[]{:S(2)}) collective-permute-start(f32[128,128]{1,0:T(8,128)S(1)} %get-tuple-element.122), channel_id=1, source_target_pairs={{0,4},{1,17},{2,6},{3,19},{4,0},{5,21},{6,2},{7,23},{8,12},{9,25},... | collective-permute-start | bytes 196616 | tf_op jit(solution)/shard_map/ppermute | solution.py:136
  40.2 7.4 %collective-permute-start.13 = (f32[512,128]{1,0:T(8,128)S(1)}, f32[512,128]{1,0:T(8,128)S(1)}, u32[]{:S(2)}, u32[]{:S(2)}) collective-permute-start(f32[512,128]{1,0:T(8,128)S(1)} %constant_dynamic-update-slice_fusion.refs_4_), channel_id=1, source_target_pairs={{0,24},{1,7},{2,26},{3,5},{4,28},{5,3},{6,30},{7,1},{8,16},{9,15},... | collective-permute-start | bytes 786440 | tf_op jit(solution)/shard_map/ppermute | solution.py:136
  42.0 8.4 %collective-permute-start.12 = (f32[512,128]{1,0:T(8,128)S(1)}, f32[512,128]{1,0:T(8,128)S(1)}, u32[]{:S(2)}, u32[]{:S(2)}) collective-permute-start(f32[512,128]{1,0:T(8,128)S(1)} %constant_dynamic-update-slice_fusion.refs_4_), channel_id=1, source_target_pairs={{0,16},{1,5},{2,18},{3,7},{4,20},{5,1},{6,22},{7,3},{8,24},{9,13},... | collective-permute-start | bytes 786440 | tf_op jit(solution)/shard_map/ppermute | solution.py:136
  42.7 9.1 %collective-permute-start.11 = (f32[512,128]{1,0:T(8,128)S(1)}, f32[512,128]{1,0:T(8,128)S(1)}, u32[]{:S(2)}, u32[]{:S(2)}) collective-permute-start(f32[512,128]{1,0:T(8,128)S(1)} %constant_dynamic-update-slice_fusion.refs_4_), channel_id=1, source_target_pairs={{0,8},{1,3},{2,10},{3,1},{4,12},{5,7},{6,14},{7,5},{8,0},{9,11},{1... | collective-permute-start | bytes 786440 | tf_op jit(solution)/shard_map/ppermute | solution.py:136
  43.8 9.8 %collective-permute-start.14 = (f32[512,128]{1,0:T(8,128)S(1)}, f32[512,128]{1,0:T(8,128)S(1)}, u32[]{:S(2)}, u32[]{:S(2)}) collective-permute-start(f32[512,128]{1,0:T(8,128)S(1)} %constant_dynamic-update-slice_fusion.refs_4_), channel_id=1, source_target_pairs={{0,1},{1,0},{2,3},{3,2},{4,5},{5,4},{6,7},{7,6},{8,9},{9,8},{10,11... | collective-permute-start | bytes 786440 | tf_op jit(solution)/shard_map/ppermute | solution.py:136
  47.7 6.5 %collective-permute-start.17 = (f32[512,128]{1,0:T(8,128)S(1)}, f32[512,128]{1,0:T(8,128)S(1)}, u32[]{:S(2)}, u32[]{:S(2)}) collective-permute-start(f32[512,128]{1,0:T(8,128)S(1)} %collective-permute-done.13.refs_7_), channel_id=1, source_target_pairs={{0,1},{1,0},{2,3},{3,2},{4,5},{5,4},{6,7},{7,6},{8,9},{9,8},{10,11... | collective-permute-start | bytes 786440 | tf_op jit(solution)/shard_map/ppermute | solution.py:136
  51.8 37.7 %collective-permute-start.18 = (f32[512,512]{1,0:T(8,128)S(1)}, f32[512,512]{1,0:T(8,128)S(1)}, u32[]{:S(2)}, u32[]{:S(2)}) collective-permute-start(f32[512,512]{1,0:T(8,128)S(1)} %get-tuple-element.130), channel_id=1, source_target_pairs={{0,8},{1,9},{2,10},{3,11},{4,12},{5,13},{6,14},{7,15},{8,0},{9,1},... | collective-permute-start | bytes 3145736 | tf_op jit(solution)/shard_map/ppermute | solution.py:136
  53.6 35.9 %collective-permute-start.19 = (f32[512,512]{1,0:T(8,128)S(1)}, f32[512,512]{1,0:T(8,128)S(1)}, u32[]{:S(2)}, u32[]{:S(2)}) collective-permute-start(f32[512,512]{1,0:T(8,128)S(1)} %get-tuple-element.131), channel_id=1, source_target_pairs={{0,16},{1,17},{2,18},{3,19},{4,20},{5,21},{6,22},{7,23},{8,24},{9,... | collective-permute-start | bytes 3145736 | tf_op jit(solution)/shard_map/ppermute | solution.py:136
  54.2 35.3 %collective-permute-start.20 = (f32[512,512]{1,0:T(8,128)S(1)}, f32[512,512]{1,0:T(8,128)S(1)}, u32[]{:S(2)}, u32[]{:S(2)}) collective-permute-start(f32[512,512]{1,0:T(8,128)S(1)} %get-tuple-element.132), channel_id=1, source_target_pairs={{0,2},{1,3},{2,0},{3,1},{4,6},{5,7},{6,4},{7,5},{8,10},{9,11},{10,... | collective-permute-start | bytes 3145736 | tf_op jit(solution)/shard_map/ppermute | solution.py:136
  92.4 6.6 %collective-permute-start.22 = (f32[536,128]{1,0:T(8,128)S(1)}, f32[536,128]{1,0:T(8,128)S(1)}, u32[]{:S(2)}, u32[]{:S(2)}) collective-permute-start(f32[536,128]{1,0:T(8,128)S(1)} %get-tuple-element.137), channel_id=1, source_target_pairs={{0,8},{1,3},{2,10},{3,1},{4,12},{5,7},{6,14},{7,5},{8,0},{9,11},{1... | collective-permute-start | bytes 823304 | tf_op jit(solution)/shard_map/ppermute | solution.py:136
  93.8 9.4 %collective-permute-start.23 = (f32[536,128]{1,0:T(8,128)S(1)}, f32[536,128]{1,0:T(8,128)S(1)}, u32[]{:S(2)}, u32[]{:S(2)}) collective-permute-start(f32[536,128]{1,0:T(8,128)S(1)} %get-tuple-element.138), channel_id=1, source_target_pairs={{0,16},{1,5},{2,18},{3,7},{4,20},{5,1},{6,22},{7,3},{8,24},{9,13},... | collective-permute-start | bytes 823304 | tf_op jit(solution)/shard_map/ppermute | solution.py:136
  94.6 8.7 %collective-permute-start.24 = (f32[536,128]{1,0:T(8,128)S(1)}, f32[536,128]{1,0:T(8,128)S(1)}, u32[]{:S(2)}, u32[]{:S(2)}) collective-permute-start(f32[536,128]{1,0:T(8,128)S(1)} %get-tuple-element.139), channel_id=1, source_target_pairs={{0,24},{1,7},{2,26},{3,5},{4,28},{5,3},{6,30},{7,1},{8,16},{9,15},... | collective-permute-start | bytes 823304 | tf_op jit(solution)/shard_map/ppermute | solution.py:136
  105.0 6.3 %collective-permute-start.26 = (f32[152,128]{1,0:T(8,128)S(1)}, f32[152,128]{1,0:T(8,128)S(1)}, u32[]{:S(2)}, u32[]{:S(2)}) collective-permute-start(f32[152,128]{1,0:T(8,128)S(1)} %get-tuple-element.142), channel_id=1, source_target_pairs={{0,4},{1,17},{2,6},{3,19},{4,0},{5,21},{6,2},{7,23},{8,12},{9,25},... | collective-permute-start | bytes 233480 | tf_op jit(solution)/shard_map/ppermute | solution.py:136
  106.2 6.3 %collective-permute-start.27 = (f32[152,128]{1,0:T(8,128)S(1)}, f32[152,128]{1,0:T(8,128)S(1)}, u32[]{:S(2)}, u32[]{:S(2)}) collective-permute-start(f32[152,128]{1,0:T(8,128)S(1)} %get-tuple-element.143), channel_id=1, source_target_pairs={{0,6},{1,25},{2,4},{3,27},{4,2},{5,29},{6,0},{7,31},{8,14},{9,17},... | collective-permute-start | bytes 233480 | tf_op jit(solution)/shard_map/ppermute | solution.py:136
  120.4 7.4 %collective-permute-start.33 = (f32[512,128]{1,0:T(8,128)S(1)}, f32[512,128]{1,0:T(8,128)S(1)}, u32[]{:S(2)}, u32[]{:S(2)}) collective-permute-start(f32[512,128]{1,0:T(8,128)S(1)} %constant_dynamic-update-slice_fusion.4.refs_7_), channel_id=1, source_target_pairs={{0,24},{1,7},{2,26},{3,5},{4,28},{5,3},{6,30},{7,1},{8,16},{9,15},... | collective-permute-start | bytes 786440 | tf_op jit(solution)/shard_map/ppermute | solution.py:136
  122.2 8.3 %collective-permute-start.32 = (f32[512,128]{1,0:T(8,128)S(1)}, f32[512,128]{1,0:T(8,128)S(1)}, u32[]{:S(2)}, u32[]{:S(2)}) collective-permute-start(f32[512,128]{1,0:T(8,128)S(1)} %constant_dynamic-update-slice_fusion.4.refs_7_), channel_id=1, source_target_pairs={{0,16},{1,5},{2,18},{3,7},{4,20},{5,1},{6,22},{7,3},{8,24},{9,13},... | collective-permute-start | bytes 786440 | tf_op jit(solution)/shard_map/ppermute | solution.py:136
  123.2 10.5 %collective-permute-start.31 = (f32[512,128]{1,0:T(8,128)S(1)}, f32[512,128]{1,0:T(8,128)S(1)}, u32[]{:S(2)}, u32[]{:S(2)}) collective-permute-start(f32[512,128]{1,0:T(8,128)S(1)} %constant_dynamic-update-slice_fusion.4.refs_7_), channel_id=1, source_target_pairs={{0,8},{1,3},{2,10},{3,1},{4,12},{5,7},{6,14},{7,5},{8,0},{9,11},{1... | collective-permute-start | bytes 786440 | tf_op jit(solution)/shard_map/ppermute | solution.py:136
  123.9 9.8 %collective-permute-start.34 = (f32[512,128]{1,0:T(8,128)S(1)}, f32[512,128]{1,0:T(8,128)S(1)}, u32[]{:S(2)}, u32[]{:S(2)}) collective-permute-start(f32[512,128]{1,0:T(8,128)S(1)} %constant_dynamic-update-slice_fusion.4.refs_7_), channel_id=1, source_target_pairs={{0,1},{1,0},{2,3},{3,2},{4,5},{5,4},{6,7},{7,6},{8,9},{9,8},{10,11... | collective-permute-start | bytes 786440 | tf_op jit(solution)/shard_map/ppermute | solution.py:136
  140.5 8.4 %collective-permute-start.43 = (f32[256,256]{1,0:T(8,128)S(1)}, f32[256,256]{1,0:T(8,128)S(1)}, u32[]{:S(2)}, u32[]{:S(2)}) collective-permute-start(f32[256,256]{1,0:T(8,128)S(1)} %get-tuple-element.162.refs_0_), channel_id=1, source_target_pairs={{0,2},{1,3},{2,0},{3,1},{4,6},{5,7},{6,4},{7,5},{8,10},{9,11},{10,... | collective-permute-start | bytes 786440 | tf_op jit(solution)/shard_map/ppermute | solution.py:136
  140.7 11.5 %collective-permute-start.38 = (f32[256,384]{1,0:T(8,128)S(1)}, f32[256,384]{1,0:T(8,128)S(1)}, u32[]{:S(2)}, u32[]{:S(2)}) collective-permute-start(f32[256,384]{1,0:T(8,128)S(1)} %get-tuple-element.160.refs_0_), channel_id=1, source_target_pairs={{0,8},{1,9},{2,10},{3,11},{4,12},{5,13},{6,14},{7,15},{8,0},{9,1},... | collective-permute-start | bytes 1179656 | tf_op jit(solution)/shard_map/ppermute | solution.py:136
  141.7 11.4 %collective-permute-start.39 = (f32[256,384]{1,0:T(8,128)S(1)}, f32[256,384]{1,0:T(8,128)S(1)}, u32[]{:S(2)}, u32[]{:S(2)}) collective-permute-start(f32[256,384]{1,0:T(8,128)S(1)} %get-tuple-element.161.refs_0_), channel_id=1, source_target_pairs={{0,16},{1,17},{2,18},{3,19},{4,20},{5,21},{6,22},{7,23},{8,24},{9,... | collective-permute-start | bytes 1179656 | tf_op jit(solution)/shard_map/ppermute | solution.py:136
  153.6 15.0 %collective-permute-start.49 = (f32[256,256]{1,0:T(8,128)S(1)}, f32[256,256]{1,0:T(8,128)S(1)}, u32[]{:S(2)}, u32[]{:S(2)}) collective-permute-start(f32[256,256]{1,0:T(8,128)S(1)} %get-tuple-element.172), channel_id=1, source_target_pairs={{0,4},{1,5},{2,6},{3,7},{4,0},{5,1},{6,2},{7,3},{8,12},{9,13},{10,... | collective-permute-start | bytes 786440 | tf_op jit(solution)/shard_map/ppermute | solution.py:136
  157.2 11.4 %collective-permute-start.46 = (f32[256,384]{1,0:T(8,128)S(1)}, f32[256,384]{1,0:T(8,128)S(1)}, u32[]{:S(2)}, u32[]{:S(2)}) collective-permute-start(f32[256,384]{1,0:T(8,128)S(1)} %get-tuple-element.176), channel_id=1, source_target_pairs={{0,16},{1,17},{2,18},{3,19},{4,20},{5,21},{6,22},{7,23},{8,24},{9,... | collective-permute-start | bytes 1179656 | tf_op jit(solution)/shard_map/ppermute | solution.py:136
  159.1 10.5 %collective-permute-start.48 = (f32[256,384]{1,0:T(8,128)S(1)}, f32[256,384]{1,0:T(8,128)S(1)}, u32[]{:S(2)}, u32[]{:S(2)}) collective-permute-start(f32[256,384]{1,0:T(8,128)S(1)} %get-tuple-element.182), channel_id=1, source_target_pairs={{0,8},{1,9},{2,10},{3,11},{4,12},{5,13},{6,14},{7,15},{8,0},{9,1},... | collective-permute-start | bytes 1179656 | tf_op jit(solution)/shard_map/ppermute | solution.py:136
  169.9 11.8 %collective-permute-start.50 = (f32[128,768]{1,0:T(8,128)S(1)}, f32[128,768]{1,0:T(8,128)S(1)}, u32[]{:S(2)}, u32[]{:S(2)}) collective-permute-start(f32[128,768]{1,0:T(8,128)S(1)} %get-tuple-element.198), channel_id=1, source_target_pairs={{0,2},{1,5},{2,0},{3,7},{4,6},{5,1},{6,4},{7,3},{8,10},{9,13},{10,... | collective-permute-start | bytes 1179656 | tf_op jit(solution)/shard_map/ppermute | solution.py:136
  181.7 8.3 %collective-permute-start.52 = (f32[64,768]{1,0:T(8,128)S(1)}, f32[64,768]{1,0:T(8,128)S(1)}, u32[]{:S(2)}, u32[]{:S(2)}) collective-permute-start(f32[64,768]{1,0:T(8,128)S(1)} %slice_add_fusion.2), channel_id=1, source_target_pairs={{0,4},{1,3},{2,6},{3,1},{4,0},{5,7},{6,2},{7,5},{8,12},{9,11},{10,... | collective-permute-start | bytes 589832 | tf_op jit(solution)/shard_map/ppermute | solution.py:136
  (25 other events, 136.1 us)

commit v4 on v3

--- a/solution.py
+++ b/solution.py
@@ -159,7 +159,8 @@
     summed = keep.shape[0] - size - listed
     pieces = [keep, send]
     for at, (stride, radix) in enumerate(steps):
-        ins = [pieces[0]] + [exchange(p, (by * stride[0], by * stride[1])) for by, p in enumerate(pieces) if by]
+        ins = [exchange(pieces[by], (by * stride[0], by * stride[1])) for by in range(radix - 1, 0, -1)]
+        ins = [pieces[0]] + ins
         after = steps[at + 1][1] if at + 1 < len(steps) else 1
         more = listed * radix + summed
         shapes = [(size // after + more, BLK)] * after if after > 1 else [(size, BLK), (more, BLK)]

time: 191 us -> 189 us (0.990)
  waiting for transfers between devices: 84.1 us -> 74.7 us
  starting transfers between devices: 51.5 us -> 59.6 us
    ppermute x54, waiting for transfers between devices: 84.1 us -> 74.7 us  [exchange(): return lax.ppermute(x, AXES, [(i, i ^ bits[i % 2]) for i in range(count)])]
    ppermute x54, starting transfers between devices: 51.5 us -> 59.6 us  [exchange(): return lax.ppermute(x, AXES, [(i, i ^ bits[i % 2]) for i in range(count)])]
  transfers between devices with their start and end apart: 54 -> 54, of which waited for: 31 -> 30; matrix products, arithmetic and copies ran while one was open for 1% -> 1% of each run, Pallas kernels for 21% -> 21%
where the time goes in v4:
time: 189 us
  waiting for transfers between devices  74.7 us (40%)
  starting transfers between devices  59.6 us (32%)
  Pallas kernels  50.7 us (27%)
  matrix products  2.26 us (1%)
    ppermute x54, waiting for transfers between devices, exchange(): return lax.ppermute(x, AXES, [(i, i ^ bits[i % 2]) for i in range(count)])  74.7 us
    ppermute x54, starting transfers between devices, exchange(): return lax.ppermute(x, AXES, [(i, i ^ bits[i % 2]) for i in range(count)])  59.6 us
    pallas_call x15, Pallas kernels, call(): pl.pallas_call(kernel, out_shape=tuple((jax.ShapeDtypeStruct(s, t) for s,...  50.7 us
  transfers between devices with their start and end apart: 54, of which 30 were waited for; matrix products, arithmetic and copies ran while one was open for 1% of the time, Pallas kernels for 21%

profile of v4, /device:TPU:0, one launch (start us, length us, event | category | flops | bytes accessed | tf_op | source)
XLA Modules:
  0.0 189.3 jit_solution(5459649197349259931)
XLA Ops:
  0.7 5.8 %shard_map.58 = (f32[256,1024]{1,0:T(8,128)S(1)}, f32[2064,128]{1,0:T(8,128)S(1)}, f32[2064,128]{1,0:T(8,128)S(1)}, bf16[256,2048]{1,0:T(8,128)(2,1)S(1)}) custom-call(s32[1,1]{1,0:T(1,128)} %bitcast.pos_ref.refs_0_, bf16[256,2048]{1,0:T(8,128)(2,1)} %hid_hbm.1, bf16[2048,1024]{1,0:T(8,128)(2,1)} %w_hbm.1), custom_call_target="tpu_custom_call" | custom-call | flops 1000000 | bytes 1000000 | tf_op jit(solution)/shard_map/pallas_call | solution.py:591
  9.5 3.9 %collective-permute-start.1 = (f32[536,128]{1,0:T(8,128)S(1)}, f32[536,128]{1,0:T(8,128)S(1)}, u32[]{:S(2)}, u32[]{:S(2)}) collective-permute-start(f32[536,128]{1,0:T(8,128)S(1)} %get-tuple-element.103), channel_id=1, source_target_pairs={{0,24},{1,7},{2,26},{3,5},{4,28},{5,3},{6,30},{7,1},{8,16},{9,15},... | collective-permute-start | bytes 823304 | tf_op jit(solution)/shard_map/ppermute | solution.py:136
  14.0 3.9 %collective-permute-done.1.refs_1_ = f32[536,128]{1,0:T(8,128)S(1)} collective-permute-done((f32[536,128]{1,0:T(8,128)S(1)}, f32[536,128]{1,0:T(8,128)S(1)}, u32[]{:S(2)}, u32[]{:S(2)}) %collective-permute-start.1) | collective-permute-done | bytes 274464 | tf_op jit(solution)/shard_map/ppermute | solution.py:136
  17.9 2.8 %collective-permute-done.2.refs_2_ = f32[536,128]{1,0:T(8,128)S(1)} collective-permute-done((f32[536,128]{1,0:T(8,128)S(1)}, f32[536,128]{1,0:T(8,128)S(1)}, u32[]{:S(2)}, u32[]{:S(2)}) %collective-permute-start.2) | collective-permute-done | bytes 274464 | tf_op jit(solution)/shard_map/ppermute | solution.py:136
  21.4 3.7 %collective-permute-start.4 = (f32[200,128]{1,0:T(8,128)S(1)}, f32[200,128]{1,0:T(8,128)S(1)}, u32[]{:S(2)}, u32[]{:S(2)}) collective-permute-start(f32[200,128]{1,0:T(8,128)S(1)} %get-tuple-element.107), channel_id=1, source_target_pairs={{0,6},{1,25},{2,4},{3,27},{4,2},{5,29},{6,0},{7,31},{8,14},{9,17},... | collective-permute-start | bytes 307208 | tf_op jit(solution)/shard_map/ppermute | solution.py:136
  25.9 2.2 %collective-permute-done.4.refs_1_ = f32[200,128]{1,0:T(8,128)S(1)} collective-permute-done((f32[200,128]{1,0:T(8,128)S(1)}, f32[200,128]{1,0:T(8,128)S(1)}, u32[]{:S(2)}, u32[]{:S(2)}) %collective-permute-start.4) | collective-permute-done | bytes 102432 | tf_op jit(solution)/shard_map/ppermute | solution.py:136
  28.1 2.8 %collective-permute-done.5.refs_2_ = f32[200,128]{1,0:T(8,128)S(1)} collective-permute-done((f32[200,128]{1,0:T(8,128)S(1)}, f32[200,128]{1,0:T(8,128)S(1)}, u32[]{:S(2)}, u32[]{:S(2)}) %collective-permute-start.5) | collective-permute-done | bytes 102432 | tf_op jit(solution)/shard_map/ppermute | solution.py:136
  30.9 2.5 %collective-permute-start.9 = (f32[128,128]{1,0:T(8,128)S(1)}, f32[128,128]{1,0:T(8,128)S(1)}, u32[]{:S(2)}, u32[]{:S(2)}) collective-permute-start(f32[128,128]{1,0:T(8,128)S(1)} %get-tuple-element.122), channel_id=1, source_target_pairs={{0,6},{1,25},{2,4},{3,27},{4,2},{5,29},{6,0},{7,31},{8,14},{9,17},... | collective-permute-start | bytes 196616 | tf_op jit(solution)/shard_map/ppermute | solution.py:136
  33.6 1.8 collective-permute-start.7
  38.7 2.4 %collective-permute-start.13 = (f32[512,128]{1,0:T(8,128)S(1)}, f32[512,128]{1,0:T(8,128)S(1)}, u32[]{:S(2)}, u32[]{:S(2)}) collective-permute-start(f32[512,128]{1,0:T(8,128)S(1)} %constant_dynamic-update-slice_fusion.refs_4_), channel_id=1, source_target_pairs={{0,24},{1,7},{2,26},{3,5},{4,28},{5,3},{6,30},{7,1},{8,16},{9,15},... | collective-permute-start | bytes 786440 | tf_op jit(solution)/shard_map/ppermute | solution.py:136
  42.3 2.0 %collective-permute-start.14 = (f32[512,128]{1,0:T(8,128)S(1)}, f32[512,128]{1,0:T(8,128)S(1)}, u32[]{:S(2)}, u32[]{:S(2)}) collective-permute-start(f32[512,128]{1,0:T(8,128)S(1)} %constant_dynamic-update-slice_fusion.refs_4_), channel_id=1, source_target_pairs={{0,1},{1,0},{2,3},{3,2},{4,5},{5,4},{6,7},{7,6},{8,9},{9,8},{10,11... | collective-permute-start | bytes 786440 | tf_op jit(solution)/shard_map/ppermute | solution.py:136
  44.3 1.9 %collective-permute-done.13.refs_7_ = f32[512,128]{1,0:T(8,128)S(1)} collective-permute-done((f32[512,128]{1,0:T(8,128)S(1)}, f32[512,128]{1,0:T(8,128)S(1)}, u32[]{:S(2)}, u32[]{:S(2)}) %collective-permute-start.13) | collective-permute-done | bytes 262176 | tf_op jit(solution)/shard_map/ppermute | solution.py:136
  46.2 1.8 collective-permute-start.17
  48.9 3.7 %collective-permute-start.16 = (f32[512,128]{1,0:T(8,128)S(1)}, f32[512,128]{1,0:T(8,128)S(1)}, u32[]{:S(2)}, u32[]{:S(2)}) collective-permute-start(f32[512,128]{1,0:T(8,128)S(1)} %collective-permute-done.12.refs_6_), channel_id=1, source_target_pairs={{0,1},{1,0},{2,3},{3,2},{4,5},{5,4},{6,7},{7,6},{8,9},{9,8},{10,11... | collective-permute-start | bytes 786440 | tf_op jit(solution)/shard_map/ppermute | solution.py:136
  55.2 35.2 %shard_map.64 = (bf16[256,1024]{1,0:T(8,128)(2,1)}, bf16[256,1024]{1,0:T(8,128)(2,1)S(1)}, bf16[256,256]{1,0:T(8,128)(2,1)S(1)}, bf16[256,256]{1,0:T(8,128)(2,1)...) custom-call(s32[1,1]{1,0:T(1,128)} %bitcast.pos_ref.refs_0_, ...), custom_call_target="tpu_custom_call" | custom-call | flops 30000001024 | bytes 1000000 | tf_op jit(solution)/shard_map/pallas_call | solution.py:591
  90.5 2.7 %collective-permute-done.21.refs_1_ = f32[2072,128]{1,0:T(8,128)S(1)} collective-permute-done((f32[2072,128]{1,0:T(8,128)S(1)}, f32[2072,128]{1,0:T(8,128)S(1)}, u32[]{:S(2)}, u32[]{:S(2)}) %collective-permute-start.21) | collective-permute-done | bytes 1060896 | tf_op jit(solution)/shard_map/ppermute | solution.py:136
  96.9 4.0 %collective-permute-done.22.refs_1_ = f32[536,128]{1,0:T(8,128)S(1)} collective-permute-done((f32[536,128]{1,0:T(8,128)S(1)}, f32[536,128]{1,0:T(8,128)S(1)}, u32[]{:S(2)}, u32[]{:S(2)}) %collective-permute-start.22) | collective-permute-done | bytes 274464 | tf_op jit(solution)/shard_map/ppermute | solution.py:136
  100.9 2.8 %collective-permute-done.23.refs_2_ = f32[536,128]{1,0:T(8,128)S(1)} collective-permute-done((f32[536,128]{1,0:T(8,128)S(1)}, f32[536,128]{1,0:T(8,128)S(1)}, u32[]{:S(2)}, u32[]{:S(2)}) %collective-permute-start.23) | collective-permute-done | bytes 274464 | tf_op jit(solution)/shard_map/ppermute | solution.py:136
  103.8 2.7 %collective-permute-start.25 = (f32[152,128]{1,0:T(8,128)S(1)}, f32[152,128]{1,0:T(8,128)S(1)}, u32[]{:S(2)}, u32[]{:S(2)}) collective-permute-start(f32[152,128]{1,0:T(8,128)S(1)} %get-tuple-element.141), channel_id=1, source_target_pairs={{0,6},{1,25},{2,4},{3,27},{4,2},{5,29},{6,0},{7,31},{8,14},{9,17},... | collective-permute-start | bytes 233480 | tf_op jit(solution)/shard_map/ppermute | solution.py:136
  108.2 1.9 %collective-permute-done.25.refs_1_ = f32[152,128]{1,0:T(8,128)S(1)} collective-permute-done((f32[152,128]{1,0:T(8,128)S(1)}, f32[152,128]{1,0:T(8,128)S(1)}, u32[]{:S(2)}, u32[]{:S(2)}) %collective-permute-start.25) | collective-permute-done | bytes 77856 | tf_op jit(solution)/shard_map/ppermute | solution.py:136
  110.2 2.5 %collective-permute-done.26.refs_2_ = f32[152,128]{1,0:T(8,128)S(1)} collective-permute-done((f32[152,128]{1,0:T(8,128)S(1)}, f32[152,128]{1,0:T(8,128)S(1)}, u32[]{:S(2)}, u32[]{:S(2)}) %collective-permute-start.26) | collective-permute-done | bytes 77856 | tf_op jit(solution)/shard_map/ppermute | solution.py:136
  112.7 1.8 collective-permute-start.30
  114.5 2.7 %collective-permute-start.28 = (f32[128,128]{1,0:T(8,128)S(1)}, f32[128,128]{1,0:T(8,128)S(1)}, u32[]{:S(2)}, u32[]{:S(2)}) collective-permute-start(f32[128,128]{1,0:T(8,128)S(1)} %get-tuple-element.156), channel_id=1, source_target_pairs={{0,2},{1,9},{2,0},{3,11},{4,6},{5,13},{6,4},{7,15},{8,10},{9,1},{1... | collective-permute-start | bytes 196616 | tf_op jit(solution)/shard_map/ppermute | solution.py:136
  125.3 2.5 %collective-permute-done.33.refs_10_ = f32[512,128]{1,0:T(8,128)S(1)} collective-permute-done((f32[512,128]{1,0:T(8,128)S(1)}, f32[512,128]{1,0:T(8,128)S(1)}, u32[]{:S(2)}, u32[]{:S(2)}) %collective-permute-start.33) | collective-permute-done | bytes 262176 | tf_op jit(solution)/shard_map/ppermute | solution.py:136
  130.4 3.1 %collective-permute-start.36 = (f32[512,128]{1,0:T(8,128)S(1)}, f32[512,128]{1,0:T(8,128)S(1)}, u32[]{:S(2)}, u32[]{:S(2)}) collective-permute-start(f32[512,128]{1,0:T(8,128)S(1)} %collective-permute-done.32.refs_9_), channel_id=1, source_target_pairs={{0,1},{1,0},{2,3},{3,2},{4,5},{5,4},{6,7},{7,6},{8,9},{9,8},{10,11... | collective-permute-start | bytes 786440 | tf_op jit(solution)/shard_map/ppermute | solution.py:136
  135.1 4.8 %shard_map.69 = (bf16[256,1024]{1,0:T(8,128)(2,1)S(1)}, f32[256,384]{1,0:T(8,128)S(1)}, f32[256,384]{1,0:T(8,128)S(1)}, f32[256,256]{1,0:T(8,128)S(1)}) custom-call(s32[1,1]{1,0:T(1,128)} %bitcast.pos_ref.refs_0_, f32[24,128]{1,0:T(8,128)S(1)} %get-tuple-element.144.refs_1_, f32[256,1024]{1,0:T(8,128)S(1)} %get-tuple-element.145.refs_2_, ...), custom_call_target="tpu_custom_call" | custom-call | flops 1000000 | bytes 1000000 | tf_op jit(solution)/shard_map/pallas_call | solution.py:591
  142.2 2.3 %convolution_convert_fusion = bf16[256,2048]{1,0:T(8,128)(2,1)} fusion(bf16[256,1024]{1,0:T(8,128)(2,1)S(1)} %get-tuple-element.163, bf16[2048,1024]{1,0:T(8,128)(2,1)S(1)} %copy-done.2), kind=kOutput, calls=%fused_computation | convolution fusion | flops 1074266112 | bytes 5767168 | tf_op jit(solution)/shard_map/dot_general | solution.py:57
  144.4 4.3 %collective-permute-done.43.refs_2_ = f32[256,256]{1,0:T(8,128)S(1)} collective-permute-done((f32[256,256]{1,0:T(8,128)S(1)}, f32[256,256]{1,0:T(8,128)S(1)}, u32[]{:S(2)}, u32[]{:S(2)}) %collective-permute-start.43) | collective-permute-done | bytes 262176 | tf_op jit(solution)/shard_map/ppermute | solution.py:136
  158.0 10.2 %collective-permute-done.49 = f32[256,256]{1,0:T(8,128)S(1)} collective-permute-done((f32[256,256]{1,0:T(8,128)S(1)}, f32[256,256]{1,0:T(8,128)S(1)}, u32[]{:S(2)}, u32[]{:S(2)}) %collective-permute-start.49) | collective-permute-done | bytes 262176 | tf_op jit(solution)/shard_map/ppermute | solution.py:136
  170.7 4.1 %collective-permute-done.51 = f32[128,256]{1,0:T(8,128)S(1)} collective-permute-done((f32[128,256]{1,0:T(8,128)S(1)}, f32[128,256]{1,0:T(8,128)S(1)}, u32[]{:S(2)}, u32[]{:S(2)}) %collective-permute-start.51) | collective-permute-done | bytes 131104 | tf_op jit(solution)/shard_map/ppermute | solution.py:136
  176.2 3.7 %collective-permute-done.50 = f32[128,768]{1,0:T(8,128)S(1)} collective-permute-done((f32[128,768]{1,0:T(8,128)S(1)}, f32[128,768]{1,0:T(8,128)S(1)}, u32[]{:S(2)}, u32[]{:S(2)}) %collective-permute-start.50) | collective-permute-done | bytes 393248 | tf_op jit(solution)/shard_map/ppermute | solution.py:136
  180.9 7.6 %collective-permute-done.52 = f32[64,768]{1,0:T(8,128)S(1)} collective-permute-done((f32[64,768]{1,0:T(8,128)S(1)}, f32[64,768]{1,0:T(8,128)S(1)}, u32[]{:S(2)}, u32[]{:S(2)}) %collective-permute-start.52) | collective-permute-done | bytes 196640 | tf_op jit(solution)/shard_map/ppermute | solution.py:136
  (114 shorter events, 48.1 us)
Async XLA Ops:
  7.8 27.5 %collective-permute-start.10 = (f32[1024,256]{1,0:T(8,128)S(1)}, f32[1024,256]{1,0:T(8,128)S(1)}, u32[]{:S(2)}, u32[]{:S(2)}) collective-permute-start(f32[1024,256]{1,0:T(8,128)S(1)} %get-tuple-element.115), channel_id=1, source_target_pairs={{0,1},{1,0},{2,3},{3,2},{4,5},{5,4},{6,7},{7,6},{8,9},{9,8},{10,11... | collective-permute-start | bytes 3145736 | tf_op jit(solution)/shard_map/ppermute | solution.py:136
  9.5 8.5 %collective-permute-start.1 = (f32[536,128]{1,0:T(8,128)S(1)}, f32[536,128]{1,0:T(8,128)S(1)}, u32[]{:S(2)}, u32[]{:S(2)}) collective-permute-start(f32[536,128]{1,0:T(8,128)S(1)} %get-tuple-element.103), channel_id=1, source_target_pairs={{0,24},{1,7},{2,26},{3,5},{4,28},{5,3},{6,30},{7,1},{8,16},{9,15},... | collective-permute-start | bytes 823304 | tf_op jit(solution)/shard_map/ppermute | solution.py:136
  13.4 7.4 %collective-permute-start.2 = (f32[536,128]{1,0:T(8,128)S(1)}, f32[536,128]{1,0:T(8,128)S(1)}, u32[]{:S(2)}, u32[]{:S(2)}) collective-permute-start(f32[536,128]{1,0:T(8,128)S(1)} %get-tuple-element.104), channel_id=1, source_target_pairs={{0,16},{1,5},{2,18},{3,7},{4,20},{5,1},{6,22},{7,3},{8,24},{9,13},... | collective-permute-start | bytes 823304 | tf_op jit(solution)/shard_map/ppermute | solution.py:136
  13.9 7.5 %collective-permute-start.3 = (f32[536,128]{1,0:T(8,128)S(1)}, f32[536,128]{1,0:T(8,128)S(1)}, u32[]{:S(2)}, u32[]{:S(2)}) collective-permute-start(f32[536,128]{1,0:T(8,128)S(1)} %get-tuple-element.105), channel_id=1, source_target_pairs={{0,8},{1,3},{2,10},{3,1},{4,12},{5,7},{6,14},{7,5},{8,0},{9,11},{1... | collective-permute-start | bytes 823304 | tf_op jit(solution)/shard_map/ppermute | solution.py:136
  21.4 6.6 %collective-permute-start.4 = (f32[200,128]{1,0:T(8,128)S(1)}, f32[200,128]{1,0:T(8,128)S(1)}, u32[]{:S(2)}, u32[]{:S(2)}) collective-permute-start(f32[200,128]{1,0:T(8,128)S(1)} %get-tuple-element.107), channel_id=1, source_target_pairs={{0,6},{1,25},{2,4},{3,27},{4,2},{5,29},{6,0},{7,31},{8,14},{9,17},... | collective-permute-start | bytes 307208 | tf_op jit(solution)/shard_map/ppermute | solution.py:136
  38.7 7.4 %collective-permute-start.13 = (f32[512,128]{1,0:T(8,128)S(1)}, f32[512,128]{1,0:T(8,128)S(1)}, u32[]{:S(2)}, u32[]{:S(2)}) collective-permute-start(f32[512,128]{1,0:T(8,128)S(1)} %constant_dynamic-update-slice_fusion.refs_4_), channel_id=1, source_target_pairs={{0,24},{1,7},{2,26},{3,5},{4,28},{5,3},{6,30},{7,1},{8,16},{9,15},... | collective-permute-start | bytes 786440 | tf_op jit(solution)/shard_map/ppermute | solution.py:136
  41.1 7.7 %collective-permute-start.12 = (f32[512,128]{1,0:T(8,128)S(1)}, f32[512,128]{1,0:T(8,128)S(1)}, u32[]{:S(2)}, u32[]{:S(2)}) collective-permute-start(f32[512,128]{1,0:T(8,128)S(1)} %constant_dynamic-update-slice_fusion.refs_4_), channel_id=1, source_target_pairs={{0,16},{1,5},{2,18},{3,7},{4,20},{5,1},{6,22},{7,3},{8,24},{9,13},... | collective-permute-start | bytes 786440 | tf_op jit(solution)/shard_map/ppermute | solution.py:136
  41.7 10.9 %collective-permute-start.11 = (f32[512,128]{1,0:T(8,128)S(1)}, f32[512,128]{1,0:T(8,128)S(1)}, u32[]{:S(2)}, u32[]{:S(2)}) collective-permute-start(f32[512,128]{1,0:T(8,128)S(1)} %constant_dynamic-update-slice_fusion.refs_4_), channel_id=1, source_target_pairs={{0,8},{1,3},{2,10},{3,1},{4,12},{5,7},{6,14},{7,5},{8,0},{9,11},{1... | collective-permute-start | bytes 786440 | tf_op jit(solution)/shard_map/ppermute | solution.py:136
  42.3 11.2 %collective-permute-start.14 = (f32[512,128]{1,0:T(8,128)S(1)}, f32[512,128]{1,0:T(8,128)S(1)}, u32[]{:S(2)}, u32[]{:S(2)}) collective-permute-start(f32[512,128]{1,0:T(8,128)S(1)} %constant_dynamic-update-slice_fusion.refs_4_), channel_id=1, source_target_pairs={{0,1},{1,0},{2,3},{3,2},{4,5},{5,4},{6,7},{7,6},{8,9},{9,8},{10,11... | collective-permute-start | bytes 786440 | tf_op jit(solution)/shard_map/ppermute | solution.py:136
  46.2 9.0 %collective-permute-start.17 = (f32[512,128]{1,0:T(8,128)S(1)}, f32[512,128]{1,0:T(8,128)S(1)}, u32[]{:S(2)}, u32[]{:S(2)}) collective-permute-start(f32[512,128]{1,0:T(8,128)S(1)} %collective-permute-done.13.refs_7_), channel_id=1, source_target_pairs={{0,1},{1,0},{2,3},{3,2},{4,5},{5,4},{6,7},{7,6},{8,9},{9,8},{10,11... | collective-permute-start | bytes 786440 | tf_op jit(solution)/shard_map/ppermute | solution.py:136
  48.9 6.3 %collective-permute-start.16 = (f32[512,128]{1,0:T(8,128)S(1)}, f32[512,128]{1,0:T(8,128)S(1)}, u32[]{:S(2)}, u32[]{:S(2)}) collective-permute-start(f32[512,128]{1,0:T(8,128)S(1)} %collective-permute-done.12.refs_6_), channel_id=1, source_target_pairs={{0,1},{1,0},{2,3},{3,2},{4,5},{5,4},{6,7},{7,6},{8,9},{9,8},{10,11... | collective-permute-start | bytes 786440 | tf_op jit(solution)/shard_map/ppermute | solution.py:136
  52.6 37.8 %collective-permute-start.18 = (f32[512,512]{1,0:T(8,128)S(1)}, f32[512,512]{1,0:T(8,128)S(1)}, u32[]{:S(2)}, u32[]{:S(2)}) collective-permute-start(f32[512,512]{1,0:T(8,128)S(1)} %get-tuple-element.130), channel_id=1, source_target_pairs={{0,8},{1,9},{2,10},{3,11},{4,12},{5,13},{6,14},{7,15},{8,0},{9,1},... | collective-permute-start | bytes 3145736 | tf_op jit(solution)/shard_map/ppermute | solution.py:136
  53.5 36.9 %collective-permute-start.19 = (f32[512,512]{1,0:T(8,128)S(1)}, f32[512,512]{1,0:T(8,128)S(1)}, u32[]{:S(2)}, u32[]{:S(2)}) collective-permute-start(f32[512,512]{1,0:T(8,128)S(1)} %get-tuple-element.131), channel_id=1, source_target_pairs={{0,16},{1,17},{2,18},{3,19},{4,20},{5,21},{6,22},{7,23},{8,24},{9,... | collective-permute-start | bytes 3145736 | tf_op jit(solution)/shard_map/ppermute | solution.py:136
  55.1 35.2 %collective-permute-start.20 = (f32[512,512]{1,0:T(8,128)S(1)}, f32[512,512]{1,0:T(8,128)S(1)}, u32[]{:S(2)}, u32[]{:S(2)}) collective-permute-start(f32[512,512]{1,0:T(8,128)S(1)} %get-tuple-element.132), channel_id=1, source_target_pairs={{0,2},{1,3},{2,0},{3,1},{4,6},{5,7},{6,4},{7,5},{8,10},{9,11},{10,... | collective-permute-start | bytes 3145736 | tf_op jit(solution)/shard_map/ppermute | solution.py:136
  93.3 7.6 %collective-permute-start.22 = (f32[536,128]{1,0:T(8,128)S(1)}, f32[536,128]{1,0:T(8,128)S(1)}, u32[]{:S(2)}, u32[]{:S(2)}) collective-permute-start(f32[536,128]{1,0:T(8,128)S(1)} %get-tuple-element.137), channel_id=1, source_target_pairs={{0,24},{1,7},{2,26},{3,5},{4,28},{5,3},{6,30},{7,1},{8,16},{9,15},... | collective-permute-start | bytes 823304 | tf_op jit(solution)/shard_map/ppermute | solution.py:136
  94.3 9.4 %collective-permute-start.23 = (f32[536,128]{1,0:T(8,128)S(1)}, f32[536,128]{1,0:T(8,128)S(1)}, u32[]{:S(2)}, u32[]{:S(2)}) collective-permute-start(f32[536,128]{1,0:T(8,128)S(1)} %get-tuple-element.138), channel_id=1, source_target_pairs={{0,16},{1,5},{2,18},{3,7},{4,20},{5,1},{6,22},{7,3},{8,24},{9,13},... | collective-permute-start | bytes 823304 | tf_op jit(solution)/shard_map/ppermute | solution.py:136
  95.5 8.2 %collective-permute-start.24 = (f32[536,128]{1,0:T(8,128)S(1)}, f32[536,128]{1,0:T(8,128)S(1)}, u32[]{:S(2)}, u32[]{:S(2)}) collective-permute-start(f32[536,128]{1,0:T(8,128)S(1)} %get-tuple-element.139), channel_id=1, source_target_pairs={{0,8},{1,3},{2,10},{3,1},{4,12},{5,7},{6,14},{7,5},{8,0},{9,11},{1... | collective-permute-start | bytes 823304 | tf_op jit(solution)/shard_map/ppermute | solution.py:136
  103.8 6.4 %collective-permute-start.25 = (f32[152,128]{1,0:T(8,128)S(1)}, f32[152,128]{1,0:T(8,128)S(1)}, u32[]{:S(2)}, u32[]{:S(2)}) collective-permute-start(f32[152,128]{1,0:T(8,128)S(1)} %get-tuple-element.141), channel_id=1, source_target_pairs={{0,6},{1,25},{2,4},{3,27},{4,2},{5,29},{6,0},{7,31},{8,14},{9,17},... | collective-permute-start | bytes 233480 | tf_op jit(solution)/shard_map/ppermute | solution.py:136
  106.5 6.2 %collective-permute-start.26 = (f32[152,128]{1,0:T(8,128)S(1)}, f32[152,128]{1,0:T(8,128)S(1)}, u32[]{:S(2)}, u32[]{:S(2)}) collective-permute-start(f32[152,128]{1,0:T(8,128)S(1)} %get-tuple-element.142), channel_id=1, source_target_pairs={{0,4},{1,17},{2,6},{3,19},{4,0},{5,21},{6,2},{7,23},{8,12},{9,25},... | collective-permute-start | bytes 233480 | tf_op jit(solution)/shard_map/ppermute | solution.py:136
  112.7 6.1 %collective-permute-start.30 = (f32[128,128]{1,0:T(8,128)S(1)}, f32[128,128]{1,0:T(8,128)S(1)}, u32[]{:S(2)}, u32[]{:S(2)}) collective-permute-start(f32[128,128]{1,0:T(8,128)S(1)} %get-tuple-element.156), channel_id=1, source_target_pairs={{0,6},{1,25},{2,4},{3,27},{4,2},{5,29},{6,0},{7,31},{8,14},{9,17},... | collective-permute-start | bytes 196616 | tf_op jit(solution)/shard_map/ppermute | solution.py:136
  120.3 7.4 %collective-permute-start.33 = (f32[512,128]{1,0:T(8,128)S(1)}, f32[512,128]{1,0:T(8,128)S(1)}, u32[]{:S(2)}, u32[]{:S(2)}) collective-permute-start(f32[512,128]{1,0:T(8,128)S(1)} %constant_dynamic-update-slice_fusion.4.refs_7_), channel_id=1, source_target_pairs={{0,24},{1,7},{2,26},{3,5},{4,28},{5,3},{6,30},{7,1},{8,16},{9,15},... | collective-permute-start | bytes 786440 | tf_op jit(solution)/shard_map/ppermute | solution.py:136
  121.3 9.1 %collective-permute-start.32 = (f32[512,128]{1,0:T(8,128)S(1)}, f32[512,128]{1,0:T(8,128)S(1)}, u32[]{:S(2)}, u32[]{:S(2)}) collective-permute-start(f32[512,128]{1,0:T(8,128)S(1)} %constant_dynamic-update-slice_fusion.4.refs_7_), channel_id=1, source_target_pairs={{0,16},{1,5},{2,18},{3,7},{4,20},{5,1},{6,22},{7,3},{8,24},{9,13},... | collective-permute-start | bytes 786440 | tf_op jit(solution)/shard_map/ppermute | solution.py:136
  122.5 11.1 %collective-permute-start.31 = (f32[512,128]{1,0:T(8,128)S(1)}, f32[512,128]{1,0:T(8,128)S(1)}, u32[]{:S(2)}, u32[]{:S(2)}) collective-permute-start(f32[512,128]{1,0:T(8,128)S(1)} %constant_dynamic-update-slice_fusion.4.refs_7_), channel_id=1, source_target_pairs={{0,8},{1,3},{2,10},{3,1},{4,12},{5,7},{6,14},{7,5},{8,0},{9,11},{1... | collective-permute-start | bytes 786440 | tf_op jit(solution)/shard_map/ppermute | solution.py:136
  123.8 9.7 %collective-permute-start.34 = (f32[512,128]{1,0:T(8,128)S(1)}, f32[512,128]{1,0:T(8,128)S(1)}, u32[]{:S(2)}, u32[]{:S(2)}) collective-permute-start(f32[512,128]{1,0:T(8,128)S(1)} %constant_dynamic-update-slice_fusion.4.refs_7_), channel_id=1, source_target_pairs={{0,1},{1,0},{2,3},{3,2},{4,5},{5,4},{6,7},{7,6},{8,9},{9,8},{10,11... | collective-permute-start | bytes 786440 | tf_op jit(solution)/shard_map/ppermute | solution.py:136
  140.4 8.3 %collective-permute-start.43 = (f32[256,256]{1,0:T(8,128)S(1)}, f32[256,256]{1,0:T(8,128)S(1)}, u32[]{:S(2)}, u32[]{:S(2)}) collective-permute-start(f32[256,256]{1,0:T(8,128)S(1)} %get-tuple-element.162.refs_0_), channel_id=1, source_target_pairs={{0,2},{1,3},{2,0},{3,1},{4,6},{5,7},{6,4},{7,5},{8,10},{9,11},{10,... | collective-permute-start | bytes 786440 | tf_op jit(solution)/shard_map/ppermute | solution.py:136
  140.6 11.4 %collective-permute-start.38 = (f32[256,384]{1,0:T(8,128)S(1)}, f32[256,384]{1,0:T(8,128)S(1)}, u32[]{:S(2)}, u32[]{:S(2)}) collective-permute-start(f32[256,384]{1,0:T(8,128)S(1)} %get-tuple-element.160.refs_0_), channel_id=1, source_target_pairs={{0,8},{1,9},{2,10},{3,11},{4,12},{5,13},{6,14},{7,15},{8,0},{9,1},... | collective-permute-start | bytes 1179656 | tf_op jit(solution)/shard_map/ppermute | solution.py:136
  141.6 11.4 %collective-permute-start.39 = (f32[256,384]{1,0:T(8,128)S(1)}, f32[256,384]{1,0:T(8,128)S(1)}, u32[]{:S(2)}, u32[]{:S(2)}) collective-permute-start(f32[256,384]{1,0:T(8,128)S(1)} %get-tuple-element.161.refs_0_), channel_id=1, source_target_pairs={{0,16},{1,17},{2,18},{3,19},{4,20},{5,21},{6,22},{7,23},{8,24},{9,... | collective-permute-start | bytes 1179656 | tf_op jit(solution)/shard_map/ppermute | solution.py:136
  153.5 14.7 %collective-permute-start.49 = (f32[256,256]{1,0:T(8,128)S(1)}, f32[256,256]{1,0:T(8,128)S(1)}, u32[]{:S(2)}, u32[]{:S(2)}) collective-permute-start(f32[256,256]{1,0:T(8,128)S(1)} %get-tuple-element.172), channel_id=1, source_target_pairs={{0,4},{1,5},{2,6},{3,7},{4,0},{5,1},{6,2},{7,3},{8,12},{9,13},{10,... | collective-permute-start | bytes 786440 | tf_op jit(solution)/shard_map/ppermute | solution.py:136
  155.5 12.8 %collective-permute-start.46 = (f32[256,384]{1,0:T(8,128)S(1)}, f32[256,384]{1,0:T(8,128)S(1)}, u32[]{:S(2)}, u32[]{:S(2)}) collective-permute-start(f32[256,384]{1,0:T(8,128)S(1)} %get-tuple-element.176), channel_id=1, source_target_pairs={{0,16},{1,17},{2,18},{3,19},{4,20},{5,21},{6,22},{7,23},{8,24},{9,... | collective-permute-start | bytes 1179656 | tf_op jit(solution)/shard_map/ppermute | solution.py:136
  157.1 11.2 %collective-permute-start.48 = (f32[256,384]{1,0:T(8,128)S(1)}, f32[256,384]{1,0:T(8,128)S(1)}, u32[]{:S(2)}, u32[]{:S(2)}) collective-permute-start(f32[256,384]{1,0:T(8,128)S(1)} %get-tuple-element.182), channel_id=1, source_target_pairs={{0,8},{1,9},{2,10},{3,11},{4,12},{5,13},{6,14},{7,15},{8,0},{9,1},... | collective-permute-start | bytes 1179656 | tf_op jit(solution)/shard_map/ppermute | solution.py:136
  168.5 11.3 %collective-permute-start.50 = (f32[128,768]{1,0:T(8,128)S(1)}, f32[128,768]{1,0:T(8,128)S(1)}, u32[]{:S(2)}, u32[]{:S(2)}) collective-permute-start(f32[128,768]{1,0:T(8,128)S(1)} %get-tuple-element.198), channel_id=1, source_target_pairs={{0,2},{1,5},{2,0},{3,7},{4,6},{5,1},{6,4},{7,3},{8,10},{9,13},{10,... | collective-permute-start | bytes 1179656 | tf_op jit(solution)/shard_map/ppermute | solution.py:136
  179.9 8.7 %collective-permute-start.52 = (f32[64,768]{1,0:T(8,128)S(1)}, f32[64,768]{1,0:T(8,128)S(1)}, u32[]{:S(2)}, u32[]{:S(2)}) collective-permute-start(f32[64,768]{1,0:T(8,128)S(1)} %slice_add_fusion.2), channel_id=1, source_target_pairs={{0,4},{1,3},{2,6},{3,1},{4,0},{5,7},{6,2},{7,5},{8,12},{9,11},{10,... | collective-permute-start | bytes 589832 | tf_op jit(solution)/shard_map/ppermute | solution.py:136
  (25 other events, 136.0 us)
